TPU v7x, 32 devices: a whole 2x2x4 slice. The times are simulated.
32 devices in a mesh: grp: 4 (over y, x), ctx: 8 (over z, core).
Axes of the slice: x: 2, y: 2, z: 4, core: 2. Of those that a mesh axis runs over, the one named last changes fastest.
Arguments:
- tokens: bfloat16 [4096, 2048], P(('grp', 'ctx')), may hold values from -3 to 3
- queries: bfloat16 [4096, 4096], P(('grp', 'ctx')), may hold values from -6 to 6
- keys_values: bfloat16 [4, 2048, 1024], P('grp', 'ctx'), may hold values from -600 to 600
- out_weight: bfloat16 [4096, 2048], P('grp'), may hold values from -1 to 1
- moe_gain: float32 [2048], replicated, may hold values from 0.1 to 1.9
- expert_ids: int32 [4096, 8], P(('grp', 'ctx')), may hold values from 0 to 127, all different within a row; in each aligned block of 128 rows (0 to 127, 128 to 255, ...) at most 12 rows name the same one
- gates: float32 [4096, 8], P(('grp', 'ctx')), may hold values from 0.05 to 0.3
- w_gate_experts: bfloat16 [128, 2048, 768], P(('grp', 'ctx')), may hold values from -0.125 to 0.125
- w_up_experts: bfloat16 [128, 2048, 768], P(('grp', 'ctx')), may hold values from -0.125 to 0.125
- w_down_experts: bfloat16 [128, 768, 2048], P(('grp', 'ctx')), may hold values from -0.21875 to 0.21875
Outputs:
- layer_out: bfloat16 [4096, 2048], P(('grp', 'ctx'))
Inputs may be any that keep to these rules, and one draw needn't show every extreme that they name: `expert_ids`: each row names 8 different experts; among the 128 rows of one device no expert is named more than 12 times, a bound that some block reaches.
All inputs are finite; a program needn't handle non-finite values.
Results may differ from a plain program's by a relative error of at most 0.015.
Values may be sent and summed in bfloat16 or wider, within the bound.
No kernel may reach another device: no remote copies, remote signals or barrier semaphores. Data moves between devices by JAX's collectives and lax.ppermute only.
A program may use at most 128 MiB of HBM per device.

v0:
```python
import math

import jax
import jax.numpy as jnp
from jax import lax
from jax.sharding import PartitionSpec as P

H = 32
KV_HEADS = 4
HEAD_DIM = 128
EXPERTS = 128
TOPK = 8
CAP = 12


masked_score = -1e30


def softmax_step(running, grouped, key_block, value_block, key_position, query_position, scaling):
    top_score, total_weight, weighted = running
    scores = (
        jnp.einsum("gqd,gkd->gqk", grouped, key_block, preferred_element_type=jnp.float32) * scaling
    )
    allowed = key_position[None, None, :] <= query_position[None, :, None]
    scores = jnp.where(allowed, scores, masked_score)
    fresh_top = jnp.maximum(top_score, jnp.max(scores, axis=2))
    weights = jnp.where(allowed, jnp.exp(scores - fresh_top[:, :, None]), 0.0).astype(jnp.bfloat16)
    factor = jnp.exp(top_score - fresh_top)
    total_weight = total_weight * factor + jnp.sum(weights, axis=2, dtype=jnp.float32)
    weighted = weighted * factor[:, :, None] + jnp.einsum(
        "gqk,gkd->gqd", weights, value_block, preferred_element_type=jnp.float32
    )
    return (fresh_top, total_weight, weighted)


def per_device(
    tokens,
    queries,
    keys_values,
    out_weight,
    moe_gain,
    expert_ids,
    gates,
    w_gate_experts,
    w_up_experts,
    w_down_experts,
):
    tok_count = tokens.shape[0]
    ctx_count = lax.axis_size("ctx")
    kv_width = keys_values.shape[2] // 2
    group_heads = H // KV_HEADS
    keys_total = keys_values.shape[1] * ctx_count
    query_position = (
        keys_total
        - tok_count * ctx_count
        + lax.axis_index("ctx") * tok_count
        + jnp.arange(tok_count, dtype=jnp.int32)
    )
    query_tiled = jnp.tile(query_position, group_heads)
    grouped = (
        queries.reshape(tok_count, KV_HEADS, group_heads, HEAD_DIM)
        .transpose(1, 2, 0, 3)
        .reshape(KV_HEADS, group_heads * tok_count, HEAD_DIM)
    )
    scaling = 1.0 / math.sqrt(HEAD_DIM)
    query_rows = group_heads * tok_count
    initial = (
        jnp.full((KV_HEADS, query_rows), masked_score, jnp.float32),
        jnp.zeros((KV_HEADS, query_rows), jnp.float32),
        jnp.zeros((KV_HEADS, query_rows, HEAD_DIM), jnp.float32),
    )
    piece = lax.all_gather(keys_values, "ctx", axis=1, tiled=True)
    length = piece.shape[1]
    block_size = 1024

    def one_block(index, state):
        offset = index * block_size
        window = lax.dynamic_slice_in_dim(piece[0], offset, block_size, 0)
        key_block = window[:, :kv_width].reshape(block_size, KV_HEADS, HEAD_DIM).transpose(1, 0, 2)
        value_block = (
            window[:, kv_width:].reshape(block_size, KV_HEADS, HEAD_DIM).transpose(1, 0, 2)
        )
        key_position = offset + jnp.arange(block_size, dtype=jnp.int32)
        return softmax_step(
            state, grouped, key_block, value_block, key_position, query_tiled, scaling
        )

    top_score, total_weight, weighted = lax.fori_loop(0, length // block_size, one_block, initial)
    attended = (
        (weighted / total_weight[:, :, None])
        .reshape(KV_HEADS, group_heads, tok_count, HEAD_DIM)
        .transpose(2, 0, 1, 3)
        .reshape(tok_count, H * HEAD_DIM)
        .astype(jnp.bfloat16)
    )
    head_parts = lax.all_to_all(attended, "grp", split_axis=1, concat_axis=0, tiled=True)
    projected = lax.psum_scatter(
        jnp.dot(head_parts, out_weight, preferred_element_type=jnp.float32).astype(jnp.bfloat16),
        "grp",
        scatter_dimension=0,
        tiled=True,
    ).astype(jnp.float32)
    residual = (tokens.astype(jnp.float32) + projected).astype(jnp.bfloat16)
    wide = residual.astype(jnp.float32)
    normed = (
        wide * lax.rsqrt(jnp.mean(wide * wide, axis=1, keepdims=True) + 1e-06) * moe_gain
    ).astype(jnp.bfloat16)
    flat_ids = expert_ids.reshape(-1)
    one_hot = (flat_ids[:, None] == jnp.arange(EXPERTS, dtype=jnp.int32)[None, :]).astype(jnp.int32)
    slot_index = jnp.sum((jnp.cumsum(one_hot, axis=0) - one_hot) * one_hot, axis=1)
    position = flat_ids * CAP + slot_index
    token_index = jnp.arange(tok_count * TOPK, dtype=jnp.int32) // TOPK
    table = jnp.full((EXPERTS * CAP,), tok_count, jnp.int32).at[position].set(token_index)
    present = table < tok_count
    outgoing = jnp.where(present[:, None], normed[jnp.minimum(table, tok_count - 1)], 0.0)
    local_experts = w_gate_experts.shape[0]
    owners = EXPERTS // local_experts
    width = normed.shape[1]
    outgoing = outgoing.reshape(owners, local_experts, CAP, width)
    incoming = lax.all_to_all(outgoing, ("grp", "ctx"), split_axis=0, concat_axis=0, tiled=True)
    gate_part = jnp.einsum(
        "sjcd,jdf->sjcf", incoming, w_gate_experts, preferred_element_type=jnp.float32
    )
    up_part = jnp.einsum(
        "sjcd,jdf->sjcf", incoming, w_up_experts, preferred_element_type=jnp.float32
    )
    hidden = (jax.nn.silu(gate_part) * up_part).astype(jnp.bfloat16)
    result_rows = jnp.einsum(
        "sjcf,jfd->sjcd", hidden, w_down_experts, preferred_element_type=jnp.float32
    ).astype(jnp.bfloat16)
    returned = lax.all_to_all(result_rows, ("grp", "ctx"), split_axis=0, concat_axis=0, tiled=True)
    picked = returned.reshape(EXPERTS * CAP, width)[position].reshape(tok_count, TOPK, width)
    combined = jnp.sum(picked.astype(jnp.float32) * gates[:, :, None], axis=1)
    return (wide + combined).astype(jnp.bfloat16)


def solution(mesh):
    return jax.shard_map(
        per_device,
        mesh=mesh,
        in_specs=(
            P(("grp", "ctx"), None),
            P(("grp", "ctx"), None),
            P("grp", "ctx", None),
            P("grp", None),
            P(),
            P(("grp", "ctx"), None),
            P(("grp", "ctx"), None),
            P(("grp", "ctx"), None, None),
            P(("grp", "ctx"), None, None),
            P(("grp", "ctx"), None, None),
        ),
        out_specs=P(("grp", "ctx"), None),
        check_vma=False,
    )
```

profile of v0, /device:TPU:0, one launch (start us, length us, event | category | flops | bytes accessed | tf_op | source)
XLA Modules:
  0.0 615.3 jit_solution(13399219058795606794)
XLA Ops:
  6.5 2.0 copy.64
  8.7 1.4 copy.83
  11.6 47.9 %all-gather.2.cloned.1.call-done = bf16[1,2048,1024]{1,2,0:T(8,128)(2,1)} async-done(((bf16[1,256,1024]{1,2,0:T(8,128)(2,1)}), bf16[1,2048,1024]{1,2,0:T(8,128)(2,1)}) %all-gather.2.cloned.1.call-update) | async-done | bytes 4194320 | tf_op jit(solution)/shard_map/all_gather | solution.py:72
  59.5 62.2 %while.18 = (s32[]{:T(128)}, f32[4,1024]{1,0:T(4,128)S(1)}, f32[4,1024]{1,0:T(4,128)S(1)}, f32[4,1024,128]{2,1,0:T(8,128)}, bf16[1,2048,1024]{1,2,0:T(8,128)(2,1...) while((s32[]{:T(128)}, f32[4,1024]{1,0:T(4,128)S(1)}, ...), condition=%wide.region_3.4_spmd.clone, body=%wide.region_0.3_spmd.clone.sunk | while | flops 2213041152 | bytes 74728112 | solution.py:88
  59.5 1.8 dynamic-slice_bitcast_fusion.2
  62.8 8.6 %fusion.60 = (f32[4,1024]{1,0:T(4,128)S(1)}, f32[4,1024,1024]{2,1,0:T(8,128)}) fusion(pred[1024,1024]{0,1:T(8,128)(4,1)S(1)} %broadcast_compare_fusion.3, bf16[4,1024,128]{2,1,0:T(8,128)(2,1)} %get-tuple-element.261, bf16[1024,4,128]{2,0,1:T(8,128)(2,1)S(1)} %copy.94), kind=kOutput, calls=%fused_computation.7.clone.1 | convolution fusion | flops 1086320640 | bytes 19939328 | tf_op jit(solution)/shard_map/while/body/eval_jaxpr/gqd,gkd->gqk/dot_general | solution.py:22
  71.4 8.0 %convert_reduce_fusion.2 = f32[4,1024]{1,0:T(4,128)S(1)} fusion(f32[4,1024]{1,0:T(4,128)S(1)} %select_maximum_fusion.2, f32[4,1024,1024]{2,1,0:T(8,128)} %get-tuple-element.230, pred[1024,1024]{0,1:T(8,128)(4,1)S(1)} %broadcast_compare_fusion.3), kind=kLoop, calls=%fused_computation.5.clone.1 | loop fusion | flops 29356032 | bytes 17858560 | tf_op jit(solution)/shard_map/while/body/eval_jaxpr/reduce_sum | solution.py:29
  80.1 10.4 %fusion.62 = f32[4,1024,128]{2,1,0:T(8,128)} fusion(f32[4,1024,128]{2,1,0:T(8,128)} %get-tuple-element.248, bf16[1024,4,128]{2,0,1:T(8,128)(2,1)S(1)} %copy.95, f32[4,1024]{1,0:T(4,128)S(1)} %get-tuple-element.233, pred[]{:T(512)S(6)} %compare.5, f32[4,1024,1024]{2,1,0:T(8,128)} %get-tuple-element.230, f32[4,1024]{1,0:T(4,128)S(1)} %select_maximum_fusion.2, ...), kind=kOutput, calls=%fused_computation.9.clone.1 | convolution fusion | flops 1096286208 | bytes 23101440 | tf_op jit(solution)/shard_map/while/body/eval_jaxpr/gqk,gkd->gqd/dot_general | solution.py:30
  90.5 1.8 dynamic-slice_bitcast_fusion.2
  93.8 8.6 %fusion.60 = (f32[4,1024]{1,0:T(4,128)S(1)}, f32[4,1024,1024]{2,1,0:T(8,128)}) fusion(pred[1024,1024]{0,1:T(8,128)(4,1)S(1)} %broadcast_compare_fusion.3, bf16[4,1024,128]{2,1,0:T(8,128)(2,1)} %get-tuple-element.261, bf16[1024,4,128]{2,0,1:T(8,128)(2,1)S(1)} %copy.94), kind=kOutput, calls=%fused_computation.7.clone.1 | convolution fusion | flops 1086320640 | bytes 19939328 | tf_op jit(solution)/shard_map/while/body/eval_jaxpr/gqd,gkd->gqk/dot_general | solution.py:22
  102.4 8.0 %convert_reduce_fusion.2 = f32[4,1024]{1,0:T(4,128)S(1)} fusion(f32[4,1024]{1,0:T(4,128)S(1)} %select_maximum_fusion.2, f32[4,1024,1024]{2,1,0:T(8,128)} %get-tuple-element.230, pred[1024,1024]{0,1:T(8,128)(4,1)S(1)} %broadcast_compare_fusion.3), kind=kLoop, calls=%fused_computation.5.clone.1 | loop fusion | flops 29356032 | bytes 17858560 | tf_op jit(solution)/shard_map/while/body/eval_jaxpr/reduce_sum | solution.py:29
  111.1 10.6 %fusion.62 = f32[4,1024,128]{2,1,0:T(8,128)} fusion(f32[4,1024,128]{2,1,0:T(8,128)} %get-tuple-element.248, bf16[1024,4,128]{2,0,1:T(8,128)(2,1)S(1)} %copy.95, f32[4,1024]{1,0:T(4,128)S(1)} %get-tuple-element.233, pred[]{:T(512)S(6)} %compare.5, f32[4,1024,1024]{2,1,0:T(8,128)} %get-tuple-element.230, f32[4,1024]{1,0:T(4,128)S(1)} %select_maximum_fusion.2, ...), kind=kOutput, calls=%fused_computation.9.clone.1 | convolution fusion | flops 1096286208 | bytes 23101440 | tf_op jit(solution)/shard_map/while/body/eval_jaxpr/gqk,gkd->gqd/dot_general | solution.py:30
  121.7 2.0 divide_convert_fusion
  124.4 18.6 %all_to_all.26 = bf16[128,4,1024]{0,2,1:T(8,128)(2,1)S(1)} all-to-all(bf16[128,4,1024]{0,2,1:T(8,128)(2,1)S(1)} %bitcast.121), channel_id=1, replica_groups=mesh['grp'=4,'ctx'=8] {'grp'}, dimensions={1} | all-to-all | bytes 2097152 | tf_op jit(solution)/shard_map/all_to_all | solution.py:96
  143.5 5.9 convolution_convert_fusion
  150.8 4.3 scatter_custom_fusion
  155.3 26.2 %reduce-scatter.2.cloned.1.call-done = bf16[128,2048]{1,0:T(8,128)(2,1)} async-done(((bf16[512,2048]{1,0:T(8,128)(2,1)}), bf16[128,2048]{1,0:T(8,128)(2,1)}) %reduce-scatter.2.cloned.1.call-update) | async-done | bytes 524304 | tf_op jit(solution)/shard_map/reduce_scatter | solution.py:97
  184.1 7.1 %gather_fusion = bf16[1536,2048]{1,0:T(8,128)(2,1)} fusion(bf16[128,2048]{1,0:T(8,128)(2,1)S(1)} %fusion.34, s32[2048]{0:T(1024)S(1)} %pad_clamp_fusion), kind=kCustom, calls=%fused_computation | custom fusion | bytes 12589056 | tf_op jit(solution)/shard_map/gather | solution.py:115
  191.2 10.6 %gather.9 = bf16[32,4,12,2048]{3,2,1,0:T(8,128)(2,1)} reshape(bf16[1536,2048]{1,0:T(8,128)(2,1)} %gather_fusion) | data formatting | bytes 12582912 | tf_op jit(solution)/shard_map/gather | solution.py:115
  201.8 7.3 %broadcast_select_fusion = bf16[32,4,12,2048]{3,2,1,0:T(8,128)(2,1)} fusion(bf16[32,4,12,2048]{3,2,1,0:T(8,128)(2,1)} %gather.9, pred[32,4,12]{2,1,0:T(4,128)(4,1)S(1)} %broadcast_in_dim.82), kind=kLoop, calls=%fused_computation.29 | loop fusion | flops 3145728 | bytes 12584448 | tf_op jit(solution)/shard_map/jit(_where)/select_n | solution.py:115
  209.0 12.1 %copy.73 = bf16[32,4,12,2048]{3,1,2,0:T(4,128)(2,1)} copy(bf16[32,4,12,2048]{3,2,1,0:T(8,128)(2,1)} %broadcast_select_fusion) | data formatting | bytes 12582912 | tf_op jit(solution)/shard_map/jit(_where)/select_n | solution.py:115
  221.1 144.7 %all_to_all.27 = bf16[32,4,12,2048]{3,1,2,0:T(4,128)(2,1)S(1)} all-to-all(bf16[32,4,12,2048]{3,1,2,0:T(4,128)(2,1)} %copy.73), channel_id=1, replica_groups=mesh['grp'=4,'ctx'=8] {'grp','ctx'}, dimensions={0} | all-to-all | bytes 12582912 | tf_op jit(solution)/shard_map/all_to_all | solution.py:120
  365.8 2.7 copy-done
  368.5 14.5 %fusion.10 = f32[4,32,12,768]{3,1,2,0:T(8,128)} fusion(bf16[4,2048,768]{2,1,0:T(8,128)(2,1)} %param.20, bf16[32,4,12,2048]{3,1,2,0:T(4,128)(2,1)S(1)} %all_to_all.27), kind=kOutput, calls=%fused_computation.23 | convolution fusion | flops 4831838208 | bytes 23592960 | tf_op jit(solution)/shard_map/sjcd,jdf->sjcf/dot_general | solution.py:124
  382.9 28.4 %convert_bitcast_fusion = bf16[32,4,12,2048]{3,0,2,1:T(8,128)(2,1)} fusion(bf16[4,768,2048]{2,1,0:T(8,128)(2,1)} %param.21, f32[4,32,12,768]{3,1,2,0:T(8,128)} %fusion.10, bf16[4,2048,768]{2,1,0:T(8,128)(2,1)} %param.19, bf16[32,4,12,2048]{3,1,2,0:T(4,128)(2,1)} %copy-done), kind=kOutput, calls=%fused_computation.30 | convolution fusion | flops 9673900032 | bytes 42467328 | tf_op jit(solution)/shard_map/sjcf,jfd->sjcd/dot_general | solution.py:128
  411.3 10.2 %copy.76 = bf16[32,4,12,2048]{3,1,2,0:T(4,128)(2,1)} copy(bf16[32,4,12,2048]{3,0,2,1:T(8,128)(2,1)} %convert_bitcast_fusion) | data formatting | bytes 12582912 | tf_op jit(solution)/shard_map/convert_element_type | solution.py:130
  421.5 4.0 all-to-all-start.2
  425.7 139.8 %all-to-all-done.2 = bf16[32,4,12,2048]{3,1,2,0:T(4,128)(2,1)} async-done(((bf16[32,4,12,2048]{3,1,2,0:T(4,128)(2,1)}), bf16[32,4,12,2048]{3,1,2,0:T(4,128)(2,1)}, u32[]{:S(2)}, u32[]{:S(2)}) %all-to-all-start.2) | async-done | bytes 6291488 | tf_op jit(solution)/shard_map/all_to_all | solution.py:131
  565.5 11.5 %copy.77 = bf16[32,4,12,2048]{3,2,1,0:T(8,128)(2,1)} copy(bf16[32,4,12,2048]{3,1,2,0:T(4,128)(2,1)} %all-to-all-done.2) | data formatting | bytes 12582912 | tf_op jit(solution)/shard_map/all_to_all | solution.py:131
  577.0 10.7 %reshape.153 = bf16[1536,2048]{1,0:T(8,128)(2,1)} reshape(bf16[32,4,12,2048]{3,2,1,0:T(8,128)(2,1)} %copy.77) | data formatting | bytes 12582912 | tf_op jit(solution)/shard_map/reshape | solution.py:132
  587.7 12.7 %gather_fusion.1 = bf16[1024,2048]{1,0:T(8,128)(2,1)} fusion(bf16[1536,2048]{1,0:T(8,128)(2,1)} %reshape.153, s32[1024]{0:T(1024)S(1)} %broadcast_clamp_fusion), kind=kCustom, calls=%fused_computation.1 | custom fusion | bytes 8392704 | tf_op jit(solution)/shard_map/gather | solution.py:132
  600.4 6.5 %fusion.14 = f32[128,2048]{1,0:T(8,128)S(1)} fusion(bf16[1024,2048]{1,0:T(8,128)(2,1)} %gather_fusion.1, f32[128,8]{1,0:T(8,128)S(1)} %copy.78), kind=kLoop, calls=%fused_computation.28 | loop fusion | flops 6029312 | bytes 5246976 | tf_op jit(solution)/shard_map/reduce_sum | solution.py:133
  (66 shorter events, 12.2 us)
Async XLA Ops:
  6.5 52.9 %all-gather.2.cloned.1.call-start = ((), (), s32[]{:S(2)}) async-start(), calls=%async_computation.4 | async-start | bytes 4718592 | tf_op jit(solution)/shard_map/all_gather | solution.py:72
  8.6 172.9 %reduce-scatter.2.cloned.1.call-start = ((), (), s32[]{:S(2)}) async-start(), calls=%async_computation.5 | async-start | bytes 2621440 | tf_op jit(solution)/shard_map/reduce_scatter | solution.py:97
  143.4 6.0 copy-start.3
  143.5 38.1 %copy-start.1 = (bf16[128,2048]{1,0:T(8,128)(2,1)S(1)}, bf16[128,2048]{1,0:T(8,128)(2,1)}, u32[]{:S(2)}) copy-start(bf16[128,2048]{1,0:T(8,128)(2,1)} %param.12) | copy-start | bytes 1572868
  149.4 33.4 %copy-start.4 = (f32[2048]{0:T(1024)S(1)}, f32[2048]{0:T(1024)}, u32[]{:S(2)}) copy-start(f32[2048]{0:T(1024)} %param.16) | copy-start | bytes 24580
  365.8 2.7 copy-start
  421.5 4.0 copy-start.5
  421.5 144.0 %all-to-all-start.2 = ((bf16[32,4,12,2048]{3,1,2,0:T(4,128)(2,1)}), bf16[32,4,12,2048]{3,1,2,0:T(4,128)(2,1)}, u32[]{:S(2)}, u32[]{:S(2)}) async-start(bf16[32,4,12,2048]{3,1,2,0:T(4,128)(2,1)} %copy.76), calls=%async_computation.3 | async-start | bytes 12582912 | tf_op jit(solution)/shard_map/all_to_all | solution.py:131
  587.7 19.3 %copy-start.2 = (bf16[128,2048]{1,0:T(8,128)(2,1)S(1)}, bf16[128,2048]{1,0:T(8,128)(2,1)}, u32[]{:S(2)}) copy-start(bf16[128,2048]{1,0:T(8,128)(2,1)} %reduce-scatter.2.cloned.1.call-done) | copy-start | bytes 1572868
Sparse Core Ops, SparseCore 0:
  8.9 50.4 all-gather.1
  149.6 31.9 reduce-scatter.1
where the time goes:
time: 623 us; the launch traced here: 615 us
  waiting for transfers between devices  214 us (34%)
  blocking collectives  163 us (26%)
  local copies, waits for them, and re-layouts  95.4 us (15%)
  matrix products  87 us (14%)
  other arithmetic  37.4 us (6%)
  between operations  14.1 us (2%)
    all_to_all x1, blocking collectives, per_device(): lax.all_to_all(outgoing, ('grp', 'ctx'), split_axis=0, concat_axis=0, til...  145 us
    all_to_all x1, waiting for transfers between devices, per_device(): lax.all_to_all(result_rows, ('grp', 'ctx'), split_axis=0, concat_axis=0,...  140 us
    all_gather x1, waiting for transfers between devices, per_device(): piece = lax.all_gather(keys_values, 'ctx', axis=1, tiled=True)  47.9 us
    dot_general x1, matrix products, per_device(): jnp.einsum('sjcf,jfd->sjcd', hidden, w_down_experts, preferred_element_ty...  28.4 us
    reduce_scatter x1, waiting for transfers between devices, per_device(): lax.psum_scatter(jnp.dot(head_parts, out_weight, preferred_element_type=j...  26.2 us
    dot_general x2, matrix products, softmax_step(): jnp.einsum('gqk,gkd->gqd', weights, value_block, preferred_element_type=j...  21 us
    all_to_all x1, blocking collectives, per_device(): lax.all_to_all(attended, 'grp', split_axis=1, concat_axis=0, tiled=True)  18.6 us
    gather x2, local copies, waits for them, and re-layouts, per_device(): normed[jnp.minimum(table, tok_count - 1)]  17.7 us
  transfers between devices with their start and end apart: 3, of which 3 were waited for; matrix products, arithmetic and copies ran while one was open for 1% of the time, Pallas kernels for 0%

commit v1 on v0

v1 whole, which is shorter than its diff:
```python
import functools
import math

import jax
import jax.numpy as jnp
from jax import lax
from jax.experimental import pallas as pl
from jax.experimental.pallas import tpu as pltpu
from jax.sharding import PartitionSpec as P

H = 32
KV_HEADS = 4
HEAD_DIM = 128
EXPERTS = 128
TOPK = 8
CAP = 12

CHUNKS = 2
VMEM_LIMIT = 56 * 1024 * 1024


def attention_kernel(base_ref, q_ref, k_ref, v_ref, o_ref, *, heads, stack, old):
    rows = q_ref.shape[0]
    keys = k_ref.shape[0]
    factor = math.log2(math.e) / math.sqrt(HEAD_DIM)
    key = k_ref[...]
    value = jnp.concatenate([v_ref[...], jnp.ones_like(v_ref)], axis=1)
    late = (stack * rows, keys - old)
    row = lax.broadcasted_iota(jnp.int32, late, 0) % rows
    allowed = lax.broadcasted_iota(jnp.int32, late, 1) + old <= row + base_ref[0]
    for first in range(0, heads, stack):
        query = jnp.concatenate(
            [q_ref[:, h * HEAD_DIM : (h + 1) * HEAD_DIM] for h in range(first, first + stack)],
            axis=0,
        )
        scores = lax.dot_general(
            query, key, (((1,), (1,)), ((), ())), preferred_element_type=jnp.float32
        )
        scores = jnp.concatenate(
            [scores[:, :old], jnp.where(allowed, scores[:, old:], -1e30)], axis=1
        )
        top = jnp.max(scores, axis=1, keepdims=True)
        weights = jnp.exp2((scores - top) * factor).astype(jnp.bfloat16)
        summed = jnp.dot(weights, value, preferred_element_type=jnp.float32)
        out = (summed[:, :HEAD_DIM] / summed[:, HEAD_DIM:]).astype(o_ref.dtype)
        for i in range(stack):
            h = first + i
            o_ref[:, h * HEAD_DIM : (h + 1) * HEAD_DIM] = out[i * rows : (i + 1) * rows]


def attention(queries, keys_values, base, old):
    rows = queries.shape[0]
    keys = keys_values.shape[0]
    heads = H // KV_HEADS
    wide = heads * HEAD_DIM
    return pl.pallas_call(
        functools.partial(attention_kernel, heads=heads, stack=2, old=old),
        grid=(KV_HEADS,),
        in_specs=[
            pl.BlockSpec(memory_space=pltpu.SMEM),
            pl.BlockSpec((rows, wide), lambda j: (0, j)),
            pl.BlockSpec((keys, HEAD_DIM), lambda j: (0, j)),
            pl.BlockSpec((keys, HEAD_DIM), lambda j: (0, KV_HEADS + j)),
        ],
        out_specs=pl.BlockSpec((rows, wide), lambda j: (0, j)),
        out_shape=jax.ShapeDtypeStruct(queries.shape, jnp.bfloat16),
        compiler_params=pltpu.CompilerParams(vmem_limit_bytes=VMEM_LIMIT),
        cost_estimate=pl.CostEstimate(
            flops=4 * rows * H * keys * HEAD_DIM,
            bytes_accessed=2 * keys_values.size + 4 * queries.size,
            transcendentals=rows * H * keys,
        ),
        name="attention",
    )(base, queries, keys_values, keys_values)


def hidden_kernel(*refs, peers, chunks):
    x_refs = refs[: peers * chunks]
    gate_ref, up_ref, h_ref = refs[peers * chunks :]
    gate = up = None
    for c in range(chunks):
        part = jnp.concatenate([x_refs[c * peers + k][0] for k in range(peers)], axis=0)
        width = part.shape[1]
        span = slice(c * width, (c + 1) * width)
        g = jnp.dot(part, gate_ref[0, span, :], preferred_element_type=jnp.float32)
        u = jnp.dot(part, up_ref[0, span, :], preferred_element_type=jnp.float32)
        gate = g if gate is None else gate + g
        up = u if up is None else up + u
    h_ref[0] = (gate / (1.0 + jnp.exp(-gate)) * up).astype(h_ref.dtype)


def expert_hidden(parts, w_gate, w_up):
    chunks, peers = len(parts), len(parts[0])
    local, slots, width = parts[0][0].shape
    depth, inner = w_gate.shape[1:]
    rows = peers * slots
    return pl.pallas_call(
        functools.partial(hidden_kernel, peers=peers, chunks=chunks),
        grid=(local,),
        in_specs=[pl.BlockSpec((1, slots, width), lambda j: (j, 0, 0))] * (peers * chunks)
        + [pl.BlockSpec((1, depth, inner), lambda j: (j, 0, 0))] * 2,
        out_specs=pl.BlockSpec((1, rows, inner), lambda j: (j, 0, 0)),
        out_shape=jax.ShapeDtypeStruct((local, rows, inner), jnp.bfloat16),
        compiler_params=pltpu.CompilerParams(vmem_limit_bytes=VMEM_LIMIT),
        cost_estimate=pl.CostEstimate(
            flops=4 * local * rows * depth * inner,
            bytes_accessed=4 * w_gate.size + 2 * local * rows * (depth + inner),
            transcendentals=local * rows * inner,
        ),
        name="expert_hidden",
    )(*[x for part in parts for x in part], w_gate, w_up)


def down_kernel(h_ref, w_ref, *y_refs):
    slots = y_refs[0].shape[1]
    out = jnp.dot(h_ref[0], w_ref[0], preferred_element_type=jnp.float32).astype(jnp.bfloat16)
    for k, y_ref in enumerate(y_refs):
        y_ref[0] = out[k * slots : (k + 1) * slots]


def expert_down(hidden, w_down, chunk, chunks, peers):
    local, rows, inner = hidden.shape
    width = w_down.shape[2] // chunks
    slots = rows // peers
    return pl.pallas_call(
        down_kernel,
        grid=(local,),
        in_specs=[
            pl.BlockSpec((1, rows, inner), lambda j: (j, 0, 0)),
            pl.BlockSpec((1, inner, width), lambda j: (j, 0, chunk)),
        ],
        out_specs=[pl.BlockSpec((1, slots, width), lambda j: (j, 0, 0))] * peers,
        out_shape=[jax.ShapeDtypeStruct((local, slots, width), jnp.bfloat16)] * peers,
        compiler_params=pltpu.CompilerParams(vmem_limit_bytes=VMEM_LIMIT),
        cost_estimate=pl.CostEstimate(
            flops=2 * local * rows * width * inner,
            bytes_accessed=2 * local * (inner * width + rows * (inner + width)),
            transcendentals=0,
        ),
        name="expert_down",
    )(hidden, w_down)


def swap(value, k, peers):
    if k == 0:
        return value
    return lax.ppermute(value, "grp", [(i, i ^ k) for i in range(peers)])


def per_device(
    tokens,
    queries,
    keys_values,
    out_weight,
    moe_gain,
    expert_ids,
    gates,
    w_gate_experts,
    w_up_experts,
    w_down_experts,
):
    tok_count, width = tokens.shape
    ctx_count = lax.axis_size("ctx")
    peers = lax.axis_size("grp")
    here, me = lax.axis_index("ctx"), lax.axis_index("grp")
    local = w_gate_experts.shape[0]
    slots = ctx_count * CAP
    column = ctx_count * tok_count
    chunk_width = width // CHUNKS

    gathered = lax.all_gather(keys_values[0], "ctx", axis=0, tiled=True)
    old = gathered.shape[0] - column
    base = (old + here * tok_count).astype(jnp.int32).reshape(1)
    attended = attention(queries, gathered, base, old)

    packed = jnp.concatenate([expert_ids.astype(jnp.float32), gates], axis=1)
    packed, _ = lax.optimization_barrier((packed, gathered))
    routes = lax.all_gather(packed, "ctx", axis=0, tiled=True).T
    ids, gate_rows = routes[:TOPK].astype(jnp.int32), routes[TOPK:]
    owner = me ^ jnp.arange(peers, dtype=jnp.int32)
    wanted = (
        ((owner * ctx_count + here) * local)[:, None] + jnp.arange(local, dtype=jnp.int32)[None, :]
    ).reshape(-1)
    same = ids[None, :, :] == wanted[:, None, None]
    named = jnp.any(same, axis=1)
    gate_of = jnp.sum(jnp.where(same, gate_rows[None], 0.0), axis=1)
    earlier = jnp.triu(jnp.ones((tok_count, tok_count), jnp.bfloat16), 1)
    rank = jnp.einsum(
        "ebt,tu->ebu",
        named.reshape(-1, ctx_count, tok_count).astype(jnp.bfloat16),
        earlier,
        preferred_element_type=jnp.float32,
    ).astype(jnp.int32)
    place = rank + (jnp.arange(ctx_count, dtype=jnp.int32) * CAP)[None, :, None]
    place = jnp.where(named, place.reshape(-1, column), -1)
    hit = place[:, None, :] == jnp.arange(slots, dtype=jnp.int32)[None, :, None]
    pick = hit.astype(jnp.bfloat16).reshape(peers, local * slots, column)
    mix = jnp.where(hit, gate_of[:, None, :], 0.0).astype(jnp.bfloat16)
    mix = mix.reshape(peers, local * slots, column)

    head_parts = lax.all_to_all(attended, "grp", split_axis=1, concat_axis=0, tiled=True)
    projected = lax.psum_scatter(
        jnp.dot(head_parts, out_weight, preferred_element_type=jnp.float32).astype(jnp.bfloat16),
        "grp",
        scatter_dimension=0,
        tiled=True,
    ).astype(jnp.float32)
    residual = (tokens.astype(jnp.float32) + projected).astype(jnp.bfloat16)
    wide = residual.astype(jnp.float32)
    normed = (
        wide * lax.rsqrt(jnp.mean(wide * wide, axis=1, keepdims=True) + 1e-06) * moe_gain
    ).astype(jnp.bfloat16)

    parts = []
    for c in range(CHUNKS):
        piece = normed[:, c * chunk_width : (c + 1) * chunk_width]
        block = lax.all_gather(piece, "ctx", axis=0, tiled=True)
        received = []
        for k in reversed(range(peers)):
            rows = jnp.dot(pick[k], block, preferred_element_type=jnp.float32)
            received.append(swap(rows.astype(jnp.bfloat16), k, peers))
        parts.append([r.reshape(local, slots, chunk_width) for r in reversed(received)])
    hidden = expert_hidden(parts, w_gate_experts, w_up_experts)

    outs = []
    for c in range(CHUNKS):
        rows = expert_down(hidden, w_down_experts, c, CHUNKS, peers)
        back = [swap(rows[k], k, peers) for k in reversed(range(peers))][::-1]
        total = sum(
            lax.dot_general(
                mix[k],
                back[k].reshape(local * slots, chunk_width),
                (((0,), (0,)), ((), ())),
                preferred_element_type=jnp.float32,
            )
            for k in range(peers)
        ).astype(jnp.bfloat16)
        mine = lax.psum_scatter(total, "ctx", scatter_dimension=0, tiled=True)
        outs.append(wide[:, c * chunk_width : (c + 1) * chunk_width] + mine.astype(jnp.float32))
    return jnp.concatenate(outs, axis=1).astype(jnp.bfloat16)


def solution(mesh):
    return jax.shard_map(
        per_device,
        mesh=mesh,
        in_specs=(
            P(("grp", "ctx"), None),
            P(("grp", "ctx"), None),
            P("grp", "ctx", None),
            P("grp", None),
            P(),
            P(("grp", "ctx"), None),
            P(("grp", "ctx"), None),
            P(("grp", "ctx"), None, None),
            P(("grp", "ctx"), None, None),
            P(("grp", "ctx"), None, None),
        ),
        out_specs=P(("grp", "ctx"), None),
        check_vma=False,
    )
```

time: 623 us -> 394 us (0.63); the launches traced: 615 us -> 393 us
  blocking collectives: 163 us -> 32.3 us
  local copies, waits for them, and re-layouts: 95.4 us -> 4.75 us
  matrix products: 87 us -> 35.9 us
  Pallas kernels: 0 us -> 45.2 us
  other arithmetic: 37.4 us -> 6.05 us
  waiting for transfers between devices: 214 us -> 241 us
  starting transfers between devices: 4.05 us -> 14.4 us
    all_to_all x1 -> x0, blocking collectives: 145 us -> none  [per_device(): lax.all_to_all(outgoing, ('grp', 'ctx'), split_axis=0, concat_axis=0, til...]
    all_to_all x1 -> x0, waiting for transfers between devices: 140 us -> none  [per_device(): lax.all_to_all(result_rows, ('grp', 'ctx'), split_axis=0, concat_axis=0,...]
    ppermute x0 -> x12, waiting for transfers between devices: none -> 89.7 us  [swap(): return lax.ppermute(value, 'grp', [(i, i ^ k) for i in range(peers)])]
    dot_general x6 -> x17, matrix products: 81.1 us -> 32.2 us  [the longest x8 16 us: per_device(): lax.dot_general(mix[k], back[k].reshape(local * slots, chunk_width), (((0...]
    pallas_call x0 -> x4, Pallas kernels: none -> 45.2 us  [the longest x1 16 us: expert_hidden(): pl.pallas_call(functools.partial(hidden_kernel, peers=peers, chunks=chunk...]
    all_gather x1 -> x3, waiting for transfers between devices: 47.9 us -> 82.7 us  [the longest x1 51.5 us: per_device(): gathered = lax.all_gather(keys_values[0], 'ctx', axis=0, tiled=True)]
    reduce_scatter x0 -> x2, waiting for transfers between devices: none -> 34.7 us  [per_device(): mine = lax.psum_scatter(total, 'ctx', scatter_dimension=0, tiled=True)]
    gather x3 -> x0, local copies, waits for them, and re-layouts: 30.4 us -> none  [the longest x2 17.7 us: per_device(): normed[jnp.minimum(table, tok_count - 1)]]
  transfers between devices with their start and end apart: 3 -> 18, of which waited for: 3 -> 14; matrix products, arithmetic and copies ran while one was open for 1% -> 8% of each run, Pallas kernels for 0% -> 2%
where the time goes in v1:
time: 394 us; the launch traced here: 393 us
  waiting for transfers between devices  241 us (61%)
  Pallas kernels  45.2 us (11%)
  matrix products  35.9 us (9%)
  blocking collectives  32.3 us (8%)
  starting transfers between devices  14.4 us (4%)
  between operations  13.7 us (3%)
  other arithmetic  6.05 us (2%)
  local copies, waits for them, and re-layouts  4.75 us (1%)
    ppermute x12, waiting for transfers between devices, swap(): return lax.ppermute(value, 'grp', [(i, i ^ k) for i in range(peers)])  89.7 us
    all_gather x1, waiting for transfers between devices, per_device(): gathered = lax.all_gather(keys_values[0], 'ctx', axis=0, tiled=True)  51.5 us
    reduce_scatter x2, waiting for transfers between devices, per_device(): mine = lax.psum_scatter(total, 'ctx', scatter_dimension=0, tiled=True)  34.7 us
    reduce_scatter x1, waiting for transfers between devices, per_device(): lax.psum_scatter(jnp.dot(head_parts, out_weight, preferred_element_type=j...  32.5 us
    all_gather x2, waiting for transfers between devices, per_device(): block = lax.all_gather(piece, 'ctx', axis=0, tiled=True)  31.1 us
    all_to_all x1, blocking collectives, per_device(): lax.all_to_all(attended, 'grp', split_axis=1, concat_axis=0, tiled=True)  18.1 us
    dot_general x8, matrix products, per_device(): lax.dot_general(mix[k], back[k].reshape(local * slots, chunk_width), (((0...  16 us
    dot_general x8, matrix products, per_device(): rows = jnp.dot(pick[k], block, preferred_element_type=jnp.float32)  16 us
  transfers between devices with their start and end apart: 18, of which 14 were waited for; matrix products, arithmetic and copies ran while one was open for 8% of the time, Pallas kernels for 2%

profile of v1, /device:TPU:0, one launch (start us, length us, event | category | flops | bytes accessed | tf_op | source)
XLA Modules:
  0.0 393.1 jit_solution(4107666033541993068)
XLA Ops:
  7.3 51.5 %all-gather.9.cloned.1.call-done = bf16[1,2048,1024]{2,1,0:T(8,128)(2,1)} async-done(((bf16[1,256,1024]{2,1,0:T(8,128)(2,1)}), bf16[1,2048,1024]{2,1,0:T(8,128)(2,1)}) %all-gather.9.cloned.1.call-update) | async-done | bytes 4194320 | tf_op jit(solution)/shard_map/all_gather | solution.py:171
  58.8 15.1 %attention.1 = bf16[128,4096]{1,0:T(8,128)(2,1)} custom-call(s32[1]{0:T(128)} %bitcast.base_ref, bf16[128,4096]{1,0:T(8,128)(2,1)} %q_ref.1, bf16[2048,1024]{1,0:T(8,128)(2,1)} %bitcast.100, bf16[2048,1024]{1,0:T(8,128)(2,1)} %bitcast.101), custom_call_target="tpu_custom_call" | custom-call | flops 4294967296 | bytes 6291456 | tf_op jit(solution)/shard_map/attention/pallas_call | solution.py:56
  75.4 18.1 %all_to_all.19 = bf16[128,4,1024]{2,0,1:T(8,128)(2,1)S(1)} all-to-all(bf16[128,4,1024]{2,0,1:T(8,128)(2,1)S(1)} %bitcast.85), channel_id=1, replica_groups=mesh['grp'=4,'ctx'=8] {'grp'}, dimensions={1} | all-to-all | bytes 2097152 | tf_op jit(solution)/shard_map/all_to_all | solution.py:201
  93.6 3.7 convolution_convert_fusion
  97.4 32.5 %reduce-scatter.4.cloned.1.call-done = bf16[128,2048]{1,0:T(8,128)(2,1)} async-done(((bf16[512,2048]{1,0:T(8,128)(2,1)}), bf16[128,2048]{1,0:T(8,128)(2,1)}) %reduce-scatter.4.cloned.1.call-update) | async-done | bytes 524304 | tf_op jit(solution)/shard_map/reduce_scatter | solution.py:202
  134.2 14.2 %all_gather.13 = f32[1024,16]{0,1:T(8,128)S(1)} all-gather(f32[128,16]{0,1:T(8,128)S(1)} %pad_maximum_fusion.1), channel_id=1, replica_groups=mesh['grp'=4,'ctx'=8] {'ctx'}, dimensions={0}, use_global_device_ids=true | all-gather | bytes 73728 | tf_op jit(solution)/shard_map/all_gather | solution.py:178
  150.8 11.9 %all-gather.5.cloned.1.call-done = bf16[1024,1024]{1,0:T(8,128)(2,1)} async-done(((bf16[128,1024]{1,0:T(8,128)(2,1)}), bf16[1024,1024]{1,0:T(8,128)(2,1)}) %all-gather.5.cloned.1.call-update) | async-done | bytes 2097168 | tf_op jit(solution)/shard_map/all_gather | solution.py:217
  162.7 3.7 convolution_convert_fusion.7
  167.8 1.9 convolution_convert_fusion.6
  169.7 1.6 collective-permute-start.1
  171.3 1.9 convolution_convert_fusion.5
  173.6 19.2 %all-gather.7.cloned.1.call-done = bf16[1024,1024]{1,0:T(8,128)(2,1)} async-done(((bf16[128,1024]{1,0:T(8,128)(2,1)}), bf16[1024,1024]{1,0:T(8,128)(2,1)}) %all-gather.7.cloned.1.call-update) | async-done | bytes 2097168 | tf_op jit(solution)/shard_map/all_gather | solution.py:217
  192.9 2.7 convolution_convert_fusion.3
  201.4 1.9 convolution_convert_fusion.8
  203.3 1.9 convolution_convert_fusion.4
  205.2 2.1 collective-permute-done.1
  207.3 13.4 %collective-permute-done.3 = bf16[384,1024]{1,0:T(8,128)(2,1)S(1)} collective-permute-done((bf16[384,1024]{1,0:T(8,128)(2,1)S(1)}, bf16[384,1024]{1,0:T(8,128)(2,1)S(1)}, u32[]{:S(2)}, u32[]{:S(2)}) %collective-permute-start.3) | collective-permute-done | bytes 786464 | tf_op jit(solution)/shard_map/ppermute | solution.py:147
  220.7 19.2 %collective-permute-done.4 = bf16[384,1024]{1,0:T(8,128)(2,1)S(1)} collective-permute-done((bf16[384,1024]{1,0:T(8,128)(2,1)S(1)}, bf16[384,1024]{1,0:T(8,128)(2,1)S(1)}, u32[]{:S(2)}, u32[]{:S(2)}) %collective-permute-start.4) | collective-permute-done | bytes 786464 | tf_op jit(solution)/shard_map/ppermute | solution.py:147
  241.1 16.0 %expert_hidden.1.h_ref = bf16[4,384,768]{2,1,0:T(8,128)(2,1)} custom-call(bf16[4,96,1024]{2,1,0:T(8,128)(2,1)} %bitcast.106, bf16[4,96,1024]{2,1,0:T(8,128)(2,1)} %bitcast.102, bf16[4,96,1024]{2,1,0:T(8,128)(2,1)} %bitcast.11.refs_2_, bf16[4,96,1024]{2,1,0:T(8,128)(2,1)} %bitcast.13.refs_3_, bf16[4,96,1024]{2,1,0:T(8,128)(2,1)} %bitcast.107, ...), custom_call_target="tpu_custom_call" | custom-call | flops 9663676416 | bytes 33816576 | tf_op jit(solution)/shard_map/expert_hidden/pallas_call | solution.py:97
  257.1 6.9 %expert_down.2 = (bf16[4,96,1024]{2,1,0:T(8,128)(2,1)}, bf16[4,96,1024]{2,1,0:T(8,128)(2,1)}, bf16[4,96,1024]{2,1,0:T(8,128)(2,1)}, bf16[4,96,1024]{2,1,0:T(8,128)(2,1)}) custom-call(bf16[4,384,768]{2,1,0:T(8,128)(2,1)} %expert_hidden.1.h_ref, bf16[4,768,2048]{2,1,0:T(8,128)(2,1)} %w_ref.3), custom_call_target="tpu_custom_call" | custom-call | flops 2415919104 | bytes 11796480 | tf_op jit(solution)/shard_map/expert_down/pallas_call | solution.py:125
  264.0 1.6 collective-permute-start.7
  267.7 2.4 fusion.3
  270.2 13.6 %collective-permute-done.7 = bf16[4,96,1024]{2,1,0:T(8,128)(2,1)S(1)} collective-permute-done((bf16[4,96,1024]{2,1,0:T(8,128)(2,1)}, bf16[4,96,1024]{2,1,0:T(8,128)(2,1)S(1)}, u32[]{:S(2)}, u32[]{:S(2)}) %collective-permute-start.7) | collective-permute-done | bytes 786464 | tf_op jit(solution)/shard_map/ppermute | solution.py:147
  287.5 13.2 %collective-permute-done.8 = bf16[4,96,1024]{2,1,0:T(8,128)(2,1)S(1)} collective-permute-done((bf16[4,96,1024]{2,1,0:T(8,128)(2,1)}, bf16[4,96,1024]{2,1,0:T(8,128)(2,1)S(1)}, u32[]{:S(2)}, u32[]{:S(2)}) %collective-permute-start.8) | collective-permute-done | bytes 786464 | tf_op jit(solution)/shard_map/ppermute | solution.py:147
  300.7 3.0 fusion.9
  303.8 7.3 %expert_down.3 = (bf16[4,96,1024]{2,1,0:T(8,128)(2,1)}, bf16[4,96,1024]{2,1,0:T(8,128)(2,1)}, bf16[4,96,1024]{2,1,0:T(8,128)(2,1)}, bf16[4,96,1024]{2,1,0:T(8,128)(2,1)}) custom-call(bf16[4,384,768]{2,1,0:T(8,128)(2,1)} %expert_hidden.1.h_ref, bf16[4,768,2048]{2,1,0:T(8,128)(2,1)} %w_ref.3), custom_call_target="tpu_custom_call" | custom-call | flops 2415919104 | bytes 11796480 | tf_op jit(solution)/shard_map/expert_down/pallas_call | solution.py:125
  311.1 1.6 collective-permute-start.10
  314.6 2.4 fusion.7
  317.0 13.9 %collective-permute-done.10 = bf16[4,96,1024]{2,1,0:T(8,128)(2,1)S(1)} collective-permute-done((bf16[4,96,1024]{2,1,0:T(8,128)(2,1)}, bf16[4,96,1024]{2,1,0:T(8,128)(2,1)S(1)}, u32[]{:S(2)}, u32[]{:S(2)}) %collective-permute-start.10) | collective-permute-done | bytes 786464 | tf_op jit(solution)/shard_map/ppermute | solution.py:147
  334.7 11.9 %collective-permute-done.11 = bf16[4,96,1024]{2,1,0:T(8,128)(2,1)S(1)} collective-permute-done((bf16[4,96,1024]{2,1,0:T(8,128)(2,1)}, bf16[4,96,1024]{2,1,0:T(8,128)(2,1)S(1)}, u32[]{:S(2)}, u32[]{:S(2)}) %collective-permute-start.11) | collective-permute-done | bytes 786464 | tf_op jit(solution)/shard_map/ppermute | solution.py:147
  346.6 3.0 fusion.8
  349.7 34.6 %reduce-scatter.8.cloned.1.call-done = bf16[128,1024]{1,0:T(8,128)(2,1)} async-done(((bf16[1024,1024]{1,0:T(8,128)(2,1)}), bf16[128,1024]{1,0:T(8,128)(2,1)}) %reduce-scatter.8.cloned.1.call-update) | async-done | bytes 262160 | tf_op jit(solution)/shard_map/reduce_scatter | solution.py:238
  (78 shorter events, 31.5 us)
Async XLA Ops:
  6.5 52.3 %all-gather.9.cloned.1.call-start = ((), (), s32[]{:S(2)}) async-start(), calls=%async_computation.9 | async-start | bytes 4718592 | tf_op jit(solution)/shard_map/all_gather | solution.py:171
  7.3 122.6 %reduce-scatter.4.cloned.1.call-start = ((), (), s32[]{:S(2)}) async-start(), calls=%async_computation.4 | async-start | bytes 2621440 | tf_op jit(solution)/shard_map/reduce_scatter | solution.py:202
  74.0 19.6 %copy-start.4 = (bf16[1024,2048]{1,0:T(8,128)(2,1)S(1)}, bf16[1024,2048]{1,0:T(8,128)(2,1)}, u32[]{:S(2)}) copy-start(bf16[1024,2048]{1,0:T(8,128)(2,1)} %param.13) | copy-start | bytes 12582916
  93.6 36.4 %copy-start = (bf16[128,2048]{1,0:T(8,128)(2,1)S(1)}, bf16[128,2048]{1,0:T(8,128)(2,1)}, u32[]{:S(2)}) copy-start(bf16[128,2048]{1,0:T(8,128)(2,1)} %param.10) | copy-start | bytes 1572868
  97.3 34.0 %copy-start.1 = (f32[2048]{0:T(1024)S(1)}, f32[2048]{0:T(1024)}, u32[]{:S(2)}) copy-start(f32[2048]{0:T(1024)} %param.14) | copy-start | bytes 24580
  97.3 36.7 %copy-start.2 = (s32[128,8]{0,1:T(8,128)S(1)}, s32[128,8]{0,1:T(8,128)}, u32[]{:S(2)}) copy-start(s32[128,8]{0,1:T(8,128)} %param.15) | copy-start | bytes 12292
  97.3 36.9 %copy-start.3 = (f32[128,8]{0,1:T(8,128)S(1)}, f32[128,8]{0,1:T(8,128)}, u32[]{:S(2)}) copy-start(f32[128,8]{0,1:T(8,128)} %param.16) | copy-start | bytes 12292
  97.3 65.4 %all-gather.5.cloned.1.call-start = ((), (), s32[]{:S(2)}) async-start(), calls=%async_computation.5 | async-start | bytes 2359296 | tf_op jit(solution)/shard_map/all_gather | solution.py:217
  133.3 59.5 %all-gather.7.cloned.1.call-start = ((), (), s32[]{:S(2)}) async-start(), calls=%async_computation.6 | async-start | bytes 2359296 | tf_op jit(solution)/shard_map/all_gather | solution.py:217
  133.9 215.7 %reduce-scatter.6.cloned.1.call-start = ((), (), s32[]{:S(2)}) async-start(), calls=%async_computation.7 | async-start | bytes 2359296 | tf_op jit(solution)/shard_map/reduce_scatter | solution.py:238
  162.7 5.1 %copy-start.5 = (bf16[1024,1024]{1,0:T(8,128)(2,1)S(1)}, bf16[1024,1024]{1,0:T(8,128)(2,1)}, u32[]{:S(2)}) copy-start(bf16[1024,1024]{1,0:T(8,128)(2,1)} %all-gather.5.cloned.1.call-done) | copy-start | bytes 6291460
  166.3 34.4 %collective-permute-start = (bf16[384,1024]{1,0:T(8,128)(2,1)}, bf16[384,1024]{1,0:T(8,128)(2,1)S(1)}, u32[]{:S(2)}, u32[]{:S(2)}) collective-permute-start(bf16[384,1024]{1,0:T(8,128)(2,1)} %convolution_convert_fusion.7), channel_id=1, source_target_pairs={{0,8},{8,0},{16,24},{24,16},{1,9},{9,1},{17,25},{25,17},{2,10},{10... | collective-permute-start | bytes 2359304 | tf_op jit(solution)/shard_map/ppermute | solution.py:147
  169.7 37.6 %collective-permute-start.1 = (bf16[384,1024]{1,0:T(8,128)(2,1)}, bf16[384,1024]{1,0:T(8,128)(2,1)}, u32[]{:S(2)}, u32[]{:S(2)}) collective-permute-start(bf16[384,1024]{1,0:T(8,128)(2,1)} %convolution_convert_fusion.6), channel_id=1, source_target_pairs={{0,16},{8,24},{16,0},{24,8},{1,17},{9,25},{17,1},{25,9},{2,18},{10... | collective-permute-start | bytes 2359304 | tf_op jit(solution)/shard_map/ppermute | solution.py:147
  173.2 34.1 %collective-permute-start.2 = (bf16[384,1024]{1,0:T(8,128)(2,1)}, bf16[384,1024]{1,0:T(8,128)(2,1)}, u32[]{:S(2)}, u32[]{:S(2)}) collective-permute-start(bf16[384,1024]{1,0:T(8,128)(2,1)} %convolution_convert_fusion.5), channel_id=1, source_target_pairs={{0,24},{8,16},{16,8},{24,0},{1,25},{9,17},{17,9},{25,1},{2,26},{10... | collective-permute-start | bytes 2359304 | tf_op jit(solution)/shard_map/ppermute | solution.py:147
  192.9 4.3 %copy-start.7 = (bf16[1024,1024]{1,0:T(8,128)(2,1)S(1)}, bf16[1024,1024]{1,0:T(8,128)(2,1)}, u32[]{:S(2)}) copy-start(bf16[1024,1024]{1,0:T(8,128)(2,1)} %all-gather.7.cloned.1.call-done) | copy-start | bytes 6291460
  195.6 25.1 %collective-permute-start.3 = (bf16[384,1024]{1,0:T(8,128)(2,1)S(1)}, bf16[384,1024]{1,0:T(8,128)(2,1)S(1)}, u32[]{:S(2)}, u32[]{:S(2)}) collective-permute-start(bf16[384,1024]{1,0:T(8,128)(2,1)S(1)} %convolution_convert_fusion.3), channel_id=1, source_target_pairs={{0,8},{8,0},{16,24},{24,16},{1,9},{9,1},{17,25},{25,17},{2,10},{10... | collective-permute-start | bytes 2359304 | tf_op jit(solution)/shard_map/ppermute | solution.py:147
  198.1 3.2 copy-start.6
  198.2 41.7 %collective-permute-start.4 = (bf16[384,1024]{1,0:T(8,128)(2,1)S(1)}, bf16[384,1024]{1,0:T(8,128)(2,1)S(1)}, u32[]{:S(2)}, u32[]{:S(2)}) collective-permute-start(bf16[384,1024]{1,0:T(8,128)(2,1)S(1)} %convolution_convert_fusion.2), channel_id=1, source_target_pairs={{0,16},{8,24},{16,0},{24,8},{1,17},{9,25},{17,1},{25,9},{2,18},{10... | collective-permute-start | bytes 2359304 | tf_op jit(solution)/shard_map/ppermute | solution.py:147
  200.7 2.6 copy-start.8
  200.7 39.1 %collective-permute-start.5 = (bf16[384,1024]{1,0:T(8,128)(2,1)S(1)}, bf16[384,1024]{1,0:T(8,128)(2,1)S(1)}, u32[]{:S(2)}, u32[]{:S(2)}) collective-permute-start(bf16[384,1024]{1,0:T(8,128)(2,1)S(1)} %convolution_convert_fusion.1), channel_id=1, source_target_pairs={{0,24},{8,16},{16,8},{24,0},{1,25},{9,17},{17,9},{25,1},{2,26},{10... | collective-permute-start | bytes 2359304 | tf_op jit(solution)/shard_map/ppermute | solution.py:147
  220.7 19.2 %copy-start.9 = (bf16[384,1024]{1,0:T(8,128)(2,1)}, bf16[384,1024]{1,0:T(8,128)(2,1)S(1)}, u32[]{:S(2)}) copy-start(bf16[384,1024]{1,0:T(8,128)(2,1)S(1)} %collective-permute-done.3) | copy-start | bytes 2359300
  239.9 0.9 copy-start.10
  239.9 1.2 copy-start.11
  264.0 19.8 %collective-permute-start.7 = (bf16[4,96,1024]{2,1,0:T(8,128)(2,1)}, bf16[4,96,1024]{2,1,0:T(8,128)(2,1)S(1)}, u32[]{:S(2)}, u32[]{:S(2)}) collective-permute-start(bf16[4,96,1024]{2,1,0:T(8,128)(2,1)} %get-tuple-element.17), channel_id=1, source_target_pairs={{0,16},{8,24},{16,0},{24,8},{1,17},{9,25},{17,1},{25,9},{2,18},{10... | collective-permute-start | bytes 2359304 | tf_op jit(solution)/shard_map/ppermute | solution.py:147
  265.5 20.7 %collective-permute-start.6 = (bf16[4,96,1024]{2,1,0:T(8,128)(2,1)}, bf16[4,96,1024]{2,1,0:T(8,128)(2,1)S(1)}, u32[]{:S(2)}, u32[]{:S(2)}) collective-permute-start(bf16[4,96,1024]{2,1,0:T(8,128)(2,1)} %get-tuple-element.16), channel_id=1, source_target_pairs={{0,8},{8,0},{16,24},{24,16},{1,9},{9,1},{17,25},{25,17},{2,10},{10... | collective-permute-start | bytes 2359304 | tf_op jit(solution)/shard_map/ppermute | solution.py:147
  266.2 34.5 %collective-permute-start.8 = (bf16[4,96,1024]{2,1,0:T(8,128)(2,1)}, bf16[4,96,1024]{2,1,0:T(8,128)(2,1)S(1)}, u32[]{:S(2)}, u32[]{:S(2)}) collective-permute-start(bf16[4,96,1024]{2,1,0:T(8,128)(2,1)} %get-tuple-element.18), channel_id=1, source_target_pairs={{0,24},{8,16},{16,8},{24,0},{1,25},{9,17},{17,9},{25,1},{2,26},{10... | collective-permute-start | bytes 2359304 | tf_op jit(solution)/shard_map/ppermute | solution.py:147
  303.8 80.5 %reduce-scatter.8.cloned.1.call-start = ((), (), s32[]{:S(2)}) async-start(), calls=%async_computation.8 | async-start | bytes 2359296 | tf_op jit(solution)/shard_map/reduce_scatter | solution.py:238
  311.1 19.8 %collective-permute-start.10 = (bf16[4,96,1024]{2,1,0:T(8,128)(2,1)}, bf16[4,96,1024]{2,1,0:T(8,128)(2,1)S(1)}, u32[]{:S(2)}, u32[]{:S(2)}) collective-permute-start(bf16[4,96,1024]{2,1,0:T(8,128)(2,1)} %get-tuple-element.21), channel_id=1, source_target_pairs={{0,16},{8,24},{16,0},{24,8},{1,17},{9,25},{17,1},{25,9},{2,18},{10... | collective-permute-start | bytes 2359304 | tf_op jit(solution)/shard_map/ppermute | solution.py:147
  312.7 20.7 %collective-permute-start.9 = (bf16[4,96,1024]{2,1,0:T(8,128)(2,1)}, bf16[4,96,1024]{2,1,0:T(8,128)(2,1)S(1)}, u32[]{:S(2)}, u32[]{:S(2)}) collective-permute-start(bf16[4,96,1024]{2,1,0:T(8,128)(2,1)} %get-tuple-element.20), channel_id=1, source_target_pairs={{0,8},{8,0},{16,24},{24,16},{1,9},{9,1},{17,25},{25,17},{2,10},{10... | collective-permute-start | bytes 2359304 | tf_op jit(solution)/shard_map/ppermute | solution.py:147
  313.1 33.5 %collective-permute-start.11 = (bf16[4,96,1024]{2,1,0:T(8,128)(2,1)}, bf16[4,96,1024]{2,1,0:T(8,128)(2,1)S(1)}, u32[]{:S(2)}, u32[]{:S(2)}) collective-permute-start(bf16[4,96,1024]{2,1,0:T(8,128)(2,1)} %get-tuple-element.22), channel_id=1, source_target_pairs={{0,24},{8,16},{16,8},{24,0},{1,25},{9,17},{17,9},{25,1},{2,26},{10... | collective-permute-start | bytes 2359304 | tf_op jit(solution)/shard_map/ppermute | solution.py:147
Sparse Core Ops, SparseCore 0:
  9.0 49.8 all-gather.8
  97.4 32.4 reduce-scatter.3
  133.5 29.1 all-gather.4
  164.2 28.6 all-gather.6
  303.9 34.4 reduce-scatter.5
  349.7 34.4 reduce-scatter.7

commit v2 on v1

v2 whole, which is shorter than its diff:
```python
import functools
import math

import jax
import jax.numpy as jnp
from jax import lax
from jax.experimental import pallas as pl
from jax.experimental.pallas import tpu as pltpu
from jax.sharding import PartitionSpec as P

H = 32
KV_HEADS = 4
HEAD_DIM = 128
EXPERTS = 128
TOPK = 8
CAP = 12

CHUNKS = 4
VMEM_LIMIT = 48 * 1024 * 1024
VMEM_MOST = 60 * 1024 * 1024


def call(kernel, deps, operands, in_specs, vmem=VMEM_LIMIT, **kwargs):
    count = len(operands)

    def run(*refs):
        kernel(*refs[:count], *refs[count + len(deps) :])

    in_specs = in_specs + [pl.BlockSpec(memory_space=pl.ANY)] * len(deps)
    params = pltpu.CompilerParams(vmem_limit_bytes=vmem)
    if "grid_spec" in kwargs:
        kwargs["grid_spec"] = kwargs["grid_spec"](in_specs)
        in_specs = None
    else:
        kwargs["in_specs"] = in_specs
    return pl.pallas_call(run, compiler_params=params, **kwargs)(*operands, *deps)


def attention_kernel(where_ref, q_ref, *refs, blocks, stack, old):
    k_refs, v_refs = refs[: blocks + 1], refs[blocks + 1 : 2 * blocks + 2]
    o_ref, key_ref, value_ref = refs[2 * blocks + 2 :]
    rows, wide = q_ref.shape
    half = k_refs[1].shape[0]
    keys = key_ref.shape[0]
    factor = math.log2(math.e) / math.sqrt(HEAD_DIM)
    for b in range(blocks):
        lead = slice(2 * b * half, (2 * b + 1) * half)
        part = slice(b * half, (b + 1) * half)
        key_ref[lead, :] = k_refs[0][part, :]
        value_ref[lead, :HEAD_DIM] = v_refs[0][part, :]
        at = pl.ds(pl.multiple_of((2 * where_ref[3 + b] + 1) * half, half), half)
        key_ref[at, :] = k_refs[1 + b][...]
        value_ref[at, :HEAD_DIM] = v_refs[1 + b][...]
    value_ref[:, HEAD_DIM:] = jnp.ones((keys, HEAD_DIM), value_ref.dtype)
    late = (stack * rows, keys - old)
    row = lax.broadcasted_iota(jnp.int32, late, 0) % rows
    allowed = lax.broadcasted_iota(jnp.int32, late, 1) + old <= row + where_ref[2]
    for first in range(0, wide // HEAD_DIM, stack):
        query = jnp.concatenate(
            [q_ref[:, h * HEAD_DIM : (h + 1) * HEAD_DIM] for h in range(first, first + stack)],
            axis=0,
        )
        scores = lax.dot_general(
            query, key_ref[...], (((1,), (1,)), ((), ())), preferred_element_type=jnp.float32
        )
        scores = jnp.concatenate(
            [scores[:, :old], jnp.where(allowed, scores[:, old:], -1e30)], axis=1
        )
        top = jnp.max(scores, axis=1, keepdims=True)
        weights = jnp.exp2((scores - top) * factor).astype(jnp.bfloat16)
        summed = jnp.dot(weights, value_ref[...], preferred_element_type=jnp.float32)
        out = (summed[:, :HEAD_DIM] / summed[:, HEAD_DIM:]).astype(o_ref.dtype)
        for i in range(stack):
            h = first + i
            o_ref[:, h * HEAD_DIM : (h + 1) * HEAD_DIM] = out[i * rows : (i + 1) * rows]


def attention(queries, kv_lead, kv_blocks, where, old, peers, deps):
    rows = queries.shape[0]
    wide = queries.shape[1] // peers
    blocks = len(kv_blocks)
    half = kv_blocks[0].shape[0]
    keys = 2 * half * blocks

    def column(size, first):
        return pl.BlockSpec((size, HEAD_DIM), lambda i, where: (0, first + where[1]))

    sizes = [half * blocks] + [half] * blocks
    return call(
        functools.partial(attention_kernel, blocks=blocks, stack=2, old=old),
        deps,
        [where, queries] + [kv_lead, *kv_blocks] * 2,
        [pl.BlockSpec((rows, wide), lambda i, where: (0, where[0]))]
        + [column(size, 0) for size in sizes]
        + [column(size, KV_HEADS) for size in sizes],
        grid_spec=lambda in_specs: pltpu.PrefetchScalarGridSpec(
            num_scalar_prefetch=1,
            grid=(1,),
            in_specs=in_specs,
            out_specs=pl.BlockSpec((rows, wide), lambda i, where: (0, 0)),
            scratch_shapes=[
                pltpu.VMEM((keys, HEAD_DIM), jnp.bfloat16),
                pltpu.VMEM((keys, 2 * HEAD_DIM), jnp.bfloat16),
            ],
        ),
        out_shape=jax.ShapeDtypeStruct((rows, wide), jnp.bfloat16),
        cost_estimate=pl.CostEstimate(
            flops=4 * rows * wide * keys,
            bytes_accessed=4 * (keys * HEAD_DIM + rows * wide),
            transcendentals=rows * wide // HEAD_DIM * keys,
        ),
        name="attention",
        vmem=VMEM_MOST,
    )


def pick_kernel(order_ref, pick_ref, *refs, blocks):
    if blocks > 1:
        block_refs, outs, scratch = refs[:blocks], refs[blocks:-1], refs[-1]
        span = block_refs[0].shape[0]
        number = 0
        for ref in block_refs:
            for part in range(ref.shape[0] // span):
                at = pl.ds(pl.multiple_of(order_ref[number] * span, span), span)
                scratch[at, :] = ref[part * span : (part + 1) * span, :]
                number += 1
        block = scratch[...]
    else:
        block, outs = refs[0][...], refs[1:]
    count = outs[0].shape[0]
    for k, out in enumerate(outs):
        out[...] = jnp.dot(
            pick_ref[k * count : (k + 1) * count, :], block, preferred_element_type=jnp.float32
        ).astype(out.dtype)


def pick_rows(order, pick, blocks, peers, chunk=0, chunks=1):
    count, width = pick.shape[0] // peers, blocks[0].shape[1] // chunks

    def whole(shape):
        return pl.BlockSpec(shape, lambda i: (0, 0))

    return call(
        functools.partial(pick_kernel, blocks=len(blocks)),
        [],
        [order, pick, *blocks],
        [pl.BlockSpec(memory_space=pltpu.SMEM), whole(pick.shape)]
        + [pl.BlockSpec((b.shape[0], width), lambda i: (0, chunk)) for b in blocks],
        grid=(1,),
        out_specs=[whole((count, width))] * peers,
        out_shape=[jax.ShapeDtypeStruct((count, width), jnp.bfloat16)] * peers,
        scratch_shapes=[pltpu.VMEM((pick.shape[1], width), jnp.bfloat16)] * (len(blocks) > 1),
        cost_estimate=pl.CostEstimate(
            flops=2 * pick.size * width,
            bytes_accessed=2 * (pick.size + (pick.shape[0] + pick.shape[1]) * width),
            transcendentals=0,
        ),
        name="pick_rows",
    )


def hidden_kernel(*refs, peers, carried, last):
    x_refs, refs = refs[:peers], refs[peers:]
    gate_ref, up_ref, *refs = refs
    part = jnp.concatenate([x[...] for x in x_refs], axis=0)
    gate = jnp.dot(part, gate_ref[0], preferred_element_type=jnp.float32)
    up = jnp.dot(part, up_ref[0], preferred_element_type=jnp.float32)
    if carried:
        gate = gate + refs[0][0]
        up = up + refs[1][0]
        refs = refs[2:]
    if last:
        refs[0][0] = (gate / (1.0 + jnp.exp(-gate)) * up).astype(refs[0].dtype)
    else:
        refs[0][0] = gate
        refs[1][0] = up


def expert_hidden(part, first, w_gate, w_up, carry, last, deps=()):
    peers = len(part)
    width = part[0].shape[1]
    local, _, inner = w_gate.shape
    slots = part[0].shape[0] // local
    rows = peers * slots
    assert first % width == 0
    weight_spec = pl.BlockSpec((1, width, inner), lambda j: (j, first // width, 0))
    sum_spec = pl.BlockSpec((1, rows, inner), lambda j: (j, 0, 0))
    total = jax.ShapeDtypeStruct((local, rows, inner), jnp.float32)
    return call(
        functools.partial(hidden_kernel, peers=peers, carried=carry is not None, last=last),
        deps,
        [*part, w_gate, w_up, *(carry or ())],
        [pl.BlockSpec((slots, width), lambda j: (j, 0))] * peers
        + [weight_spec] * 2
        + ([] if carry is None else [sum_spec] * 2),
        grid=(local,),
        out_specs=sum_spec if last else [sum_spec] * 2,
        out_shape=jax.ShapeDtypeStruct(total.shape, jnp.bfloat16) if last else [total] * 2,
        cost_estimate=pl.CostEstimate(
            flops=4 * local * rows * width * inner,
            bytes_accessed=4 * local * width * inner + 10 * local * rows * inner,
            transcendentals=local * rows * inner,
        ),
        name="expert_hidden",
    )


def down_kernel(h_ref, w_ref, *y_refs):
    slots = y_refs[0].shape[0]
    out = jnp.dot(h_ref[0], w_ref[0], preferred_element_type=jnp.float32).astype(jnp.bfloat16)
    for k, y_ref in enumerate(y_refs):
        y_ref[...] = out[k * slots : (k + 1) * slots]


def expert_down(hidden, w_down, chunk, chunks, peers):
    local, rows, inner = hidden.shape
    width = w_down.shape[2] // chunks
    slots = rows // peers
    return pl.pallas_call(
        down_kernel,
        grid=(local,),
        in_specs=[
            pl.BlockSpec((1, rows, inner), lambda j: (j, 0, 0)),
            pl.BlockSpec((1, inner, width), lambda j: (j, 0, chunk)),
        ],
        out_specs=[pl.BlockSpec((slots, width), lambda j: (j, 0))] * peers,
        out_shape=[jax.ShapeDtypeStruct((local * slots, width), jnp.bfloat16)] * peers,
        compiler_params=pltpu.CompilerParams(vmem_limit_bytes=VMEM_LIMIT),
        cost_estimate=pl.CostEstimate(
            flops=2 * local * rows * width * inner,
            bytes_accessed=2 * local * (inner * width + rows * (inner + width)),
            transcendentals=0,
        ),
        name="expert_down",
    )(hidden, w_down)


def mix_kernel(order_ref, mix_ref, *refs, first, count):
    rows = jnp.concatenate([r[...] for r in refs[:-1]], axis=0)
    if count:
        span = refs[-1].shape[0] // count
        mix = jnp.concatenate(
            [
                mix_ref[pl.ds(pl.multiple_of(order_ref[first + i] * span, span), span), :]
                for i in range(count)
            ],
            axis=0,
        )
    else:
        mix = mix_ref[...]
    out = jnp.dot(mix, rows, preferred_element_type=jnp.float32)
    refs[-1][...] = out.astype(refs[-1].dtype)


def mix_rows(order, mix, parts, dtype, first=0, count=0, deps=()):
    rows = mix.shape[0] * (count or len(order)) // len(order)
    width = parts[0].shape[1]
    vmem = pl.BlockSpec(memory_space=pltpu.VMEM)
    return call(
        functools.partial(mix_kernel, first=first, count=count),
        deps,
        [order, mix, *parts],
        [pl.BlockSpec(memory_space=pltpu.SMEM)] + [vmem] * (1 + len(parts)),
        out_specs=vmem,
        out_shape=jax.ShapeDtypeStruct((rows, width), dtype),
        cost_estimate=pl.CostEstimate(
            flops=2 * rows * mix.shape[1] * width,
            bytes_accessed=2 * (mix.size + (mix.shape[0] + mix.shape[1]) * width),
            transcendentals=0,
        ),
        name="mix_rows",
    )


def table_kernel(order_ref, place_ref, gate_ref, pick_ref, mix_ref, *, slots):
    group, local, column = place_ref.shape
    blocks = order_ref.shape[0]
    span = column // blocks
    slot = lax.broadcasted_iota(jnp.int32, (slots, span), 0)
    for b in range(blocks):
        here = slice(b * span, (b + 1) * span)
        hits, gates = [], []
        for g in range(group):
            for j in range(local):
                hit = place_ref[g, j : j + 1, here] == slot
                hits.append(jnp.where(hit, 1.0, 0.0))
                gates.append(jnp.where(hit, gate_ref[g, j : j + 1, here], 0.0))
        at = pl.ds(pl.multiple_of(order_ref[b] * span, span), span)
        pick_ref[:, at] = jnp.concatenate(hits, axis=0).astype(pick_ref.dtype)
        mix_ref[at, :] = jnp.concatenate(gates, axis=0).T.astype(mix_ref.dtype)


def tables(order, place, gate, slots):
    peers, local, column = place.shape
    rows = local * slots
    group = next(g for g in range(1, peers + 1) if g == peers or not (peers % g or g * rows % 128))
    return pl.pallas_call(
        functools.partial(table_kernel, slots=slots),
        grid=(peers // group,),
        in_specs=[pl.BlockSpec(memory_space=pltpu.SMEM)]
        + [pl.BlockSpec((group, local, column), lambda k: (k, 0, 0))] * 2,
        out_specs=[
            pl.BlockSpec((group * rows, column), lambda k: (k, 0)),
            pl.BlockSpec((column, group * rows), lambda k: (0, k)),
        ],
        out_shape=[
            jax.ShapeDtypeStruct((peers * rows, column), jnp.bfloat16),
            jax.ShapeDtypeStruct((column, peers * rows), jnp.bfloat16),
        ],
        compiler_params=pltpu.CompilerParams(vmem_limit_bytes=VMEM_LIMIT),
        cost_estimate=pl.CostEstimate(
            flops=4 * peers * rows * column,
            bytes_accessed=4 * peers * rows * column,
            transcendentals=0,
        ),
        name="tables",
    )(order, place, gate)


def hold_kernel(x_ref, o_ref):
    o_ref[...] = x_ref[...]


def hold(value, deps):
    vmem = pl.BlockSpec(memory_space=pltpu.VMEM)
    return call(
        hold_kernel,
        deps,
        [value],
        [vmem],
        out_specs=vmem,
        out_shape=jax.ShapeDtypeStruct(value.shape, value.dtype),
        name="hold",
    )


def exchange(value, axis, k):
    if k == 0:
        return value
    return lax.ppermute(value, axis, [(i, i ^ k) for i in range(lax.axis_size(axis))])


def per_device(
    tokens,
    queries,
    keys_values,
    out_weight,
    moe_gain,
    expert_ids,
    gates,
    w_gate_experts,
    w_up_experts,
    w_down_experts,
):
    tok_count, width = tokens.shape
    ctx_count = lax.axis_size("ctx")
    peers = lax.axis_size("grp")
    chips = ctx_count // 2
    here, me = lax.axis_index("ctx"), lax.axis_index("grp")
    local = w_gate_experts.shape[0]
    slots = ctx_count * CAP
    column = ctx_count * tok_count
    turn = [k for k in reversed(range(peers))]

    order = here ^ jnp.concatenate(
        [2 * jnp.arange(chips, dtype=jnp.int32) + core for core in range(2)]
    )

    half = keys_values.shape[1] // 2
    kv_same = [exchange(keys_values[0, half:], "ctx", 2 * s) for s in reversed(range(chips))][::-1]
    kv_lead = lax.all_gather(keys_values[0, :half], "ctx", axis=0, tiled=True)
    kv_blocks = kv_same + [exchange(b, "ctx", 1) for b in kv_same]

    def route(attended):
        routes = jnp.concatenate([expert_ids.astype(jnp.float32), gates], axis=1).T
        routes = hold(routes, [attended])
        pair = jnp.concatenate([routes, exchange(routes, "ctx", 1)], axis=1)
        pairs = [exchange(pair, "ctx", 2 * s) for s in range(chips)]
        routes = jnp.concatenate(
            [p[:, :tok_count] for p in pairs] + [p[:, tok_count:] for p in pairs], axis=1
        )
        ids, gate_rows = routes[:TOPK].astype(jnp.int32), routes[TOPK:]
        owner = me ^ jnp.arange(peers, dtype=jnp.int32)
        wanted = (
            ((owner * ctx_count + here) * local)[:, None] + jnp.arange(local, dtype=jnp.int32)[None, :]
        ).reshape(-1)
        same = ids[None, :, :] == wanted[:, None, None]
        named = jnp.any(same, axis=1)
        gate_of = jnp.sum(jnp.where(same, gate_rows[None], 0.0), axis=1)
        earlier = jnp.triu(jnp.ones((tok_count, tok_count), jnp.bfloat16), 1)
        rank = jnp.dot(
            named.reshape(-1, tok_count).astype(jnp.bfloat16),
            earlier,
            preferred_element_type=jnp.float32,
        ).astype(jnp.int32)
        place = rank.reshape(-1, column) + jnp.repeat(order * CAP, tok_count)
        place = jnp.where(named, place, -1)
        pick, mix = tables(
            order, place.reshape(peers, local, column), gate_of.reshape(peers, local, column), slots
        )
        return pick, mix

    old = keys_values.shape[1] * ctx_count - column
    heads = H // peers
    sums, sent, deps = {}, {}, []
    for k in turn:
        peer = me ^ k
        where = jnp.concatenate(
            [
                jnp.stack([peer, peer * heads // (H // KV_HEADS), old + here * tok_count]).astype(
                    jnp.int32
                ),
                order,
            ]
        )
        if k == turn[0]:
            attended = attention(queries, kv_lead, kv_blocks, where, old, peers, deps)
            pick, mix = route(attended)
        if k == 0:
            for j in turn[:-1]:
                part = jnp.dot(sent[j], out_weight, preferred_element_type=jnp.float32)
                deps.append(part.astype(jnp.bfloat16))
                sums[j] = exchange(deps[-1], "grp", j)
            deps += [pick, mix]
        if k != turn[0]:
            attended = attention(queries, kv_lead, kv_blocks, where, old, peers, deps)
        sent[k] = exchange(attended, "grp", k)
    sums[0] = jnp.dot(sent[0], out_weight, preferred_element_type=jnp.float32)
    projected = sum(sums[k].astype(jnp.float32) for k in range(peers))
    residual = (tokens.astype(jnp.float32) + projected).astype(jnp.bfloat16)
    wide = residual.astype(jnp.float32)
    normed = (
        wide * lax.rsqrt(jnp.mean(wide * wide, axis=1, keepdims=True) + 1e-06) * moe_gain
    ).astype(jnp.bfloat16)

    span = width // CHUNKS
    same = [exchange(normed[:, :span], "ctx", 2 * s) for s in range(chips)]
    blocks = same + [exchange(jnp.concatenate(same, axis=0), "ctx", 1)]
    rest = lax.all_gather(normed[:, span:], "ctx", axis=0, tiled=True)
    rows = pick_rows(order, pick, blocks, peers)
    parts = []
    for c in range(CHUNKS):
        if c:
            rows = pick_rows(order, pick, [rest], peers, c - 1, CHUNKS - 1)
        sent = {k: exchange(rows[k], "grp", k) for k in turn}
        parts.append([sent[k] for k in range(peers)])
    carry, deps = None, [rows[0]]
    for c in range(CHUNKS):
        last = c == CHUNKS - 1
        carry = expert_hidden(
            parts[c], c * span, w_gate_experts, w_up_experts, carry, last, [] if last else deps
        )
    hidden = carry

    ready = [expert_down(hidden, w_down_experts, c, CHUNKS, peers) for c in range(CHUNKS)]
    early = CHUNKS // 2
    outs, totals = [], []
    for c in range(CHUNKS):
        sent = {k: exchange(ready[c][k], "grp", k) for k in turn}
        back = [sent[k] for k in range(peers)]
        if c < early:
            deps = [r[0] for r in ready[c + 1 :]]
            totals.append(mix_rows(order, mix, back, jnp.bfloat16, deps=deps))
            if c < early - 1:
                continue
            total = jnp.concatenate(totals, axis=1)
            total = lax.psum_scatter(total, "ctx", scatter_dimension=0, tiled=True)
            total = wide[:, : early * span] + total.astype(jnp.float32)
        else:
            other = mix_rows(order, mix, back, jnp.bfloat16, chips, chips, outs[1:])
            other = exchange(other, "ctx", 1)
            both = mix_rows(order, mix, back, jnp.float32, 0, chips) + other.astype(jnp.float32)
            total = wide[:, c * span : (c + 1) * span] + both[:tok_count]
            for s in range(1, chips):
                piece = both[s * tok_count : (s + 1) * tok_count].astype(jnp.bfloat16)
                total = total + exchange(piece, "ctx", 2 * s).astype(jnp.float32)
        outs.append(total.astype(jnp.bfloat16))
    return jnp.concatenate(outs, axis=1)


def solution(mesh):
    return jax.shard_map(
        per_device,
        mesh=mesh,
        in_specs=(
            P(("grp", "ctx"), None),
            P(("grp", "ctx"), None),
            P("grp", "ctx", None),
            P("grp", None),
            P(),
            P(("grp", "ctx"), None),
            P(("grp", "ctx"), None),
            P(("grp", "ctx"), None, None),
            P(("grp", "ctx"), None, None),
            P(("grp", "ctx"), None, None),
        ),
        out_specs=P(("grp", "ctx"), None),
        check_vma=False,
    )
```

time: 394 us -> 349 us (0.89)
  waiting for transfers between devices: 241 us -> 143 us
  Pallas kernels: 45.2 us -> 105 us
  starting transfers between devices: 14.4 us -> 56.3 us
  blocking collectives: 32.3 us -> 0 us
  matrix products: 35.9 us -> 11.1 us
  local copies, waits for them, and re-layouts: 4.75 us -> 11.4 us
    all_gather x3 -> x2, waiting for transfers between devices: 82.7 us -> 7.18 us  [the longest x1 7.17 us: per_device(): rest = lax.all_gather(normed[:, span:], 'ctx', axis=0, tiled=True)]
    reduce_scatter x3 -> x1, waiting for transfers between devices: 67.2 us -> 0.02 us  [per_device(): total = lax.psum_scatter(total, 'ctx', scatter_dimension=0, tiled=True)]
    pallas_call x2 -> x20, Pallas kernels: 31.1 us -> 90.1 us  [the longest x19 86.2 us: call(): pl.pallas_call(run, compiler_params=params, **kwargs)(*operands, *deps)]
    ppermute x12 -> x53, waiting for transfers between devices: 89.7 us -> 136 us  [exchange(): lax.ppermute(value, axis, [(i, i ^ k) for i in range(lax.axis_size(axis))])]
    ppermute x12 -> x53, starting transfers between devices: 14.2 us -> 56.2 us  [exchange(): lax.ppermute(value, axis, [(i, i ^ k) for i in range(lax.axis_size(axis))])]
    dot_general x18 -> x5, matrix products: 35.9 us -> 11.1 us  [the longest x3 6.99 us: per_device(): part = jnp.dot(sent[j], out_weight, preferred_element_type=jnp.float32)]
    all_to_all x1 -> x0, blocking collectives: 18.1 us -> none  [per_device(): lax.all_to_all(attended, 'grp', split_axis=1, concat_axis=0, tiled=True)]
    all_gather x1 -> x0, blocking collectives: 14.2 us -> none  [per_device(): routes = lax.all_gather(packed, 'ctx', axis=0, tiled=True).T]
  transfers between devices with their start and end apart: 18 -> 56, of which waited for: 14 -> 28; matrix products, arithmetic and copies ran while one was open for 8% -> 4% of each run, Pallas kernels for 2% -> 24%
where the time goes in v2:
time: 349 us; the launch traced here: 348 us
  waiting for transfers between devices  143 us (41%)
  Pallas kernels  105 us (30%)
  starting transfers between devices  56.3 us (16%)
  between operations  13.8 us (4%)
  local copies, waits for them, and re-layouts  11.4 us (3%)
  matrix products  11.1 us (3%)
  other arithmetic  7.67 us (2%)
    ppermute x53, waiting for transfers between devices, exchange(): lax.ppermute(value, axis, [(i, i ^ k) for i in range(lax.axis_size(axis))])  136 us
    pallas_call x19, Pallas kernels, call(): pl.pallas_call(run, compiler_params=params, **kwargs)(*operands, *deps)  86.2 us
    ppermute x53, starting transfers between devices, exchange(): lax.ppermute(value, axis, [(i, i ^ k) for i in range(lax.axis_size(axis))])  56.2 us
    pallas_call x4, Pallas kernels, expert_down(): pl.pallas_call(down_kernel, grid=(local,), in_specs=[pl.BlockSpec((1, row...  15.1 us
    unnamed x67, local copies, waits for them, and re-layouts  7.43 us
    all_gather x1, waiting for transfers between devices, per_device(): rest = lax.all_gather(normed[:, span:], 'ctx', axis=0, tiled=True)  7.17 us
    dot_general x3, matrix products, per_device(): part = jnp.dot(sent[j], out_weight, preferred_element_type=jnp.float32)  6.99 us
  transfers between devices with their start and end apart: 56, of which 28 were waited for; matrix products, arithmetic and copies ran while one was open for 4% of the time, Pallas kernels for 24%

profile of v2, /device:TPU:0, one launch (start us, length us, event | category | flops | bytes accessed | tf_op | source)
XLA Modules:
  0.0 348.2 jit_solution(18405015299460665896)
XLA Ops:
  8.9 4.7 %collective-permute-start.2 = (bf16[128,1024]{1,0:T(8,128)(2,1)S(1)}, bf16[128,1024]{1,0:T(8,128)(2,1)S(1)}, u32[]{:S(2)}, u32[]{:S(2)}) collective-permute-start(bf16[128,1024]{1,0:T(8,128)(2,1)S(1)} %get-tuple-element.97.refs_3_.refs_12_), channel_id=1, source_target_pairs={{0,6},{1,7},{2,4},{3,5},{4,2},{5,3},{6,0},{7,1},{8,14},{9,15},{10,... | collective-permute-start | bytes 786440 | tf_op jit(solution)/shard_map/ppermute | solution.py:340
  16.4 4.4 %collective-permute-done.2.refs_6_.refs_15_ = bf16[128,1024]{1,0:T(8,128)(2,1)S(1)} collective-permute-done((bf16[128,1024]{1,0:T(8,128)(2,1)S(1)}, bf16[128,1024]{1,0:T(8,128)(2,1)S(1)}, u32[]{:S(2)}, u32[]{:S(2)}) %collective-permute-start.2) | collective-permute-done | bytes 262176 | tf_op jit(solution)/shard_map/ppermute | solution.py:340
  20.9 32.5 %collective-permute-done.1.refs_5_.refs_14_ = bf16[128,1024]{1,0:T(8,128)(2,1)S(1)} collective-permute-done((bf16[128,1024]{1,0:T(8,128)(2,1)S(1)}, bf16[128,1024]{1,0:T(8,128)(2,1)S(1)}, u32[]{:S(2)}, u32[]{:S(2)}) %collective-permute-start.1) | collective-permute-done | bytes 262176 | tf_op jit(solution)/shard_map/ppermute | solution.py:340
  56.0 6.1 %attention.4.refs_1_ = bf16[128,1024]{1,0:T(8,128)(2,1)} custom-call(s32[11]{0:T(128)} %get-tuple-element.103.refs_0_, bf16[128,4096]{1,0:T(8,128)(2,1)} %refs_1_.7, bf16[1024,1024]{1,0:T(8,128)(2,1)} %bitcast.25, bf16[128,1024]{1,0:T(8,128)(2,1)} %copy-done.17, bf16[128,1024]{1,0:T(8,128)(2,1)} %copy-done.21, bf16[128,1024]{1,0:T(8,128)(2,1)} %copy-done.20, ...), custom_call_target="tpu_custom_call" | custom-call | flops 1073741824 | bytes 1572864 | tf_op jit(solution)/shard_map/attention/pallas_call | solution.py:36
  64.7 6.1 %attention.5 = bf16[128,1024]{1,0:T(8,128)(2,1)} custom-call(s32[11]{0:T(128)} %get-tuple-element.102.refs_0_, bf16[128,4096]{1,0:T(8,128)(2,1)} %refs_1_.7, bf16[1024,1024]{1,0:T(8,128)(2,1)} %bitcast.27, bf16[128,1024]{1,0:T(8,128)(2,1)} %copy-done.17, bf16[128,1024]{1,0:T(8,128)(2,1)} %copy-done.21, bf16[128,1024]{1,0:T(8,128)(2,1)} %copy-done.20, ...), custom_call_target="tpu_custom_call" | custom-call | flops 1073741824 | bytes 1572864 | tf_op jit(solution)/shard_map/attention/pallas_call | solution.py:36
  71.4 6.1 %attention.6 = bf16[128,1024]{1,0:T(8,128)(2,1)} custom-call(s32[11]{0:T(128)} %get-tuple-element.101.refs_0_, bf16[128,4096]{1,0:T(8,128)(2,1)} %refs_1_.7, bf16[1024,1024]{1,0:T(8,128)(2,1)} %bitcast.29, bf16[128,1024]{1,0:T(8,128)(2,1)} %copy-done.17, bf16[128,1024]{1,0:T(8,128)(2,1)} %copy-done.21, bf16[128,1024]{1,0:T(8,128)(2,1)} %copy-done.20, ...), custom_call_target="tpu_custom_call" | custom-call | flops 1073741824 | bytes 1572864 | tf_op jit(solution)/shard_map/attention/pallas_call | solution.py:36
  85.7 3.9 %convolution_convert_fusion.2.refs_20_ = bf16[128,2048]{1,0:T(8,128)(2,1)} fusion(bf16[128,1024]{1,0:T(8,128)(2,1)S(1)} %collective-permute-done.7, bf16[1024,2048]{1,0:T(8,128)(2,1)} %param.13), kind=kOutput, calls=%fused_computation.8 | convolution fusion | flops 537133056 | bytes 4980736 | tf_op jit(solution)/shard_map/dot_general | solution.py:421
  96.7 3.9 %tables.1 = (bf16[1536,1024]{1,0:T(8,128)(2,1)S(1)}, bf16[1024,1536]{1,0:T(8,128)(2,1)}) custom-call(s32[8]{0:T(128)S(1)} %get-tuple-element.90.order_ref.refs_0_, s32[4,4,1024]{2,1,0:T(4,128)S(1)} %add_select_fusion.place_ref, f32[4,4,1024]{2,1,0:T(4,128)S(1)} %reshape.52.gate_ref), custom_call_target="tpu_custom_call" | custom-call | flops 6291456 | bytes 6291456 | tf_op jit(solution)/shard_map/tables/pallas_call | solution.py:297
  102.3 6.3 %attention.7 = bf16[128,1024]{1,0:T(8,128)(2,1)} custom-call(s32[11]{0:T(128)} %add_add_fusion.refs_0_, bf16[128,4096]{1,0:T(8,128)(2,1)} %refs_1_.7, bf16[1024,1024]{1,0:T(8,128)(2,1)} %bitcast.31, bf16[128,1024]{1,0:T(8,128)(2,1)} %copy-done.17, bf16[128,1024]{1,0:T(8,128)(2,1)} %copy-done.21, bf16[128,1024]{1,0:T(8,128)(2,1)} %copy-done.20, ...), custom_call_target="tpu_custom_call" | custom-call | flops 1073741824 | bytes 1572864 | tf_op jit(solution)/shard_map/attention/pallas_call | solution.py:36
  108.6 5.8 %collective-permute-done.14 = bf16[128,2048]{1,0:T(8,128)(2,1)} collective-permute-done((bf16[128,2048]{1,0:T(8,128)(2,1)}, bf16[128,2048]{1,0:T(8,128)(2,1)}, u32[]{:S(2)}, u32[]{:S(2)}) %collective-permute-start.14) | collective-permute-done | bytes 524320 | tf_op jit(solution)/shard_map/ppermute | solution.py:340
  114.4 4.0 %multiply_reduce_fusion = (f32[128]{0:T(128)S(1)}, f32[128,2048]{1,0:T(8,128)S(1)}) fusion(bf16[128,2048]{1,0:T(8,128)(2,1)} %collective-permute-done.16, bf16[128,2048]{1,0:T(8,128)(2,1)} %collective-permute-done.15, bf16[128,2048]{1,0:T(8,128)(2,1)} %collective-permute-done.14, bf16[128,1024]{1,0:T(8,128)(2,1)} %attention.7, ...), kind=kOutput, calls=%fused_computation.14 | convolution fusion | flops 540016512 | bytes 7602688 | tf_op jit(solution)/shard_map/dot_general | solution.py:428
  126.5 3.9 %collective-permute-done.28.refs_5_ = bf16[128,512]{1,0:T(8,128)(2,1)S(1)} collective-permute-done((bf16[128,512]{1,0:T(8,128)(2,1)S(1)}, bf16[128,512]{1,0:T(8,128)(2,1)S(1)}, u32[]{:S(2)}, u32[]{:S(2)}) %collective-permute-start.28) | collective-permute-done | bytes 131104 | tf_op jit(solution)/shard_map/ppermute | solution.py:340
  130.4 16.7 %collective-permute-done.27.refs_4_ = bf16[128,512]{1,0:T(8,128)(2,1)S(1)} collective-permute-done((bf16[128,512]{1,0:T(8,128)(2,1)S(1)}, bf16[128,512]{1,0:T(8,128)(2,1)S(1)}, u32[]{:S(2)}, u32[]{:S(2)}) %collective-permute-start.27) | collective-permute-done | bytes 131104 | tf_op jit(solution)/shard_map/ppermute | solution.py:340
  155.8 7.2 %all-gather.4.cloned.1.call-done.refs_2_ = bf16[1024,1536]{1,0:T(8,128)(2,1)} async-done(((bf16[128,1536]{1,0:T(8,128)(2,1)}), bf16[1024,1536]{1,0:T(8,128)(2,1)}) %all-gather.4.cloned.1.call-update) | async-done | bytes 3145744 | tf_op jit(solution)/shard_map/all_gather | solution.py:439
  183.8 8.1 %expert_hidden.4 = (f32[4,384,768]{2,1,0:T(8,128)}, f32[4,384,768]{2,1,0:T(8,128)}) custom-call(bf16[384,512]{1,0:T(8,128)(2,1)S(1)} %get-tuple-element.59.refs_0_, bf16[384,512]{1,0:T(8,128)(2,1)} %collective-permute-done.30.refs_1_, bf16[384,512]{1,0:T(8,128)(2,1)} %collective-permute-done.31.refs_2_, bf16[384,512]{1,0:T(8,128)(2,1)} %collective-permute-done.32.refs_3_, ...), custom_call_target="tpu_custom_call" | custom-call | flops 2415919104 | bytes 18087936 | tf_op jit(solution)/shard_map/expert_hidden/pallas_call | solution.py:36
  193.1 5.2 %collective-permute-done.20.refs_1_ = bf16[384,512]{1,0:T(8,128)(2,1)S(1)} collective-permute-done((bf16[384,512]{1,0:T(8,128)(2,1)S(1)}, bf16[384,512]{1,0:T(8,128)(2,1)S(1)}, u32[]{:S(2)}, u32[]{:S(2)}) %collective-permute-start.20) | collective-permute-done | bytes 393248 | tf_op jit(solution)/shard_map/ppermute | solution.py:340
  200.7 9.8 %expert_hidden.5 = (f32[4,384,768]{2,1,0:T(8,128)}, f32[4,384,768]{2,1,0:T(8,128)}) custom-call(bf16[384,512]{1,0:T(8,128)(2,1)S(1)} %get-tuple-element.55.refs_0_, bf16[384,512]{1,0:T(8,128)(2,1)S(1)} %collective-permute-done.23.refs_1_, bf16[384,512]{1,0:T(8,128)(2,1)S(1)} %collective-permute-done.24.refs_2_, ...), custom_call_target="tpu_custom_call" | custom-call | flops 2415919104 | bytes 18087936 | tf_op jit(solution)/shard_map/expert_hidden/pallas_call | solution.py:36
  210.5 9.9 %expert_hidden.6 = (f32[4,384,768]{2,1,0:T(8,128)}, f32[4,384,768]{2,1,0:T(8,128)}) custom-call(bf16[384,512]{1,0:T(8,128)(2,1)S(1)} %get-tuple-element.51.refs_0_, bf16[384,512]{1,0:T(8,128)(2,1)S(1)} %collective-permute-done.20.refs_1_, bf16[384,512]{1,0:T(8,128)(2,1)S(1)} %collective-permute-done.21.refs_2_, ...), custom_call_target="tpu_custom_call" | custom-call | flops 2415919104 | bytes 18087936 | tf_op jit(solution)/shard_map/expert_hidden/pallas_call | solution.py:36
  223.9 7.3 %expert_hidden.7.h_ref = bf16[4,384,768]{2,1,0:T(8,128)(2,1)S(1)} custom-call(bf16[384,512]{1,0:T(8,128)(2,1)S(1)} %get-tuple-element.47.refs_6_.refs_8_.refs_0_, bf16[384,512]{1,0:T(8,128)(2,1)S(1)} %collective-permute-done.17.refs_1_, bf16[384,512]{1,0:T(8,128)(2,1)S(1)} %collective-permute-done.18.refs_2_, ...), custom_call_target="tpu_custom_call" | custom-call | flops 2415919104 | bytes 18087936 | tf_op jit(solution)/shard_map/expert_hidden/pallas_call | solution.py:36
  231.2 3.8 %expert_down.5 = (bf16[384,512]{1,0:T(8,128)(2,1)S(1)}, bf16[384,512]{1,0:T(8,128)(2,1)S(1)}, bf16[384,512]{1,0:T(8,128)(2,1)S(1)}, bf16[384,512]{1,0:T(8,128)(2,1)S(1)}) custom-call(bf16[4,384,768]{2,1,0:T(8,128)(2,1)S(1)} %expert_hidden.7.h_ref, bf16[4,768,2048]{2,1,0:T(8,128)(2,1)} %w_ref.7), custom_call_target="tpu_custom_call" | custom-call | flops 1207959552 | bytes 7077888 | tf_op jit(solution)/shard_map/expert_down/pallas_call | solution.py:219
  238.6 3.8 %expert_down.4 = (bf16[384,512]{1,0:T(8,128)(2,1)S(1)}, bf16[384,512]{1,0:T(8,128)(2,1)S(1)}, bf16[384,512]{1,0:T(8,128)(2,1)S(1)}, bf16[384,512]{1,0:T(8,128)(2,1)S(1)}) custom-call(bf16[4,384,768]{2,1,0:T(8,128)(2,1)S(1)} %expert_hidden.7.h_ref, bf16[4,768,2048]{2,1,0:T(8,128)(2,1)} %w_ref.7), custom_call_target="tpu_custom_call" | custom-call | flops 1207959552 | bytes 7077888 | tf_op jit(solution)/shard_map/expert_down/pallas_call | solution.py:219
  248.6 3.8 %expert_down.7 = (bf16[384,512]{1,0:T(8,128)(2,1)S(1)}, bf16[384,512]{1,0:T(8,128)(2,1)S(1)}, bf16[384,512]{1,0:T(8,128)(2,1)S(1)}, bf16[384,512]{1,0:T(8,128)(2,1)S(1)}) custom-call(bf16[4,384,768]{2,1,0:T(8,128)(2,1)S(1)} %expert_hidden.7.h_ref, bf16[4,768,2048]{2,1,0:T(8,128)(2,1)} %w_ref.7), custom_call_target="tpu_custom_call" | custom-call | flops 1207959552 | bytes 7077888 | tf_op jit(solution)/shard_map/expert_down/pallas_call | solution.py:219
  254.6 3.8 %expert_down.6 = (bf16[384,512]{1,0:T(8,128)(2,1)S(1)}, bf16[384,512]{1,0:T(8,128)(2,1)S(1)}, bf16[384,512]{1,0:T(8,128)(2,1)S(1)}, bf16[384,512]{1,0:T(8,128)(2,1)S(1)}) custom-call(bf16[4,384,768]{2,1,0:T(8,128)(2,1)S(1)} %expert_hidden.7.h_ref, bf16[4,768,2048]{2,1,0:T(8,128)(2,1)} %w_ref.7), custom_call_target="tpu_custom_call" | custom-call | flops 1207959552 | bytes 7077888 | tf_op jit(solution)/shard_map/expert_down/pallas_call | solution.py:219
  258.4 4.2 %mix_rows.7 = bf16[1024,512]{1,0:T(8,128)(2,1)S(1)} custom-call(s32[8]{0:T(128)S(1)} %get-tuple-element.90.order_ref.refs_0_, bf16[1024,1536]{1,0:T(8,128)(2,1)} %get-tuple-element.46.refs_24_.refs_1_, bf16[384,512]{1,0:T(8,128)(2,1)S(1)} %get-tuple-element.73.refs_6_.refs_2_, bf16[384,512]{1,0:T(8,128)(2,1)S(1)} %collective-permute-done.36.refs_3_, ...), custom_call_target="tpu_custom_call" | custom-call | flops 1610612736 | bytes 5767168 | tf_op jit(solution)/shard_map/mix_rows/pallas_call | solution.py:36
  264.0 7.6 %collective-permute-done.34.refs_4_ = bf16[384,512]{1,0:T(8,128)(2,1)S(1)} collective-permute-done((bf16[384,512]{1,0:T(8,128)(2,1)S(1)}, bf16[384,512]{1,0:T(8,128)(2,1)S(1)}, u32[]{:S(2)}, u32[]{:S(2)}) %collective-permute-start.34) | collective-permute-done | bytes 393248 | tf_op jit(solution)/shard_map/ppermute | solution.py:340
  280.6 8.8 %collective-permute-done.39.refs_3_ = bf16[384,512]{1,0:T(8,128)(2,1)S(1)} collective-permute-done((bf16[384,512]{1,0:T(8,128)(2,1)}, bf16[384,512]{1,0:T(8,128)(2,1)S(1)}, u32[]{:S(2)}, u32[]{:S(2)}) %collective-permute-start.39) | collective-permute-done | bytes 393248 | tf_op jit(solution)/shard_map/ppermute | solution.py:340
  289.4 5.9 %collective-permute-done.40.refs_4_ = bf16[384,512]{1,0:T(8,128)(2,1)S(1)} collective-permute-done((bf16[384,512]{1,0:T(8,128)(2,1)}, bf16[384,512]{1,0:T(8,128)(2,1)S(1)}, u32[]{:S(2)}, u32[]{:S(2)}) %collective-permute-start.40) | collective-permute-done | bytes 393248 | tf_op jit(solution)/shard_map/ppermute | solution.py:340
  304.9 3.8 %collective-permute-done.43 = bf16[128,512]{1,0:T(8,128)(2,1)S(1)} collective-permute-done((bf16[128,512]{1,0:T(8,128)(2,1)S(1)}, bf16[128,512]{1,0:T(8,128)(2,1)S(1)}, u32[]{:S(2)}, u32[]{:S(2)}) %collective-permute-start.43) | collective-permute-done | bytes 131104 | tf_op jit(solution)/shard_map/ppermute | solution.py:340
  308.8 4.7 %collective-permute-done.45 = bf16[128,512]{1,0:T(8,128)(2,1)S(1)} collective-permute-done((bf16[128,512]{1,0:T(8,128)(2,1)S(1)}, bf16[128,512]{1,0:T(8,128)(2,1)S(1)}, u32[]{:S(2)}, u32[]{:S(2)}) %collective-permute-start.45) | collective-permute-done | bytes 131104 | tf_op jit(solution)/shard_map/ppermute | solution.py:340
  313.6 6.2 %collective-permute-done.44 = bf16[128,512]{1,0:T(8,128)(2,1)S(1)} collective-permute-done((bf16[128,512]{1,0:T(8,128)(2,1)S(1)}, bf16[128,512]{1,0:T(8,128)(2,1)S(1)}, u32[]{:S(2)}, u32[]{:S(2)}) %collective-permute-start.44) | collective-permute-done | bytes 131104 | tf_op jit(solution)/shard_map/ppermute | solution.py:340
  330.0 4.6 %collective-permute-done.52 = bf16[128,512]{1,0:T(8,128)(2,1)S(1)} collective-permute-done((bf16[128,512]{1,0:T(8,128)(2,1)S(1)}, bf16[128,512]{1,0:T(8,128)(2,1)S(1)}, u32[]{:S(2)}, u32[]{:S(2)}) %collective-permute-start.52) | collective-permute-done | bytes 131104 | tf_op jit(solution)/shard_map/ppermute | solution.py:340
  334.6 5.0 %collective-permute-done.51 = bf16[128,512]{1,0:T(8,128)(2,1)S(1)} collective-permute-done((bf16[128,512]{1,0:T(8,128)(2,1)S(1)}, bf16[128,512]{1,0:T(8,128)(2,1)S(1)}, u32[]{:S(2)}, u32[]{:S(2)}) %collective-permute-start.51) | collective-permute-done | bytes 131104 | tf_op jit(solution)/shard_map/ppermute | solution.py:340
  (214 shorter events, 116.6 us)
Async XLA Ops:
  6.5 48.7 %all-gather.6.cloned.1.call-start = ((), (), s32[]{:S(2)}) async-start(), calls=%async_computation.3 | async-start | bytes 2359296 | tf_op jit(solution)/shard_map/all_gather | solution.py:371
  8.3 154.7 %all-gather.4.cloned.1.call-start = ((), (), s32[]{:S(2)}) async-start(), calls=%async_computation.1 | async-start | bytes 3538944 | tf_op jit(solution)/shard_map/all_gather | solution.py:439
  8.4 46.2 %collective-permute-start.3 = (bf16[128,1024]{1,0:T(8,128)(2,1)S(1)}, bf16[128,1024]{1,0:T(8,128)(2,1)S(1)}, u32[]{:S(2)}, u32[]{:S(2)}) collective-permute-start(bf16[128,1024]{1,0:T(8,128)(2,1)S(1)} %get-tuple-element.97.refs_3_.refs_12_), channel_id=1, source_target_pairs={{0,1},{1,0},{2,3},{3,2},{4,5},{5,4},{6,7},{7,6},{8,9},{9,8},{10,11... | collective-permute-start | bytes 786440 | tf_op jit(solution)/shard_map/ppermute | solution.py:340
  13.6 39.8 %collective-permute-start.1 = (bf16[128,1024]{1,0:T(8,128)(2,1)S(1)}, bf16[128,1024]{1,0:T(8,128)(2,1)S(1)}, u32[]{:S(2)}, u32[]{:S(2)}) collective-permute-start(bf16[128,1024]{1,0:T(8,128)(2,1)S(1)} %get-tuple-element.97.refs_3_.refs_12_), channel_id=1, source_target_pairs={{0,4},{1,5},{2,6},{3,7},{4,0},{5,1},{6,2},{7,3},{8,12},{9,13},{10,... | collective-permute-start | bytes 786440 | tf_op jit(solution)/shard_map/ppermute | solution.py:340
  13.6 39.8 %collective-permute-start = (bf16[128,1024]{1,0:T(8,128)(2,1)S(1)}, bf16[128,1024]{1,0:T(8,128)(2,1)S(1)}, u32[]{:S(2)}, u32[]{:S(2)}) collective-permute-start(bf16[128,1024]{1,0:T(8,128)(2,1)S(1)} %get-tuple-element.97.refs_3_.refs_12_), channel_id=1, source_target_pairs={{0,2},{1,3},{2,0},{3,1},{4,6},{5,7},{6,4},{7,5},{8,10},{9,11},{10,... | collective-permute-start | bytes 786440 | tf_op jit(solution)/shard_map/ppermute | solution.py:340
  20.9 33.7 %collective-permute-start.6 = (bf16[128,1024]{1,0:T(8,128)(2,1)S(1)}, bf16[128,1024]{1,0:T(8,128)(2,1)S(1)}, u32[]{:S(2)}, u32[]{:S(2)}) collective-permute-start(bf16[128,1024]{1,0:T(8,128)(2,1)S(1)} %collective-permute-done.2.refs_6_.refs_15_), channel_id=1, source_target_pairs={{0,1},{1,0},{2,3},{3,2},{4,5},{5,4},{6,7},{7,6},{8,9},{9,8},{10,11... | collective-permute-start | bytes 786440 | tf_op jit(solution)/shard_map/ppermute | solution.py:340
  62.3 23.5 %collective-permute-start.7 = (bf16[128,1024]{1,0:T(8,128)(2,1)}, bf16[128,1024]{1,0:T(8,128)(2,1)S(1)}, u32[]{:S(2)}, u32[]{:S(2)}) collective-permute-start(bf16[128,1024]{1,0:T(8,128)(2,1)} %attention.4.refs_1_), channel_id=1, source_target_pairs={{0,24},{8,16},{16,8},{24,0},{1,25},{9,17},{17,9},{25,1},{2,26},{10... | collective-permute-start | bytes 786440 | tf_op jit(solution)/shard_map/ppermute | solution.py:340
  70.9 23.3 %collective-permute-start.8 = (bf16[128,1024]{1,0:T(8,128)(2,1)}, bf16[128,1024]{1,0:T(8,128)(2,1)S(1)}, u32[]{:S(2)}, u32[]{:S(2)}) collective-permute-start(bf16[128,1024]{1,0:T(8,128)(2,1)} %attention.5), channel_id=1, source_target_pairs={{0,16},{8,24},{16,0},{24,8},{1,17},{9,25},{17,1},{25,9},{2,18},{10... | collective-permute-start | bytes 786440 | tf_op jit(solution)/shard_map/ppermute | solution.py:340
  89.6 19.0 %collective-permute-start.16 = (bf16[128,2048]{1,0:T(8,128)(2,1)}, bf16[128,2048]{1,0:T(8,128)(2,1)}, u32[]{:S(2)}, u32[]{:S(2)}) collective-permute-start(bf16[128,2048]{1,0:T(8,128)(2,1)} %convolution_convert_fusion.2.refs_20_), channel_id=1, source_target_pairs={{0,24},{8,16},{16,8},{24,0},{1,25},{9,17},{17,9},{25,1},{2,26},{10... | collective-permute-start | bytes 1572872 | tf_op jit(solution)/shard_map/ppermute | solution.py:340
  93.6 20.8 %collective-permute-start.14 = (bf16[128,2048]{1,0:T(8,128)(2,1)}, bf16[128,2048]{1,0:T(8,128)(2,1)}, u32[]{:S(2)}, u32[]{:S(2)}) collective-permute-start(bf16[128,2048]{1,0:T(8,128)(2,1)} %convolution_convert_fusion.refs_22_), channel_id=1, source_target_pairs={{0,8},{8,0},{16,24},{24,16},{1,9},{9,1},{17,25},{25,17},{2,10},{10... | collective-permute-start | bytes 1572872 | tf_op jit(solution)/shard_map/ppermute | solution.py:340
  95.7 18.7 %collective-permute-start.15 = (bf16[128,2048]{1,0:T(8,128)(2,1)}, bf16[128,2048]{1,0:T(8,128)(2,1)}, u32[]{:S(2)}, u32[]{:S(2)}) collective-permute-start(bf16[128,2048]{1,0:T(8,128)(2,1)} %convolution_convert_fusion.1.refs_21_), channel_id=1, source_target_pairs={{0,16},{8,24},{16,0},{24,8},{1,17},{9,25},{17,1},{25,9},{2,18},{10... | collective-permute-start | bytes 1572872 | tf_op jit(solution)/shard_map/ppermute | solution.py:340
  121.1 218.6 %reduce-scatter.2.cloned.1.call-start = ((), (), s32[]{:S(2)}) async-start(), calls=%async_computation.2 | async-start | bytes 2359296 | tf_op jit(solution)/shard_map/reduce_scatter | solution.py:467
  123.2 23.9 %collective-permute-start.27 = (bf16[128,512]{1,0:T(8,128)(2,1)S(1)}, bf16[128,512]{1,0:T(8,128)(2,1)S(1)}, u32[]{:S(2)}, u32[]{:S(2)}) collective-permute-start(bf16[128,512]{1,0:T(8,128)(2,1)S(1)} %slice.114.refs_2_), channel_id=1, source_target_pairs={{0,4},{1,5},{2,6},{3,7},{4,0},{5,1},{6,2},{7,3},{8,12},{9,13},{10,... | collective-permute-start | bytes 393224 | tf_op jit(solution)/shard_map/ppermute | solution.py:340
  124.2 22.9 %collective-permute-start.26 = (bf16[128,512]{1,0:T(8,128)(2,1)S(1)}, bf16[128,512]{1,0:T(8,128)(2,1)S(1)}, u32[]{:S(2)}, u32[]{:S(2)}) collective-permute-start(bf16[128,512]{1,0:T(8,128)(2,1)S(1)} %slice.114.refs_2_), channel_id=1, source_target_pairs={{0,2},{1,3},{2,0},{3,1},{4,6},{5,7},{6,4},{7,5},{8,10},{9,11},{10,... | collective-permute-start | bytes 393224 | tf_op jit(solution)/shard_map/ppermute | solution.py:340
  152.4 19.9 %collective-permute-start.30 = (bf16[384,512]{1,0:T(8,128)(2,1)}, bf16[384,512]{1,0:T(8,128)(2,1)}, u32[]{:S(2)}, u32[]{:S(2)}) collective-permute-start(bf16[384,512]{1,0:T(8,128)(2,1)} %get-tuple-element.60), channel_id=1, source_target_pairs={{0,8},{8,0},{16,24},{24,16},{1,9},{9,1},{17,25},{25,17},{2,10},{10... | collective-permute-start | bytes 1179656 | tf_op jit(solution)/shard_map/ppermute | solution.py:340
  153.8 19.6 %collective-permute-start.31 = (bf16[384,512]{1,0:T(8,128)(2,1)}, bf16[384,512]{1,0:T(8,128)(2,1)}, u32[]{:S(2)}, u32[]{:S(2)}) collective-permute-start(bf16[384,512]{1,0:T(8,128)(2,1)} %get-tuple-element.61), channel_id=1, source_target_pairs={{0,16},{8,24},{16,0},{24,8},{1,17},{9,25},{17,1},{25,9},{2,18},{10... | collective-permute-start | bytes 1179656 | tf_op jit(solution)/shard_map/ppermute | solution.py:340
  155.3 22.1 %collective-permute-start.32 = (bf16[384,512]{1,0:T(8,128)(2,1)}, bf16[384,512]{1,0:T(8,128)(2,1)}, u32[]{:S(2)}, u32[]{:S(2)}) collective-permute-start(bf16[384,512]{1,0:T(8,128)(2,1)} %get-tuple-element.62), channel_id=1, source_target_pairs={{0,24},{8,16},{16,8},{24,0},{1,25},{9,17},{17,9},{25,1},{2,26},{10... | collective-permute-start | bytes 1179656 | tf_op jit(solution)/shard_map/ppermute | solution.py:340
  167.6 24.2 %collective-permute-start.24 = (bf16[384,512]{1,0:T(8,128)(2,1)S(1)}, bf16[384,512]{1,0:T(8,128)(2,1)S(1)}, u32[]{:S(2)}, u32[]{:S(2)}) collective-permute-start(bf16[384,512]{1,0:T(8,128)(2,1)S(1)} %get-tuple-element.57), channel_id=1, source_target_pairs={{0,16},{8,24},{16,0},{24,8},{1,17},{9,25},{17,1},{25,9},{2,18},{10... | collective-permute-start | bytes 1179656 | tf_op jit(solution)/shard_map/ppermute | solution.py:340
  172.3 20.3 %collective-permute-start.25 = (bf16[384,512]{1,0:T(8,128)(2,1)S(1)}, bf16[384,512]{1,0:T(8,128)(2,1)S(1)}, u32[]{:S(2)}, u32[]{:S(2)}) collective-permute-start(bf16[384,512]{1,0:T(8,128)(2,1)S(1)} %get-tuple-element.58), channel_id=1, source_target_pairs={{0,24},{8,16},{16,8},{24,0},{1,25},{9,17},{17,9},{25,1},{2,26},{10... | collective-permute-start | bytes 1179656 | tf_op jit(solution)/shard_map/ppermute | solution.py:340
  173.4 24.9 %collective-permute-start.20 = (bf16[384,512]{1,0:T(8,128)(2,1)S(1)}, bf16[384,512]{1,0:T(8,128)(2,1)S(1)}, u32[]{:S(2)}, u32[]{:S(2)}) collective-permute-start(bf16[384,512]{1,0:T(8,128)(2,1)S(1)} %get-tuple-element.52), channel_id=1, source_target_pairs={{0,8},{8,0},{16,24},{24,16},{1,9},{9,1},{17,25},{25,17},{2,10},{10... | collective-permute-start | bytes 1179656 | tf_op jit(solution)/shard_map/ppermute | solution.py:340
  177.4 33.1 %collective-permute-start.21 = (bf16[384,512]{1,0:T(8,128)(2,1)S(1)}, bf16[384,512]{1,0:T(8,128)(2,1)S(1)}, u32[]{:S(2)}, u32[]{:S(2)}) collective-permute-start(bf16[384,512]{1,0:T(8,128)(2,1)S(1)} %get-tuple-element.53), channel_id=1, source_target_pairs={{0,16},{8,24},{16,0},{24,8},{1,17},{9,25},{17,1},{25,9},{2,18},{10... | collective-permute-start | bytes 1179656 | tf_op jit(solution)/shard_map/ppermute | solution.py:340
  181.4 29.1 %collective-permute-start.22 = (bf16[384,512]{1,0:T(8,128)(2,1)S(1)}, bf16[384,512]{1,0:T(8,128)(2,1)S(1)}, u32[]{:S(2)}, u32[]{:S(2)}) collective-permute-start(bf16[384,512]{1,0:T(8,128)(2,1)S(1)} %get-tuple-element.54), channel_id=1, source_target_pairs={{0,24},{8,16},{16,8},{24,0},{1,25},{9,17},{17,9},{25,1},{2,26},{10... | collective-permute-start | bytes 1179656 | tf_op jit(solution)/shard_map/ppermute | solution.py:340
  191.9 28.5 %collective-permute-start.17 = (bf16[384,512]{1,0:T(8,128)(2,1)S(1)}, bf16[384,512]{1,0:T(8,128)(2,1)S(1)}, u32[]{:S(2)}, u32[]{:S(2)}) collective-permute-start(bf16[384,512]{1,0:T(8,128)(2,1)S(1)} %get-tuple-element.48), channel_id=1, source_target_pairs={{0,8},{8,0},{16,24},{24,16},{1,9},{9,1},{17,25},{25,17},{2,10},{10... | collective-permute-start | bytes 1179656 | tf_op jit(solution)/shard_map/ppermute | solution.py:340
  192.5 31.4 %collective-permute-start.18 = (bf16[384,512]{1,0:T(8,128)(2,1)S(1)}, bf16[384,512]{1,0:T(8,128)(2,1)S(1)}, u32[]{:S(2)}, u32[]{:S(2)}) collective-permute-start(bf16[384,512]{1,0:T(8,128)(2,1)S(1)} %get-tuple-element.49), channel_id=1, source_target_pairs={{0,16},{8,24},{16,0},{24,8},{1,17},{9,25},{17,1},{25,9},{2,18},{10... | collective-permute-start | bytes 1179656 | tf_op jit(solution)/shard_map/ppermute | solution.py:340
  198.3 25.6 %collective-permute-start.19 = (bf16[384,512]{1,0:T(8,128)(2,1)S(1)}, bf16[384,512]{1,0:T(8,128)(2,1)S(1)}, u32[]{:S(2)}, u32[]{:S(2)}) collective-permute-start(bf16[384,512]{1,0:T(8,128)(2,1)S(1)} %get-tuple-element.50), channel_id=1, source_target_pairs={{0,24},{8,16},{16,8},{24,0},{1,25},{9,17},{17,9},{25,1},{2,26},{10... | collective-permute-start | bytes 1179656 | tf_op jit(solution)/shard_map/ppermute | solution.py:340
  236.3 22.1 %collective-permute-start.37 = (bf16[384,512]{1,0:T(8,128)(2,1)S(1)}, bf16[384,512]{1,0:T(8,128)(2,1)S(1)}, u32[]{:S(2)}, u32[]{:S(2)}) collective-permute-start(bf16[384,512]{1,0:T(8,128)(2,1)S(1)} %get-tuple-element.77), channel_id=1, source_target_pairs={{0,16},{8,24},{16,0},{24,8},{1,17},{9,25},{17,1},{25,9},{2,18},{10... | collective-permute-start | bytes 1179656 | tf_op jit(solution)/shard_map/ppermute | solution.py:340
  237.1 21.4 %collective-permute-start.38 = (bf16[384,512]{1,0:T(8,128)(2,1)S(1)}, bf16[384,512]{1,0:T(8,128)(2,1)S(1)}, u32[]{:S(2)}, u32[]{:S(2)}) collective-permute-start(bf16[384,512]{1,0:T(8,128)(2,1)S(1)} %get-tuple-element.78), channel_id=1, source_target_pairs={{0,24},{8,16},{16,8},{24,0},{1,25},{9,17},{17,9},{25,1},{2,26},{10... | collective-permute-start | bytes 1179656 | tf_op jit(solution)/shard_map/ppermute | solution.py:340
  242.3 21.7 %collective-permute-start.33 = (bf16[384,512]{1,0:T(8,128)(2,1)S(1)}, bf16[384,512]{1,0:T(8,128)(2,1)S(1)}, u32[]{:S(2)}, u32[]{:S(2)}) collective-permute-start(bf16[384,512]{1,0:T(8,128)(2,1)S(1)} %get-tuple-element.70), channel_id=1, source_target_pairs={{0,8},{8,0},{16,24},{24,16},{1,9},{9,1},{17,25},{25,17},{2,10},{10... | collective-permute-start | bytes 1179656 | tf_op jit(solution)/shard_map/ppermute | solution.py:340
  243.7 28.0 %collective-permute-start.34 = (bf16[384,512]{1,0:T(8,128)(2,1)S(1)}, bf16[384,512]{1,0:T(8,128)(2,1)S(1)}, u32[]{:S(2)}, u32[]{:S(2)}) collective-permute-start(bf16[384,512]{1,0:T(8,128)(2,1)S(1)} %get-tuple-element.71), channel_id=1, source_target_pairs={{0,16},{8,24},{16,0},{24,8},{1,17},{9,25},{17,1},{25,9},{2,18},{10... | collective-permute-start | bytes 1179656 | tf_op jit(solution)/shard_map/ppermute | solution.py:340
  247.1 24.5 %collective-permute-start.35 = (bf16[384,512]{1,0:T(8,128)(2,1)S(1)}, bf16[384,512]{1,0:T(8,128)(2,1)S(1)}, u32[]{:S(2)}, u32[]{:S(2)}) collective-permute-start(bf16[384,512]{1,0:T(8,128)(2,1)S(1)} %get-tuple-element.72), channel_id=1, source_target_pairs={{0,24},{8,16},{16,8},{24,0},{1,25},{9,17},{17,9},{25,1},{2,26},{10... | collective-permute-start | bytes 1179656 | tf_op jit(solution)/shard_map/ppermute | solution.py:340
  300.2 19.7 %collective-permute-start.46 = (bf16[384,512]{1,0:T(8,128)(2,1)S(1)}, bf16[384,512]{1,0:T(8,128)(2,1)S(1)}, u32[]{:S(2)}, u32[]{:S(2)}) collective-permute-start(bf16[384,512]{1,0:T(8,128)(2,1)S(1)} %copy-done.12), channel_id=1, source_target_pairs={{0,8},{8,0},{16,24},{24,16},{1,9},{9,1},{17,25},{25,17},{2,10},{10... | collective-permute-start | bytes 1179656 | tf_op jit(solution)/shard_map/ppermute | solution.py:340
  301.3 18.6 %collective-permute-start.47 = (bf16[384,512]{1,0:T(8,128)(2,1)S(1)}, bf16[384,512]{1,0:T(8,128)(2,1)S(1)}, u32[]{:S(2)}, u32[]{:S(2)}) collective-permute-start(bf16[384,512]{1,0:T(8,128)(2,1)S(1)} %copy-done.10), channel_id=1, source_target_pairs={{0,16},{8,24},{16,0},{24,8},{1,17},{9,25},{17,1},{25,9},{2,18},{10... | collective-permute-start | bytes 1179656 | tf_op jit(solution)/shard_map/ppermute | solution.py:340
  (54 other events, 526.1 us)
Sparse Core Ops, SparseCore 0:
  9.0 44.0 all-gather.5
  121.2 41.7 all-gather.3
  277.2 36.6 reduce-scatter.1

commit v3 on v2

--- a/solution.py
+++ b/solution.py
@@ -40,15 +40,15 @@
     k_refs, v_refs = refs[: blocks + 1], refs[blocks + 1 : 2 * blocks + 2]
     o_ref, key_ref, value_ref = refs[2 * blocks + 2 :]
     rows, wide = q_ref.shape
-    half = k_refs[1].shape[0]
     keys = key_ref.shape[0]
+    span, lead = keys // blocks, k_refs[0].shape[0] // blocks
     factor = math.log2(math.e) / math.sqrt(HEAD_DIM)
     for b in range(blocks):
-        lead = slice(2 * b * half, (2 * b + 1) * half)
-        part = slice(b * half, (b + 1) * half)
-        key_ref[lead, :] = k_refs[0][part, :]
-        value_ref[lead, :HEAD_DIM] = v_refs[0][part, :]
-        at = pl.ds(pl.multiple_of((2 * where_ref[3 + b] + 1) * half, half), half)
+        at = slice(b * span, b * span + lead)
+        part = slice(b * lead, (b + 1) * lead)
+        key_ref[at, :] = k_refs[0][part, :]
+        value_ref[at, :HEAD_DIM] = v_refs[0][part, :]
+        at = pl.ds(pl.multiple_of(where_ref[3 + b] * span + lead, lead), span - lead)
         key_ref[at, :] = k_refs[1 + b][...]
         value_ref[at, :HEAD_DIM] = v_refs[1 + b][...]
     value_ref[:, HEAD_DIM:] = jnp.ones((keys, HEAD_DIM), value_ref.dtype)
@@ -75,17 +75,17 @@
             o_ref[:, h * HEAD_DIM : (h + 1) * HEAD_DIM] = out[i * rows : (i + 1) * rows]
 
 
-def attention(queries, kv_lead, kv_blocks, where, old, peers, deps):
+def attention(queries, kv_lead, kv_blocks, span, where, old, peers, deps):
     rows = queries.shape[0]
     wide = queries.shape[1] // peers
     blocks = len(kv_blocks)
-    half = kv_blocks[0].shape[0]
-    keys = 2 * half * blocks
+    keys = blocks * span
+    lead = kv_lead.shape[0] // blocks
 
     def column(size, first):
         return pl.BlockSpec((size, HEAD_DIM), lambda i, where: (0, first + where[1]))
 
-    sizes = [half * blocks] + [half] * blocks
+    sizes = [lead * blocks] + [span - lead] * blocks
     return call(
         functools.partial(attention_kernel, blocks=blocks, stack=2, old=old),
         deps,
@@ -317,20 +317,35 @@
     )(order, place, gate)
 
 
-def hold_kernel(x_ref, o_ref):
-    o_ref[...] = x_ref[...]
-
-
-def hold(value, deps):
+def norm_kernel(tokens_ref, own_ref, gain_ref, *refs):
+    *part_refs, res_ref, first_ref, rest_ref = refs
+    width, span = tokens_ref.shape[1], first_ref.shape[1]
+    total = own_ref[...]
+    for ref in part_refs:
+        total = total + ref[...].astype(jnp.float32)
+    res = (tokens_ref[...].astype(jnp.float32) + total).astype(res_ref.dtype)
+    res_ref[...] = res
+    res = res.astype(jnp.float32)
+    mean = jnp.sum(res * res, axis=1, keepdims=True) * (1.0 / width)
+    normed = (res * lax.rsqrt(mean + 1e-06) * gain_ref[...]).astype(first_ref.dtype)
+    first_ref[...] = normed[:, :span]
+    rest_ref[...] = normed[:, span:]
+
+
+def norm(tokens, own, gain, parts, span):
+    rows, width = tokens.shape
     vmem = pl.BlockSpec(memory_space=pltpu.VMEM)
+    operands = [tokens, own, gain, *parts]
     return call(
-        hold_kernel,
-        deps,
-        [value],
-        [vmem],
-        out_specs=vmem,
-        out_shape=jax.ShapeDtypeStruct(value.shape, value.dtype),
-        name="hold",
+        norm_kernel,
+        [],
+        operands,
+        [vmem] * len(operands),
+        out_specs=[vmem] * 3,
+        out_shape=[
+            jax.ShapeDtypeStruct((rows, size), jnp.bfloat16) for size in (width, span, width - span)
+        ],
+        name="norm",
     )
 
 
@@ -338,6 +353,14 @@
     if k == 0:
         return value
     return lax.ppermute(value, axis, [(i, i ^ k) for i in range(lax.axis_size(axis))])
+
+
+def chip_exchange(value, turn):
+    if turn == 0:
+        return value
+    count = lax.axis_size("ctx")
+    steps = (2 * turn, count - 2 * turn)
+    return lax.ppermute(value, "ctx", [(i, i ^ steps[i % 2]) for i in range(count)])
 
 
 def per_device(
@@ -362,47 +385,49 @@
     column = ctx_count * tok_count
     turn = [k for k in reversed(range(peers))]
 
+    turns = 2 * jnp.arange(chips, dtype=jnp.int32)
+    back_turns = (ctx_count - turns) % ctx_count
+    even = here % 2 == 0
     order = here ^ jnp.concatenate(
-        [2 * jnp.arange(chips, dtype=jnp.int32) + core for core in range(2)]
-    )
-
-    half = keys_values.shape[1] // 2
-    kv_same = [exchange(keys_values[0, half:], "ctx", 2 * s) for s in reversed(range(chips))][::-1]
-    kv_lead = lax.all_gather(keys_values[0, :half], "ctx", axis=0, tiled=True)
+        [
+            jnp.where(even, turns, back_turns),
+            jnp.where(even, back_turns, turns) + 1,
+        ]
+    )
+
+    kv_span = keys_values.shape[1]
+    lead = kv_span // 2
+    routes = jnp.concatenate([expert_ids.astype(jnp.bfloat16), gates.astype(jnp.bfloat16)], axis=1)
+    routes = jnp.pad(routes.T, ((0, 0), (0, keys_values.shape[2] - tok_count)))
+    block = jnp.concatenate([keys_values[0, lead:], routes], axis=0)
+    kv_same = [chip_exchange(block, s) for s in reversed(range(chips))][::-1]
+    kv_lead = lax.all_gather(keys_values[0, :lead], "ctx", axis=0, tiled=True)
     kv_blocks = kv_same + [exchange(b, "ctx", 1) for b in kv_same]
 
-    def route(attended):
-        routes = jnp.concatenate([expert_ids.astype(jnp.float32), gates], axis=1).T
-        routes = hold(routes, [attended])
-        pair = jnp.concatenate([routes, exchange(routes, "ctx", 1)], axis=1)
-        pairs = [exchange(pair, "ctx", 2 * s) for s in range(chips)]
-        routes = jnp.concatenate(
-            [p[:, :tok_count] for p in pairs] + [p[:, tok_count:] for p in pairs], axis=1
-        )
-        ids, gate_rows = routes[:TOPK].astype(jnp.int32), routes[TOPK:]
-        owner = me ^ jnp.arange(peers, dtype=jnp.int32)
-        wanted = (
-            ((owner * ctx_count + here) * local)[:, None] + jnp.arange(local, dtype=jnp.int32)[None, :]
-        ).reshape(-1)
-        same = ids[None, :, :] == wanted[:, None, None]
-        named = jnp.any(same, axis=1)
-        gate_of = jnp.sum(jnp.where(same, gate_rows[None], 0.0), axis=1)
-        earlier = jnp.triu(jnp.ones((tok_count, tok_count), jnp.bfloat16), 1)
-        rank = jnp.dot(
-            named.reshape(-1, tok_count).astype(jnp.bfloat16),
-            earlier,
-            preferred_element_type=jnp.float32,
-        ).astype(jnp.int32)
-        place = rank.reshape(-1, column) + jnp.repeat(order * CAP, tok_count)
-        place = jnp.where(named, place, -1)
-        pick, mix = tables(
-            order, place.reshape(peers, local, column), gate_of.reshape(peers, local, column), slots
-        )
-        return pick, mix
+    routes = jnp.concatenate([b[kv_span - lead :, :tok_count] for b in kv_blocks], axis=1).astype(jnp.float32)
+    ids, gate_rows = routes[:TOPK].astype(jnp.int32), routes[TOPK:]
+    owner = me ^ jnp.arange(peers, dtype=jnp.int32)
+    wanted = (
+        ((owner * ctx_count + here) * local)[:, None] + jnp.arange(local, dtype=jnp.int32)[None, :]
+    ).reshape(-1)
+    same = ids[None, :, :] == wanted[:, None, None]
+    named = jnp.any(same, axis=1)
+    gate_of = jnp.sum(jnp.where(same, gate_rows[None], 0.0), axis=1)
+    earlier = jnp.triu(jnp.ones((tok_count, tok_count), jnp.bfloat16), 1)
+    rank = jnp.dot(
+        named.reshape(-1, tok_count).astype(jnp.bfloat16),
+        earlier,
+        preferred_element_type=jnp.float32,
+    ).astype(jnp.int32)
+    place = rank.reshape(-1, column) + jnp.repeat(order * CAP, tok_count)
+    place = jnp.where(named, place, -1)
+    pick, mix = tables(
+        order, place.reshape(peers, local, column), gate_of.reshape(peers, local, column), slots
+    )
 
     old = keys_values.shape[1] * ctx_count - column
     heads = H // peers
-    sums, sent, deps = {}, {}, []
+    sent, deps = {}, []
     for k in turn:
         peer = me ^ k
         where = jnp.concatenate(
@@ -413,30 +438,23 @@
                 order,
             ]
         )
-        if k == turn[0]:
-            attended = attention(queries, kv_lead, kv_blocks, where, old, peers, deps)
-            pick, mix = route(attended)
         if k == 0:
-            for j in turn[:-1]:
-                part = jnp.dot(sent[j], out_weight, preferred_element_type=jnp.float32)
-                deps.append(part.astype(jnp.bfloat16))
-                sums[j] = exchange(deps[-1], "grp", j)
-            deps += [pick, mix]
-        if k != turn[0]:
-            attended = attention(queries, kv_lead, kv_blocks, where, old, peers, deps)
+            deps = [
+                jnp.dot(sent[j], out_weight, preferred_element_type=jnp.float32).astype(jnp.bfloat16)
+                for j in turn[:-1]
+            ]
+            sums = [exchange(d, "grp", j) for j, d in zip(turn[:-1], deps)]
+            deps = deps + [pick, mix]
+        attended = attention(queries, kv_lead, kv_blocks, kv_span, where, old, peers, deps)
         sent[k] = exchange(attended, "grp", k)
-    sums[0] = jnp.dot(sent[0], out_weight, preferred_element_type=jnp.float32)
-    projected = sum(sums[k].astype(jnp.float32) for k in range(peers))
-    residual = (tokens.astype(jnp.float32) + projected).astype(jnp.bfloat16)
+    own = jnp.dot(sent[0], out_weight, preferred_element_type=jnp.float32)
+    span = width // CHUNKS
+    residual, first, rest = norm(tokens, own, moe_gain[None, :], sums, span)
     wide = residual.astype(jnp.float32)
-    normed = (
-        wide * lax.rsqrt(jnp.mean(wide * wide, axis=1, keepdims=True) + 1e-06) * moe_gain
-    ).astype(jnp.bfloat16)
-
-    span = width // CHUNKS
-    same = [exchange(normed[:, :span], "ctx", 2 * s) for s in range(chips)]
+
+    same = [chip_exchange(first, s) for s in range(chips)]
     blocks = same + [exchange(jnp.concatenate(same, axis=0), "ctx", 1)]
-    rest = lax.all_gather(normed[:, span:], "ctx", axis=0, tiled=True)
+    rest = lax.all_gather(rest, "ctx", axis=0, tiled=True)
     rows = pick_rows(order, pick, blocks, peers)
     parts = []
     for c in range(CHUNKS):
@@ -473,7 +491,7 @@
             total = wide[:, c * span : (c + 1) * span] + both[:tok_count]
             for s in range(1, chips):
                 piece = both[s * tok_count : (s + 1) * tok_count].astype(jnp.bfloat16)
-                total = total + exchange(piece, "ctx", 2 * s).astype(jnp.float32)
+                total = total + chip_exchange(piece, s).astype(jnp.float32)
         outs.append(total.astype(jnp.bfloat16))
     return jnp.concatenate(outs, axis=1)
 

time: 349 us -> 343 us (0.983)
  waiting for transfers between devices: 143 us -> 115 us
  starting transfers between devices: 56.3 us -> 78.8 us
    ppermute x53 -> x37, waiting for transfers between devices: 136 us -> 49.8 us  [exchange(): lax.ppermute(value, axis, [(i, i ^ k) for i in range(lax.axis_size(axis))])]
    ppermute x0 -> x12, waiting for transfers between devices: none -> 51.1 us  [chip_exchange(): lax.ppermute(value, 'ctx', [(i, i ^ steps[i % 2]) for i in range(count)])]
    ppermute x0 -> x12, starting transfers between devices: none -> 27.3 us  [chip_exchange(): lax.ppermute(value, 'ctx', [(i, i ^ steps[i % 2]) for i in range(count)])]
    all_gather x2, waiting for transfers between devices: 7.18 us -> 14.1 us  [the longest x1 13.5 us: per_device(): rest = lax.all_gather(rest, 'ctx', axis=0, tiled=True)]
    ppermute x53 -> x37, starting transfers between devices: 56.2 us -> 51.4 us  [exchange(): lax.ppermute(value, axis, [(i, i ^ k) for i in range(lax.axis_size(axis))])]
    unnamed x67 -> x70, local copies, waits for them, and re-layouts: 7.43 us -> 6.77 us
  transfers between devices with their start and end apart: 56 -> 52, of which waited for: 28 -> 28; matrix products, arithmetic and copies ran while one was open for 4% -> 4% of each run, Pallas kernels for 24% -> 25%
where the time goes in v3:
time: 343 us; the launch traced here: 342 us
  waiting for transfers between devices  115 us (34%)
  Pallas kernels  108 us (31%)
  starting transfers between devices  78.8 us (23%)
  between operations  13.7 us (4%)
  matrix products  10.6 us (3%)
  local copies, waits for them, and re-layouts  8.85 us (3%)
  other arithmetic  7.73 us (2%)
    pallas_call x19, Pallas kernels, call(): pl.pallas_call(run, compiler_params=params, **kwargs)(*operands, *deps)  88.8 us
    ppermute x37, starting transfers between devices, exchange(): lax.ppermute(value, axis, [(i, i ^ k) for i in range(lax.axis_size(axis))])  51.4 us
    ppermute x12, waiting for transfers between devices, chip_exchange(): lax.ppermute(value, 'ctx', [(i, i ^ steps[i % 2]) for i in range(count)])  51.1 us
    ppermute x37, waiting for transfers between devices, exchange(): lax.ppermute(value, axis, [(i, i ^ k) for i in range(lax.axis_size(axis))])  49.8 us
    ppermute x12, starting transfers between devices, chip_exchange(): lax.ppermute(value, 'ctx', [(i, i ^ steps[i % 2]) for i in range(count)])  27.3 us
    pallas_call x4, Pallas kernels, expert_down(): pl.pallas_call(down_kernel, grid=(local,), in_specs=[pl.BlockSpec((1, row...  15.1 us
    all_gather x1, waiting for transfers between devices, per_device(): rest = lax.all_gather(rest, 'ctx', axis=0, tiled=True)  13.5 us
    dot_general x3, matrix products, per_device(): jnp.dot(sent[j], out_weight, preferred_element_type=jnp.float32)  7.32 us
  transfers between devices with their start and end apart: 52, of which 28 were waited for; matrix products, arithmetic and copies ran while one was open for 4% of the time, Pallas kernels for 25%

profile of v3, /device:TPU:0, one launch (start us, length us, event | category | flops | bytes accessed | tf_op | source)
XLA Modules:
  0.0 342.5 jit_solution(7155297941527483617)
XLA Ops:
  17.1 8.6 %collective-permute-done.refs_4_.refs_13_ = bf16[144,1024]{1,0:T(8,128)(2,1)S(1)} collective-permute-done((bf16[144,1024]{1,0:T(8,128)(2,1)S(1)}, bf16[144,1024]{1,0:T(8,128)(2,1)S(1)}, u32[]{:S(2)}, u32[]{:S(2)}) %collective-permute-start) | collective-permute-done | bytes 294944 | tf_op jit(solution)/shard_map/ppermute | solution.py:363
  25.8 15.1 %collective-permute-done.1.refs_5_.refs_14_ = bf16[144,1024]{1,0:T(8,128)(2,1)S(1)} collective-permute-done((bf16[144,1024]{1,0:T(8,128)(2,1)S(1)}, bf16[144,1024]{1,0:T(8,128)(2,1)S(1)}, u32[]{:S(2)}, u32[]{:S(2)}) %collective-permute-start.1) | collective-permute-done | bytes 294944 | tf_op jit(solution)/shard_map/ppermute | solution.py:363
  40.8 14.1 %collective-permute-start.5 = (bf16[144,1024]{1,0:T(8,128)(2,1)S(1)}, bf16[144,1024]{1,0:T(8,128)(2,1)S(1)}, u32[]{:S(2)}, u32[]{:S(2)}) collective-permute-start(bf16[144,1024]{1,0:T(8,128)(2,1)S(1)} %collective-permute-done.1.refs_5_.refs_14_), channel_id=1, source_target_pairs={{0,1},{1,0},{2,3},{3,2},{4,5},{5,4},{6,7},{7,6},{8,9},{9,8},{10,11... | collective-permute-start | bytes 884744 | tf_op jit(solution)/shard_map/ppermute | solution.py:355
  57.8 6.2 %attention.4 = bf16[128,1024]{1,0:T(8,128)(2,1)} custom-call(s32[11]{0:T(128)} %get-tuple-element.107.refs_0_, bf16[128,4096]{1,0:T(8,128)(2,1)} %refs_1_.7, bf16[1024,1024]{1,0:T(8,128)(2,1)} %bitcast.29, bf16[144,1024]{1,0:T(8,128)(2,1)} %copy-done.23, bf16[144,1024]{1,0:T(8,128)(2,1)} %copy-done.24, bf16[144,1024]{1,0:T(8,128)(2,1)} %copy-done.25, ...), custom_call_target="tpu_custom_call" | custom-call | flops 1073741824 | bytes 1572864 | tf_op jit(solution)/shard_map/attention/pallas_call | solution.py:36
  66.4 6.1 %attention.5 = bf16[128,1024]{1,0:T(8,128)(2,1)} custom-call(s32[11]{0:T(128)} %get-tuple-element.106.refs_0_, bf16[128,4096]{1,0:T(8,128)(2,1)} %refs_1_.7, bf16[1024,1024]{1,0:T(8,128)(2,1)} %bitcast.31, bf16[144,1024]{1,0:T(8,128)(2,1)} %copy-done.23, bf16[144,1024]{1,0:T(8,128)(2,1)} %copy-done.24, bf16[144,1024]{1,0:T(8,128)(2,1)} %copy-done.25, ...), custom_call_target="tpu_custom_call" | custom-call | flops 1073741824 | bytes 1572864 | tf_op jit(solution)/shard_map/attention/pallas_call | solution.py:36
  73.1 6.1 %attention.6 = bf16[128,1024]{1,0:T(8,128)(2,1)} custom-call(s32[11]{0:T(128)} %get-tuple-element.105.refs_0_, bf16[128,4096]{1,0:T(8,128)(2,1)} %refs_1_.7, bf16[1024,1024]{1,0:T(8,128)(2,1)} %bitcast.33, bf16[144,1024]{1,0:T(8,128)(2,1)} %copy-done.23, bf16[144,1024]{1,0:T(8,128)(2,1)} %copy-done.24, bf16[144,1024]{1,0:T(8,128)(2,1)} %copy-done.25, ...), custom_call_target="tpu_custom_call" | custom-call | flops 1073741824 | bytes 1572864 | tf_op jit(solution)/shard_map/attention/pallas_call | solution.py:36
  79.8 4.2 %convolution_convert_fusion.2.refs_20_ = bf16[128,2048]{1,0:T(8,128)(2,1)} fusion(bf16[128,1024]{1,0:T(8,128)(2,1)S(1)} %collective-permute-done.7, bf16[1024,2048]{1,0:T(8,128)(2,1)} %param.13), kind=kOutput, calls=%fused_computation.2 | convolution fusion | flops 537133056 | bytes 4980736 | tf_op jit(solution)/shard_map/dot_general | solution.py:443
  90.9 3.9 %tables.1 = (bf16[1536,1024]{1,0:T(8,128)(2,1)S(1)}, bf16[1024,1536]{1,0:T(8,128)(2,1)}) custom-call(s32[8]{0:T(128)S(1)} %get-tuple-element.96.order_ref.refs_0_, s32[4,4,1024]{2,1,0:T(4,128)S(1)} %add_select_fusion.place_ref, f32[4,4,1024]{2,1,0:T(4,128)S(1)} %reshape.43.gate_ref), custom_call_target="tpu_custom_call" | custom-call | flops 6291456 | bytes 6291456 | tf_op jit(solution)/shard_map/tables/pallas_call | solution.py:297
  96.4 6.1 %attention.7 = bf16[128,1024]{1,0:T(8,128)(2,1)} custom-call(s32[11]{0:T(128)} %add_add_fusion.refs_0_, bf16[128,4096]{1,0:T(8,128)(2,1)} %refs_1_.7, bf16[1024,1024]{1,0:T(8,128)(2,1)} %bitcast.35, bf16[144,1024]{1,0:T(8,128)(2,1)} %copy-done.23, bf16[144,1024]{1,0:T(8,128)(2,1)} %copy-done.24, bf16[144,1024]{1,0:T(8,128)(2,1)} %copy-done.25, ...), custom_call_target="tpu_custom_call" | custom-call | flops 1073741824 | bytes 1572864 | tf_op jit(solution)/shard_map/attention/pallas_call | solution.py:36
  105.7 5.1 %collective-permute-done.11.refs_4_ = bf16[128,2048]{1,0:T(8,128)(2,1)} collective-permute-done((bf16[128,2048]{1,0:T(8,128)(2,1)}, bf16[128,2048]{1,0:T(8,128)(2,1)}, u32[]{:S(2)}, u32[]{:S(2)}) %collective-permute-start.11) | collective-permute-done | bytes 524320 | tf_op jit(solution)/shard_map/ppermute | solution.py:355
  121.3 9.6 %collective-permute-done.23.refs_4_ = bf16[128,512]{1,0:T(8,128)(2,1)S(1)} collective-permute-done((bf16[128,512]{1,0:T(8,128)(2,1)S(1)}, bf16[128,512]{1,0:T(8,128)(2,1)S(1)}, u32[]{:S(2)}, u32[]{:S(2)}) %collective-permute-start.23) | collective-permute-done | bytes 131104 | tf_op jit(solution)/shard_map/ppermute | solution.py:363
  136.3 3.2 pick_rows.7
  143.1 13.5 %all-gather.4.cloned.1.call-done.refs_2_ = bf16[1024,1536]{1,0:T(8,128)(2,1)} async-done(((bf16[128,1536]{1,0:T(8,128)(2,1)}), bf16[1024,1536]{1,0:T(8,128)(2,1)}) %all-gather.4.cloned.1.call-update) | async-done | bytes 3145744 | tf_op jit(solution)/shard_map/all_gather | solution.py:457
  173.0 8.1 %expert_hidden.4 = (f32[4,384,768]{2,1,0:T(8,128)}, f32[4,384,768]{2,1,0:T(8,128)}) custom-call(bf16[384,512]{1,0:T(8,128)(2,1)S(1)} %get-tuple-element.65.refs_0_, bf16[384,512]{1,0:T(8,128)(2,1)} %collective-permute-done.26.refs_1_, bf16[384,512]{1,0:T(8,128)(2,1)} %collective-permute-done.27.refs_2_, bf16[384,512]{1,0:T(8,128)(2,1)} %collective-permute-done.28.refs_3_, ...), custom_call_target="tpu_custom_call" | custom-call | flops 2415919104 | bytes 18087936 | tf_op jit(solution)/shard_map/expert_hidden/pallas_call | solution.py:36
  183.3 5.2 %collective-permute-done.21.refs_3_ = bf16[384,512]{1,0:T(8,128)(2,1)S(1)} collective-permute-done((bf16[384,512]{1,0:T(8,128)(2,1)S(1)}, bf16[384,512]{1,0:T(8,128)(2,1)S(1)}, u32[]{:S(2)}, u32[]{:S(2)}) %collective-permute-start.21) | collective-permute-done | bytes 393248 | tf_op jit(solution)/shard_map/ppermute | solution.py:355
  190.1 9.8 %expert_hidden.5 = (f32[4,384,768]{2,1,0:T(8,128)}, f32[4,384,768]{2,1,0:T(8,128)}) custom-call(bf16[384,512]{1,0:T(8,128)(2,1)S(1)} %get-tuple-element.60.refs_0_, bf16[384,512]{1,0:T(8,128)(2,1)S(1)} %collective-permute-done.19.refs_1_, bf16[384,512]{1,0:T(8,128)(2,1)S(1)} %collective-permute-done.20.refs_2_, ...), custom_call_target="tpu_custom_call" | custom-call | flops 2415919104 | bytes 18087936 | tf_op jit(solution)/shard_map/expert_hidden/pallas_call | solution.py:36
  202.2 9.9 %expert_hidden.6 = (f32[4,384,768]{2,1,0:T(8,128)}, f32[4,384,768]{2,1,0:T(8,128)}) custom-call(bf16[384,512]{1,0:T(8,128)(2,1)S(1)} %get-tuple-element.56.refs_0_, bf16[384,512]{1,0:T(8,128)(2,1)S(1)} %collective-permute-done.16.refs_1_, bf16[384,512]{1,0:T(8,128)(2,1)S(1)} %collective-permute-done.17.refs_2_, ...), custom_call_target="tpu_custom_call" | custom-call | flops 2415919104 | bytes 18087936 | tf_op jit(solution)/shard_map/expert_hidden/pallas_call | solution.py:36
  212.0 5.6 %collective-permute-done.14.refs_2_ = bf16[384,512]{1,0:T(8,128)(2,1)S(1)} collective-permute-done((bf16[384,512]{1,0:T(8,128)(2,1)S(1)}, bf16[384,512]{1,0:T(8,128)(2,1)S(1)}, u32[]{:S(2)}, u32[]{:S(2)}) %collective-permute-start.14) | collective-permute-done | bytes 393248 | tf_op jit(solution)/shard_map/ppermute | solution.py:355
  217.7 7.3 %expert_hidden.7.h_ref = bf16[4,384,768]{2,1,0:T(8,128)(2,1)S(1)} custom-call(bf16[384,512]{1,0:T(8,128)(2,1)S(1)} %get-tuple-element.52.refs_6_.refs_8_.refs_0_, bf16[384,512]{1,0:T(8,128)(2,1)S(1)} %collective-permute-done.13.refs_1_, bf16[384,512]{1,0:T(8,128)(2,1)S(1)} %collective-permute-done.14.refs_2_, ...), custom_call_target="tpu_custom_call" | custom-call | flops 2415919104 | bytes 18087936 | tf_op jit(solution)/shard_map/expert_hidden/pallas_call | solution.py:36
  225.0 3.8 %expert_down.5 = (bf16[384,512]{1,0:T(8,128)(2,1)S(1)}, bf16[384,512]{1,0:T(8,128)(2,1)S(1)}, bf16[384,512]{1,0:T(8,128)(2,1)S(1)}, bf16[384,512]{1,0:T(8,128)(2,1)S(1)}) custom-call(bf16[4,384,768]{2,1,0:T(8,128)(2,1)S(1)} %expert_hidden.7.h_ref, bf16[4,768,2048]{2,1,0:T(8,128)(2,1)} %w_ref.7), custom_call_target="tpu_custom_call" | custom-call | flops 1207959552 | bytes 7077888 | tf_op jit(solution)/shard_map/expert_down/pallas_call | solution.py:219
  232.3 3.8 %expert_down.4 = (bf16[384,512]{1,0:T(8,128)(2,1)S(1)}, bf16[384,512]{1,0:T(8,128)(2,1)S(1)}, bf16[384,512]{1,0:T(8,128)(2,1)S(1)}, bf16[384,512]{1,0:T(8,128)(2,1)S(1)}) custom-call(bf16[4,384,768]{2,1,0:T(8,128)(2,1)S(1)} %expert_hidden.7.h_ref, bf16[4,768,2048]{2,1,0:T(8,128)(2,1)} %w_ref.7), custom_call_target="tpu_custom_call" | custom-call | flops 1207959552 | bytes 7077888 | tf_op jit(solution)/shard_map/expert_down/pallas_call | solution.py:219
  237.8 3.1 collective-permute-done.32.refs_3_
  241.9 3.8 %expert_down.7 = (bf16[384,512]{1,0:T(8,128)(2,1)S(1)}, bf16[384,512]{1,0:T(8,128)(2,1)S(1)}, bf16[384,512]{1,0:T(8,128)(2,1)S(1)}, bf16[384,512]{1,0:T(8,128)(2,1)S(1)}) custom-call(bf16[4,384,768]{2,1,0:T(8,128)(2,1)S(1)} %expert_hidden.7.h_ref, bf16[4,768,2048]{2,1,0:T(8,128)(2,1)} %w_ref.7), custom_call_target="tpu_custom_call" | custom-call | flops 1207959552 | bytes 7077888 | tf_op jit(solution)/shard_map/expert_down/pallas_call | solution.py:219
  248.0 3.8 %expert_down.6 = (bf16[384,512]{1,0:T(8,128)(2,1)S(1)}, bf16[384,512]{1,0:T(8,128)(2,1)S(1)}, bf16[384,512]{1,0:T(8,128)(2,1)S(1)}, bf16[384,512]{1,0:T(8,128)(2,1)S(1)}) custom-call(bf16[4,384,768]{2,1,0:T(8,128)(2,1)S(1)} %expert_hidden.7.h_ref, bf16[4,768,2048]{2,1,0:T(8,128)(2,1)} %w_ref.7), custom_call_target="tpu_custom_call" | custom-call | flops 1207959552 | bytes 7077888 | tf_op jit(solution)/shard_map/expert_down/pallas_call | solution.py:219
  251.8 4.2 %mix_rows.7 = bf16[1024,512]{1,0:T(8,128)(2,1)S(1)} custom-call(s32[8]{0:T(128)S(1)} %get-tuple-element.96.order_ref.refs_0_, bf16[1024,1536]{1,0:T(8,128)(2,1)} %get-tuple-element.49.refs_24_.refs_1_, bf16[384,512]{1,0:T(8,128)(2,1)S(1)} %get-tuple-element.79.refs_6_.refs_2_, bf16[384,512]{1,0:T(8,128)(2,1)S(1)} %collective-permute-done.32.refs_3_, ...), custom_call_target="tpu_custom_call" | custom-call | flops 1610612736 | bytes 5767168 | tf_op jit(solution)/shard_map/mix_rows/pallas_call | solution.py:36
  257.8 6.4 %collective-permute-done.30.refs_4_ = bf16[384,512]{1,0:T(8,128)(2,1)S(1)} collective-permute-done((bf16[384,512]{1,0:T(8,128)(2,1)S(1)}, bf16[384,512]{1,0:T(8,128)(2,1)S(1)}, u32[]{:S(2)}, u32[]{:S(2)}) %collective-permute-start.30) | collective-permute-done | bytes 393248 | tf_op jit(solution)/shard_map/ppermute | solution.py:355
  264.3 3.7 %mix_rows.6 = bf16[1024,512]{1,0:T(8,128)(2,1)S(1)} custom-call(s32[8]{0:T(128)S(1)} %get-tuple-element.96.order_ref.refs_0_, bf16[1024,1536]{1,0:T(8,128)(2,1)} %get-tuple-element.49.refs_24_.refs_1_, bf16[384,512]{1,0:T(8,128)(2,1)S(1)} %get-tuple-element.75.refs_2_, bf16[384,512]{1,0:T(8,128)(2,1)S(1)} %collective-permute-done.29.refs_3_, ...), custom_call_target="tpu_custom_call" | custom-call | flops 1610612736 | bytes 5767168 | tf_op jit(solution)/shard_map/mix_rows/pallas_call | solution.py:36
  273.2 8.8 %collective-permute-done.35.refs_3_ = bf16[384,512]{1,0:T(8,128)(2,1)S(1)} collective-permute-done((bf16[384,512]{1,0:T(8,128)(2,1)}, bf16[384,512]{1,0:T(8,128)(2,1)S(1)}, u32[]{:S(2)}, u32[]{:S(2)}) %collective-permute-start.35) | collective-permute-done | bytes 393248 | tf_op jit(solution)/shard_map/ppermute | solution.py:355
  282.0 4.5 %collective-permute-done.36.refs_4_ = bf16[384,512]{1,0:T(8,128)(2,1)S(1)} collective-permute-done((bf16[384,512]{1,0:T(8,128)(2,1)}, bf16[384,512]{1,0:T(8,128)(2,1)S(1)}, u32[]{:S(2)}, u32[]{:S(2)}) %collective-permute-start.36) | collective-permute-done | bytes 393248 | tf_op jit(solution)/shard_map/ppermute | solution.py:355
  302.8 7.4 %collective-permute-start.39 = (bf16[128,512]{1,0:T(8,128)(2,1)S(1)}, bf16[128,512]{1,0:T(8,128)(2,1)S(1)}, u32[]{:S(2)}, u32[]{:S(2)}) collective-permute-start(bf16[128,512]{1,0:T(8,128)(2,1)S(1)} %get-tuple-element.100), channel_id=1, source_target_pairs={{0,2},{1,7},{2,0},{3,5},{4,6},{5,3},{6,4},{7,1},{8,10},{9,15},{10,... | collective-permute-start | bytes 393224 | tf_op jit(solution)/shard_map/ppermute | solution.py:363
  323.1 3.8 %collective-permute-done.48 = bf16[128,512]{1,0:T(8,128)(2,1)S(1)} collective-permute-done((bf16[128,512]{1,0:T(8,128)(2,1)S(1)}, bf16[128,512]{1,0:T(8,128)(2,1)S(1)}, u32[]{:S(2)}, u32[]{:S(2)}) %collective-permute-start.48) | collective-permute-done | bytes 131104 | tf_op jit(solution)/shard_map/ppermute | solution.py:363
  326.9 6.9 %collective-permute-done.47 = bf16[128,512]{1,0:T(8,128)(2,1)S(1)} collective-permute-done((bf16[128,512]{1,0:T(8,128)(2,1)S(1)}, bf16[128,512]{1,0:T(8,128)(2,1)S(1)}, u32[]{:S(2)}, u32[]{:S(2)}) %collective-permute-start.47) | collective-permute-done | bytes 131104 | tf_op jit(solution)/shard_map/ppermute | solution.py:363
  (210 shorter events, 117.1 us)
Async XLA Ops:
  6.5 51.2 %all-gather.6.cloned.1.call-start = ((), (), s32[]{:S(2)}) async-start(), calls=%async_computation.3 | async-start | bytes 2359296 | tf_op jit(solution)/shard_map/all_gather | solution.py:404
  8.3 148.2 %all-gather.4.cloned.1.call-start = ((), (), s32[]{:S(2)}) async-start(), calls=%async_computation.1 | async-start | bytes 3538944 | tf_op jit(solution)/shard_map/all_gather | solution.py:457
  9.8 15.9 %collective-permute-start = (bf16[144,1024]{1,0:T(8,128)(2,1)S(1)}, bf16[144,1024]{1,0:T(8,128)(2,1)S(1)}, u32[]{:S(2)}, u32[]{:S(2)}) collective-permute-start(bf16[144,1024]{1,0:T(8,128)(2,1)S(1)} %fusion.3.refs_3_.refs_12_), channel_id=1, source_target_pairs={{0,2},{1,7},{2,0},{3,5},{4,6},{5,3},{6,4},{7,1},{8,10},{9,15},{10,... | collective-permute-start | bytes 884744 | tf_op jit(solution)/shard_map/ppermute | solution.py:363
  12.9 27.9 %collective-permute-start.1 = (bf16[144,1024]{1,0:T(8,128)(2,1)S(1)}, bf16[144,1024]{1,0:T(8,128)(2,1)S(1)}, u32[]{:S(2)}, u32[]{:S(2)}) collective-permute-start(bf16[144,1024]{1,0:T(8,128)(2,1)S(1)} %fusion.3.refs_3_.refs_12_), channel_id=1, source_target_pairs={{0,4},{1,5},{2,6},{3,7},{4,0},{5,1},{6,2},{7,3},{8,12},{9,13},{10,... | collective-permute-start | bytes 884744 | tf_op jit(solution)/shard_map/ppermute | solution.py:363
  15.5 39.5 %collective-permute-start.2 = (bf16[144,1024]{1,0:T(8,128)(2,1)S(1)}, bf16[144,1024]{1,0:T(8,128)(2,1)S(1)}, u32[]{:S(2)}, u32[]{:S(2)}) collective-permute-start(bf16[144,1024]{1,0:T(8,128)(2,1)S(1)} %fusion.3.refs_3_.refs_12_), channel_id=1, source_target_pairs={{0,6},{1,3},{2,4},{3,1},{4,2},{5,7},{6,0},{7,5},{8,14},{9,11},{10,... | collective-permute-start | bytes 884744 | tf_op jit(solution)/shard_map/ppermute | solution.py:363
  15.5 39.6 %collective-permute-start.3 = (bf16[144,1024]{1,0:T(8,128)(2,1)S(1)}, bf16[144,1024]{1,0:T(8,128)(2,1)S(1)}, u32[]{:S(2)}, u32[]{:S(2)}) collective-permute-start(bf16[144,1024]{1,0:T(8,128)(2,1)S(1)} %fusion.3.refs_3_.refs_12_), channel_id=1, source_target_pairs={{0,1},{1,0},{2,3},{3,2},{4,5},{5,4},{6,7},{7,6},{8,9},{9,8},{10,11... | collective-permute-start | bytes 884744 | tf_op jit(solution)/shard_map/ppermute | solution.py:355
  25.7 29.4 %collective-permute-start.4 = (bf16[144,1024]{1,0:T(8,128)(2,1)S(1)}, bf16[144,1024]{1,0:T(8,128)(2,1)S(1)}, u32[]{:S(2)}, u32[]{:S(2)}) collective-permute-start(bf16[144,1024]{1,0:T(8,128)(2,1)S(1)} %collective-permute-done.refs_4_.refs_13_), channel_id=1, source_target_pairs={{0,1},{1,0},{2,3},{3,2},{4,5},{5,4},{6,7},{7,6},{8,9},{9,8},{10,11... | collective-permute-start | bytes 884744 | tf_op jit(solution)/shard_map/ppermute | solution.py:355
  64.0 15.8 %collective-permute-start.7 = (bf16[128,1024]{1,0:T(8,128)(2,1)}, bf16[128,1024]{1,0:T(8,128)(2,1)S(1)}, u32[]{:S(2)}, u32[]{:S(2)}) collective-permute-start(bf16[128,1024]{1,0:T(8,128)(2,1)} %attention.4), channel_id=1, source_target_pairs={{0,24},{8,16},{16,8},{24,0},{1,25},{9,17},{17,9},{25,1},{2,26},{10... | collective-permute-start | bytes 786440 | tf_op jit(solution)/shard_map/ppermute | solution.py:355
  84.0 21.7 %collective-permute-start.10 = (bf16[128,2048]{1,0:T(8,128)(2,1)}, bf16[128,2048]{1,0:T(8,128)(2,1)}, u32[]{:S(2)}, u32[]{:S(2)}) collective-permute-start(bf16[128,2048]{1,0:T(8,128)(2,1)} %convolution_convert_fusion.2.refs_20_), channel_id=1, source_target_pairs={{0,24},{8,16},{16,8},{24,0},{1,25},{9,17},{17,9},{25,1},{2,26},{10... | collective-permute-start | bytes 1572872 | tf_op jit(solution)/shard_map/ppermute | solution.py:355
  87.7 23.2 %collective-permute-start.11 = (bf16[128,2048]{1,0:T(8,128)(2,1)}, bf16[128,2048]{1,0:T(8,128)(2,1)}, u32[]{:S(2)}, u32[]{:S(2)}) collective-permute-start(bf16[128,2048]{1,0:T(8,128)(2,1)} %convolution_convert_fusion.1.refs_21_), channel_id=1, source_target_pairs={{0,16},{8,24},{16,0},{24,8},{1,17},{9,25},{17,1},{25,9},{2,18},{10... | collective-permute-start | bytes 1572872 | tf_op jit(solution)/shard_map/ppermute | solution.py:355
  89.8 21.1 %collective-permute-start.12 = (bf16[128,2048]{1,0:T(8,128)(2,1)}, bf16[128,2048]{1,0:T(8,128)(2,1)}, u32[]{:S(2)}, u32[]{:S(2)}) collective-permute-start(bf16[128,2048]{1,0:T(8,128)(2,1)} %convolution_convert_fusion.refs_22_), channel_id=1, source_target_pairs={{0,8},{8,0},{16,24},{24,16},{1,9},{9,1},{17,25},{25,17},{2,10},{10... | collective-permute-start | bytes 1572872 | tf_op jit(solution)/shard_map/ppermute | solution.py:355
  114.4 219.5 %reduce-scatter.2.cloned.1.call-start = ((), (), s32[]{:S(2)}) async-start(), calls=%async_computation.2 | async-start | bytes 2359296 | tf_op jit(solution)/shard_map/reduce_scatter | solution.py:485
  139.6 25.3 %collective-permute-start.26 = (bf16[384,512]{1,0:T(8,128)(2,1)}, bf16[384,512]{1,0:T(8,128)(2,1)}, u32[]{:S(2)}, u32[]{:S(2)}) collective-permute-start(bf16[384,512]{1,0:T(8,128)(2,1)} %get-tuple-element.66), channel_id=1, source_target_pairs={{0,8},{8,0},{16,24},{24,16},{1,9},{9,1},{17,25},{25,17},{2,10},{10... | collective-permute-start | bytes 1179656 | tf_op jit(solution)/shard_map/ppermute | solution.py:355
  139.7 25.7 %collective-permute-start.27 = (bf16[384,512]{1,0:T(8,128)(2,1)}, bf16[384,512]{1,0:T(8,128)(2,1)}, u32[]{:S(2)}, u32[]{:S(2)}) collective-permute-start(bf16[384,512]{1,0:T(8,128)(2,1)} %get-tuple-element.67), channel_id=1, source_target_pairs={{0,16},{8,24},{16,0},{24,8},{1,17},{9,25},{17,1},{25,9},{2,18},{10... | collective-permute-start | bytes 1179656 | tf_op jit(solution)/shard_map/ppermute | solution.py:355
  140.6 29.4 %collective-permute-start.28 = (bf16[384,512]{1,0:T(8,128)(2,1)}, bf16[384,512]{1,0:T(8,128)(2,1)}, u32[]{:S(2)}, u32[]{:S(2)}) collective-permute-start(bf16[384,512]{1,0:T(8,128)(2,1)} %get-tuple-element.68), channel_id=1, source_target_pairs={{0,24},{8,16},{16,8},{24,0},{1,25},{9,17},{17,9},{25,1},{2,26},{10... | collective-permute-start | bytes 1179656 | tf_op jit(solution)/shard_map/ppermute | solution.py:355
  163.4 17.7 %collective-permute-start.19 = (bf16[384,512]{1,0:T(8,128)(2,1)S(1)}, bf16[384,512]{1,0:T(8,128)(2,1)S(1)}, u32[]{:S(2)}, u32[]{:S(2)}) collective-permute-start(bf16[384,512]{1,0:T(8,128)(2,1)S(1)} %get-tuple-element.61), channel_id=1, source_target_pairs={{0,8},{8,0},{16,24},{24,16},{1,9},{9,1},{17,25},{25,17},{2,10},{10... | collective-permute-start | bytes 1179656 | tf_op jit(solution)/shard_map/ppermute | solution.py:355
  164.9 17.0 %collective-permute-start.20 = (bf16[384,512]{1,0:T(8,128)(2,1)S(1)}, bf16[384,512]{1,0:T(8,128)(2,1)S(1)}, u32[]{:S(2)}, u32[]{:S(2)}) collective-permute-start(bf16[384,512]{1,0:T(8,128)(2,1)S(1)} %get-tuple-element.62), channel_id=1, source_target_pairs={{0,16},{8,24},{16,0},{24,8},{1,17},{9,25},{17,1},{25,9},{2,18},{10... | collective-permute-start | bytes 1179656 | tf_op jit(solution)/shard_map/ppermute | solution.py:355
  165.4 23.2 %collective-permute-start.21 = (bf16[384,512]{1,0:T(8,128)(2,1)S(1)}, bf16[384,512]{1,0:T(8,128)(2,1)S(1)}, u32[]{:S(2)}, u32[]{:S(2)}) collective-permute-start(bf16[384,512]{1,0:T(8,128)(2,1)S(1)} %get-tuple-element.63), channel_id=1, source_target_pairs={{0,24},{8,16},{16,8},{24,0},{1,25},{9,17},{17,9},{25,1},{2,26},{10... | collective-permute-start | bytes 1179656 | tf_op jit(solution)/shard_map/ppermute | solution.py:355
  170.0 32.2 %collective-permute-start.17 = (bf16[384,512]{1,0:T(8,128)(2,1)S(1)}, bf16[384,512]{1,0:T(8,128)(2,1)S(1)}, u32[]{:S(2)}, u32[]{:S(2)}) collective-permute-start(bf16[384,512]{1,0:T(8,128)(2,1)S(1)} %get-tuple-element.58), channel_id=1, source_target_pairs={{0,16},{8,24},{16,0},{24,8},{1,17},{9,25},{17,1},{25,9},{2,18},{10... | collective-permute-start | bytes 1179656 | tf_op jit(solution)/shard_map/ppermute | solution.py:355
  171.6 30.5 %collective-permute-start.18 = (bf16[384,512]{1,0:T(8,128)(2,1)S(1)}, bf16[384,512]{1,0:T(8,128)(2,1)S(1)}, u32[]{:S(2)}, u32[]{:S(2)}) collective-permute-start(bf16[384,512]{1,0:T(8,128)(2,1)S(1)} %get-tuple-element.59), channel_id=1, source_target_pairs={{0,24},{8,16},{16,8},{24,0},{1,25},{9,17},{17,9},{25,1},{2,26},{10... | collective-permute-start | bytes 1179656 | tf_op jit(solution)/shard_map/ppermute | solution.py:355
  181.1 30.9 %collective-permute-start.13 = (bf16[384,512]{1,0:T(8,128)(2,1)S(1)}, bf16[384,512]{1,0:T(8,128)(2,1)S(1)}, u32[]{:S(2)}, u32[]{:S(2)}) collective-permute-start(bf16[384,512]{1,0:T(8,128)(2,1)S(1)} %get-tuple-element.53), channel_id=1, source_target_pairs={{0,8},{8,0},{16,24},{24,16},{1,9},{9,1},{17,25},{25,17},{2,10},{10... | collective-permute-start | bytes 1179656 | tf_op jit(solution)/shard_map/ppermute | solution.py:355
  181.8 35.9 %collective-permute-start.14 = (bf16[384,512]{1,0:T(8,128)(2,1)S(1)}, bf16[384,512]{1,0:T(8,128)(2,1)S(1)}, u32[]{:S(2)}, u32[]{:S(2)}) collective-permute-start(bf16[384,512]{1,0:T(8,128)(2,1)S(1)} %get-tuple-element.54), channel_id=1, source_target_pairs={{0,16},{8,24},{16,0},{24,8},{1,17},{9,25},{17,1},{25,9},{2,18},{10... | collective-permute-start | bytes 1179656 | tf_op jit(solution)/shard_map/ppermute | solution.py:355
  188.5 29.1 %collective-permute-start.15 = (bf16[384,512]{1,0:T(8,128)(2,1)S(1)}, bf16[384,512]{1,0:T(8,128)(2,1)S(1)}, u32[]{:S(2)}, u32[]{:S(2)}) collective-permute-start(bf16[384,512]{1,0:T(8,128)(2,1)S(1)} %get-tuple-element.55), channel_id=1, source_target_pairs={{0,24},{8,16},{16,8},{24,0},{1,25},{9,17},{17,9},{25,1},{2,26},{10... | collective-permute-start | bytes 1179656 | tf_op jit(solution)/shard_map/ppermute | solution.py:355
  229.4 22.4 %collective-permute-start.33 = (bf16[384,512]{1,0:T(8,128)(2,1)S(1)}, bf16[384,512]{1,0:T(8,128)(2,1)S(1)}, u32[]{:S(2)}, u32[]{:S(2)}) collective-permute-start(bf16[384,512]{1,0:T(8,128)(2,1)S(1)} %get-tuple-element.83), channel_id=1, source_target_pairs={{0,16},{8,24},{16,0},{24,8},{1,17},{9,25},{17,1},{25,9},{2,18},{10... | collective-permute-start | bytes 1179656 | tf_op jit(solution)/shard_map/ppermute | solution.py:355
  230.4 21.4 %collective-permute-start.34 = (bf16[384,512]{1,0:T(8,128)(2,1)S(1)}, bf16[384,512]{1,0:T(8,128)(2,1)S(1)}, u32[]{:S(2)}, u32[]{:S(2)}) collective-permute-start(bf16[384,512]{1,0:T(8,128)(2,1)S(1)} %get-tuple-element.84), channel_id=1, source_target_pairs={{0,24},{8,16},{16,8},{24,0},{1,25},{9,17},{17,9},{25,1},{2,26},{10... | collective-permute-start | bytes 1179656 | tf_op jit(solution)/shard_map/ppermute | solution.py:355
  236.1 21.7 %collective-permute-start.29 = (bf16[384,512]{1,0:T(8,128)(2,1)S(1)}, bf16[384,512]{1,0:T(8,128)(2,1)S(1)}, u32[]{:S(2)}, u32[]{:S(2)}) collective-permute-start(bf16[384,512]{1,0:T(8,128)(2,1)S(1)} %get-tuple-element.76), channel_id=1, source_target_pairs={{0,8},{8,0},{16,24},{24,16},{1,9},{9,1},{17,25},{25,17},{2,10},{10... | collective-permute-start | bytes 1179656 | tf_op jit(solution)/shard_map/ppermute | solution.py:355
  236.8 27.5 %collective-permute-start.30 = (bf16[384,512]{1,0:T(8,128)(2,1)S(1)}, bf16[384,512]{1,0:T(8,128)(2,1)S(1)}, u32[]{:S(2)}, u32[]{:S(2)}) collective-permute-start(bf16[384,512]{1,0:T(8,128)(2,1)S(1)} %get-tuple-element.77), channel_id=1, source_target_pairs={{0,16},{8,24},{16,0},{24,8},{1,17},{9,25},{17,1},{25,9},{2,18},{10... | collective-permute-start | bytes 1179656 | tf_op jit(solution)/shard_map/ppermute | solution.py:355
  240.9 23.3 %collective-permute-start.31 = (bf16[384,512]{1,0:T(8,128)(2,1)S(1)}, bf16[384,512]{1,0:T(8,128)(2,1)S(1)}, u32[]{:S(2)}, u32[]{:S(2)}) collective-permute-start(bf16[384,512]{1,0:T(8,128)(2,1)S(1)} %get-tuple-element.78), channel_id=1, source_target_pairs={{0,24},{8,16},{16,8},{24,0},{1,25},{9,17},{17,9},{25,1},{2,26},{10... | collective-permute-start | bytes 1179656 | tf_op jit(solution)/shard_map/ppermute | solution.py:355
  271.7 16.2 %collective-permute-start.37 = (bf16[384,512]{1,0:T(8,128)(2,1)}, bf16[384,512]{1,0:T(8,128)(2,1)S(1)}, u32[]{:S(2)}, u32[]{:S(2)}) collective-permute-start(bf16[384,512]{1,0:T(8,128)(2,1)} %copy-done.19), channel_id=1, source_target_pairs={{0,24},{8,16},{16,8},{24,0},{1,25},{9,17},{17,9},{25,1},{2,26},{10... | collective-permute-start | bytes 1179656 | tf_op jit(solution)/shard_map/ppermute | solution.py:355
  295.1 18.7 %collective-permute-start.42 = (bf16[384,512]{1,0:T(8,128)(2,1)S(1)}, bf16[384,512]{1,0:T(8,128)(2,1)S(1)}, u32[]{:S(2)}, u32[]{:S(2)}) collective-permute-start(bf16[384,512]{1,0:T(8,128)(2,1)S(1)} %copy-done.18), channel_id=1, source_target_pairs={{0,8},{8,0},{16,24},{24,16},{1,9},{9,1},{17,25},{25,17},{2,10},{10... | collective-permute-start | bytes 1179656 | tf_op jit(solution)/shard_map/ppermute | solution.py:355
  296.0 19.0 %collective-permute-start.43 = (bf16[384,512]{1,0:T(8,128)(2,1)S(1)}, bf16[384,512]{1,0:T(8,128)(2,1)S(1)}, u32[]{:S(2)}, u32[]{:S(2)}) collective-permute-start(bf16[384,512]{1,0:T(8,128)(2,1)S(1)} %copy-done.16), channel_id=1, source_target_pairs={{0,16},{8,24},{16,0},{24,8},{1,17},{9,25},{17,1},{25,9},{2,18},{10... | collective-permute-start | bytes 1179656 | tf_op jit(solution)/shard_map/ppermute | solution.py:355
  297.4 17.5 %collective-permute-start.44 = (bf16[384,512]{1,0:T(8,128)(2,1)S(1)}, bf16[384,512]{1,0:T(8,128)(2,1)S(1)}, u32[]{:S(2)}, u32[]{:S(2)}) collective-permute-start(bf16[384,512]{1,0:T(8,128)(2,1)S(1)} %copy-done.14), channel_id=1, source_target_pairs={{0,24},{8,16},{16,8},{24,0},{1,25},{9,17},{17,9},{25,1},{2,26},{10... | collective-permute-start | bytes 1179656 | tf_op jit(solution)/shard_map/ppermute | solution.py:355
  (52 other events, 558.7 us)
Sparse Core Ops, SparseCore 0:
  9.0 48.7 all-gather.5
  114.5 41.9 all-gather.3
  269.8 38.7 reduce-scatter.1

commit v4 on v3

--- a/solution.py
+++ b/solution.py
@@ -16,7 +16,7 @@
 CAP = 12
 
 CHUNKS = 4
-VMEM_LIMIT = 48 * 1024 * 1024
+VMEM_LIMIT = 24 * 1024 * 1024
 VMEM_MOST = 60 * 1024 * 1024
 
 
@@ -110,7 +110,7 @@
             transcendentals=rows * wide // HEAD_DIM * keys,
         ),
         name="attention",
-        vmem=VMEM_MOST,
+        vmem=51 * 1024 * 1024,
     )
 
 
@@ -156,6 +156,7 @@
             transcendentals=0,
         ),
         name="pick_rows",
+        vmem=48 * 1024 * 1024,
     )
 
 
@@ -202,6 +203,7 @@
             transcendentals=local * rows * inner,
         ),
         name="expert_hidden",
+        vmem=24 * 1024 * 1024,
     )
 
 
@@ -225,7 +227,7 @@
         ],
         out_specs=[pl.BlockSpec((slots, width), lambda j: (j, 0))] * peers,
         out_shape=[jax.ShapeDtypeStruct((local * slots, width), jnp.bfloat16)] * peers,
-        compiler_params=pltpu.CompilerParams(vmem_limit_bytes=VMEM_LIMIT),
+        compiler_params=pltpu.CompilerParams(vmem_limit_bytes=48 * 1024 * 1024),
         cost_estimate=pl.CostEstimate(
             flops=2 * local * rows * width * inner,
             bytes_accessed=2 * local * (inner * width + rows * (inner + width)),
@@ -269,6 +271,7 @@
             transcendentals=0,
         ),
         name="mix_rows",
+        vmem=48 * 1024 * 1024,
     )
 
 
@@ -307,7 +310,7 @@
             jax.ShapeDtypeStruct((peers * rows, column), jnp.bfloat16),
             jax.ShapeDtypeStruct((column, peers * rows), jnp.bfloat16),
         ],
-        compiler_params=pltpu.CompilerParams(vmem_limit_bytes=VMEM_LIMIT),
+        compiler_params=pltpu.CompilerParams(vmem_limit_bytes=48 * 1024 * 1024),
         cost_estimate=pl.CostEstimate(
             flops=4 * peers * rows * column,
             bytes_accessed=4 * peers * rows * column,

time: 343 us -> 336 us (0.980)
  Pallas kernels: 108 us -> 91.4 us
  waiting for transfers between devices: 115 us -> 129 us
  matrix products: 10.6 us -> 5.45 us
  local copies, waits for them, and re-layouts: 8.85 us -> 13.4 us
  starting transfers between devices: 78.8 us -> 75 us
    pallas_call x19, Pallas kernels: 88.8 us -> 72.3 us  [call(): pl.pallas_call(run, compiler_params=params, **kwargs)(*operands, *deps)]
    ppermute x37, waiting for transfers between devices: 49.8 us -> 60.2 us  [exchange(): lax.ppermute(value, axis, [(i, i ^ k) for i in range(lax.axis_size(axis))])]
    unnamed x70 -> x68, local copies, waits for them, and re-layouts: 6.77 us -> 11.3 us
  transfers between devices with their start and end apart: 52 -> 52, of which waited for: 28 -> 29; matrix products, arithmetic and copies ran while one was open for 4% -> 3% of each run, Pallas kernels for 25% -> 21%
where the time goes in v4:
time: 336 us; the launch traced here: 335 us
  waiting for transfers between devices  129 us (38%)
  Pallas kernels  91.4 us (27%)
  starting transfers between devices  75 us (22%)
  between operations  13.8 us (4%)
  local copies, waits for them, and re-layouts  13.4 us (4%)
  other arithmetic  6.65 us (2%)
  matrix products  5.45 us (2%)
    pallas_call x19, Pallas kernels, call(): pl.pallas_call(run, compiler_params=params, **kwargs)(*operands, *deps)  72.3 us
    ppermute x37, waiting for transfers between devices, exchange(): lax.ppermute(value, axis, [(i, i ^ k) for i in range(lax.axis_size(axis))])  60.2 us
    ppermute x12, waiting for transfers between devices, chip_exchange(): lax.ppermute(value, 'ctx', [(i, i ^ steps[i % 2]) for i in range(count)])  52.6 us
    ppermute x37, starting transfers between devices, exchange(): lax.ppermute(value, axis, [(i, i ^ k) for i in range(lax.axis_size(axis))])  50.9 us
    ppermute x12, starting transfers between devices, chip_exchange(): lax.ppermute(value, 'ctx', [(i, i ^ steps[i % 2]) for i in range(count)])  23.9 us
    all_gather x1, waiting for transfers between devices, per_device(): rest = lax.all_gather(rest, 'ctx', axis=0, tiled=True)  15.8 us
    pallas_call x4, Pallas kernels, expert_down(): pl.pallas_call(down_kernel, grid=(local,), in_specs=[pl.BlockSpec((1, row...  15.2 us
    unnamed x68, local copies, waits for them, and re-layouts  11.3 us
  transfers between devices with their start and end apart: 52, of which 29 were waited for; matrix products, arithmetic and copies ran while one was open for 3% of the time, Pallas kernels for 21%

profile of v4, /device:TPU:0, one launch (start us, length us, event | category | flops | bytes accessed | tf_op | source)
XLA Modules:
  0.0 334.9 jit_solution(2071214742335802600)
XLA Ops:
  16.0 9.7 %collective-permute-done.refs_4_.refs_13_ = bf16[144,1024]{1,0:T(8,128)(2,1)S(1)} collective-permute-done((bf16[144,1024]{1,0:T(8,128)(2,1)S(1)}, bf16[144,1024]{1,0:T(8,128)(2,1)S(1)}, u32[]{:S(2)}, u32[]{:S(2)}) %collective-permute-start) | collective-permute-done | bytes 294944 | tf_op jit(solution)/shard_map/ppermute | solution.py:366
  25.7 15.1 %collective-permute-done.1.refs_5_.refs_14_ = bf16[144,1024]{1,0:T(8,128)(2,1)S(1)} collective-permute-done((bf16[144,1024]{1,0:T(8,128)(2,1)S(1)}, bf16[144,1024]{1,0:T(8,128)(2,1)S(1)}, u32[]{:S(2)}, u32[]{:S(2)}) %collective-permute-start.1) | collective-permute-done | bytes 294944 | tf_op jit(solution)/shard_map/ppermute | solution.py:366
  40.8 14.1 %collective-permute-start.5 = (bf16[144,1024]{1,0:T(8,128)(2,1)S(1)}, bf16[144,1024]{1,0:T(8,128)(2,1)S(1)}, u32[]{:S(2)}, u32[]{:S(2)}) collective-permute-start(bf16[144,1024]{1,0:T(8,128)(2,1)S(1)} %collective-permute-done.1.refs_5_.refs_14_), channel_id=1, source_target_pairs={{0,1},{1,0},{2,3},{3,2},{4,5},{5,4},{6,7},{7,6},{8,9},{9,8},{10,11... | collective-permute-start | bytes 884744 | tf_op jit(solution)/shard_map/ppermute | solution.py:358
  57.8 5.1 %attention.4 = bf16[128,1024]{1,0:T(8,128)(2,1)S(1)} custom-call(s32[11]{0:T(128)S(1)} %get-tuple-element.107.refs_0_, bf16[128,4096]{1,0:T(8,128)(2,1)} %refs_1_.7, bf16[1024,1024]{1,0:T(8,128)(2,1)} %bitcast.31, bf16[144,1024]{1,0:T(8,128)(2,1)S(1)} %fusion.3.refs_3_.refs_12_, bf16[144,1024]{1,0:T(8,128)(2,1)S(1)} %collective-permute-done.refs_4_.refs_13_, ...), custom_call_target="tpu_custom_call" | custom-call | flops 1073741824 | bytes 1572864 | tf_op jit(solution)/shard_map/attention/pallas_call | solution.py:36
  65.4 5.1 %attention.5 = bf16[128,1024]{1,0:T(8,128)(2,1)S(1)} custom-call(s32[11]{0:T(128)S(1)} %get-tuple-element.106.refs_0_, bf16[128,4096]{1,0:T(8,128)(2,1)} %refs_1_.7, bf16[1024,1024]{1,0:T(8,128)(2,1)} %bitcast.33, bf16[144,1024]{1,0:T(8,128)(2,1)S(1)} %fusion.3.refs_3_.refs_12_, bf16[144,1024]{1,0:T(8,128)(2,1)S(1)} %collective-permute-done.refs_4_.refs_13_, ...), custom_call_target="tpu_custom_call" | custom-call | flops 1073741824 | bytes 1572864 | tf_op jit(solution)/shard_map/attention/pallas_call | solution.py:36
  71.2 5.4 %attention.6 = bf16[128,1024]{1,0:T(8,128)(2,1)S(1)} custom-call(s32[11]{0:T(128)S(1)} %get-tuple-element.105.refs_0_, bf16[128,4096]{1,0:T(8,128)(2,1)} %refs_1_.7, bf16[1024,1024]{1,0:T(8,128)(2,1)} %bitcast.35, bf16[144,1024]{1,0:T(8,128)(2,1)S(1)} %fusion.3.refs_3_.refs_12_, bf16[144,1024]{1,0:T(8,128)(2,1)S(1)} %collective-permute-done.refs_4_.refs_13_, ...), custom_call_target="tpu_custom_call" | custom-call | flops 1073741824 | bytes 1572864 | tf_op jit(solution)/shard_map/attention/pallas_call | solution.py:36
  88.4 3.9 %tables.1 = (bf16[1536,1024]{1,0:T(8,128)(2,1)S(1)}, bf16[1024,1536]{1,0:T(8,128)(2,1)}) custom-call(s32[8]{0:T(128)S(1)} %get-tuple-element.96.order_ref.refs_0_, s32[4,4,1024]{2,1,0:T(4,128)S(1)} %add_select_fusion.place_ref, f32[4,4,1024]{2,1,0:T(4,128)S(1)} %reshape.43.gate_ref), custom_call_target="tpu_custom_call" | custom-call | flops 6291456 | bytes 6291456 | tf_op jit(solution)/shard_map/tables/pallas_call | solution.py:300
  94.0 5.4 %attention.7 = bf16[128,1024]{1,0:T(8,128)(2,1)S(1)} custom-call(s32[11]{0:T(128)S(1)} %add_add_fusion.refs_0_, bf16[128,4096]{1,0:T(8,128)(2,1)} %refs_1_.7, bf16[1024,1024]{1,0:T(8,128)(2,1)} %bitcast.37, bf16[144,1024]{1,0:T(8,128)(2,1)S(1)} %fusion.3.refs_3_.refs_12_, bf16[144,1024]{1,0:T(8,128)(2,1)S(1)} %collective-permute-done.refs_4_.refs_13_, ...), custom_call_target="tpu_custom_call" | custom-call | flops 1073741824 | bytes 1572864 | tf_op jit(solution)/shard_map/attention/pallas_call | solution.py:36
  100.2 6.9 %collective-permute-done.11.refs_4_ = bf16[128,2048]{1,0:T(8,128)(2,1)} collective-permute-done((bf16[128,2048]{1,0:T(8,128)(2,1)}, bf16[128,2048]{1,0:T(8,128)(2,1)}, u32[]{:S(2)}, u32[]{:S(2)}) %collective-permute-start.11) | collective-permute-done | bytes 524320 | tf_op jit(solution)/shard_map/ppermute | solution.py:358
  115.3 5.5 %collective-permute-done.22.refs_3_ = bf16[128,512]{1,0:T(8,128)(2,1)S(1)} collective-permute-done((bf16[128,512]{1,0:T(8,128)(2,1)S(1)}, bf16[128,512]{1,0:T(8,128)(2,1)S(1)}, u32[]{:S(2)}, u32[]{:S(2)}) %collective-permute-start.22) | collective-permute-done | bytes 131104 | tf_op jit(solution)/shard_map/ppermute | solution.py:366
  135.9 15.8 %all-gather.4.cloned.1.call-done.refs_2_ = bf16[1024,1536]{1,0:T(8,128)(2,1)} async-done(((bf16[128,1536]{1,0:T(8,128)(2,1)}), bf16[1024,1536]{1,0:T(8,128)(2,1)}) %all-gather.4.cloned.1.call-update) | async-done | bytes 3145744 | tf_op jit(solution)/shard_map/all_gather | solution.py:460
  161.9 3.8 %pick_rows.4 = (bf16[384,512]{1,0:T(8,128)(2,1)S(1)}, bf16[384,512]{1,0:T(8,128)(2,1)}, bf16[384,512]{1,0:T(8,128)(2,1)}, bf16[384,512]{1,0:T(8,128)(2,1)}) custom-call(s32[8]{0:T(128)S(1)} %get-tuple-element.96.order_ref.refs_0_, bf16[1536,1024]{1,0:T(8,128)(2,1)S(1)} %copy-done.3, bf16[1024,1536]{1,0:T(8,128)(2,1)} %all-gather.4.cloned.1.call-done.refs_2_), custom_call_target="tpu_custom_call" | custom-call | flops 1610612736 | bytes 5767168 | tf_op jit(solution)/shard_map/pick_rows/pallas_call | solution.py:36
  169.6 4.6 %copy-done = bf16[4,2048,768]{2,1,0:T(8,128)(2,1)S(1)} copy-done((bf16[4,2048,768]{2,1,0:T(8,128)(2,1)S(1)}, bf16[4,2048,768]{2,1,0:T(8,128)(2,1)}, u32[]{:S(2)}) %copy-start) | copy-done | bytes 12582936
  174.1 5.0 %expert_hidden.4 = (f32[4,384,768]{2,1,0:T(8,128)S(1)}, f32[4,384,768]{2,1,0:T(8,128)S(1)}) custom-call(bf16[384,512]{1,0:T(8,128)(2,1)S(1)} %copy-done.14, bf16[384,512]{1,0:T(8,128)(2,1)} %collective-permute-done.26.refs_1_, bf16[384,512]{1,0:T(8,128)(2,1)} %collective-permute-done.27.refs_2_, bf16[384,512]{1,0:T(8,128)(2,1)} %collective-permute-done.28.refs_3_, ...), custom_call_target="tpu_custom_call" | custom-call | flops 2415919104 | bytes 18087936 | tf_op jit(solution)/shard_map/expert_hidden/pallas_call | solution.py:36
  185.1 5.3 %expert_hidden.5 = (f32[4,384,768]{2,1,0:T(8,128)S(1)}, f32[4,384,768]{2,1,0:T(8,128)S(1)}) custom-call(bf16[384,512]{1,0:T(8,128)(2,1)S(1)} %get-tuple-element.60.refs_0_, bf16[384,512]{1,0:T(8,128)(2,1)S(1)} %collective-permute-done.19.refs_1_, bf16[384,512]{1,0:T(8,128)(2,1)S(1)} %collective-permute-done.20.refs_2_, ...), custom_call_target="tpu_custom_call" | custom-call | flops 2415919104 | bytes 18087936 | tf_op jit(solution)/shard_map/expert_hidden/pallas_call | solution.py:36
  190.4 6.9 %collective-permute-done.17.refs_2_ = bf16[384,512]{1,0:T(8,128)(2,1)S(1)} collective-permute-done((bf16[384,512]{1,0:T(8,128)(2,1)S(1)}, bf16[384,512]{1,0:T(8,128)(2,1)S(1)}, u32[]{:S(2)}, u32[]{:S(2)}) %collective-permute-start.17) | collective-permute-done | bytes 393248 | tf_op jit(solution)/shard_map/ppermute | solution.py:358
  197.3 6.1 %expert_hidden.6 = (f32[4,384,768]{2,1,0:T(8,128)S(1)}, f32[4,384,768]{2,1,0:T(8,128)S(1)}) custom-call(bf16[384,512]{1,0:T(8,128)(2,1)S(1)} %get-tuple-element.56.refs_0_, bf16[384,512]{1,0:T(8,128)(2,1)S(1)} %copy-done.12, bf16[384,512]{1,0:T(8,128)(2,1)S(1)} %collective-permute-done.17.refs_2_, bf16[384,512]{1,0:T(8,128)(2,1)S(1)} %collective-permute-done.18.refs_3_, ...), custom_call_target="tpu_custom_call" | custom-call | flops 2415919104 | bytes 18087936 | tf_op jit(solution)/shard_map/expert_hidden/pallas_call | solution.py:36
  203.5 9.3 %collective-permute-done.14.refs_2_ = bf16[384,512]{1,0:T(8,128)(2,1)S(1)} collective-permute-done((bf16[384,512]{1,0:T(8,128)(2,1)}, bf16[384,512]{1,0:T(8,128)(2,1)S(1)}, u32[]{:S(2)}, u32[]{:S(2)}) %collective-permute-start.14) | collective-permute-done | bytes 393248 | tf_op jit(solution)/shard_map/ppermute | solution.py:358
  212.9 5.1 %expert_hidden.7.h_ref = bf16[4,384,768]{2,1,0:T(8,128)(2,1)S(1)} custom-call(bf16[384,512]{1,0:T(8,128)(2,1)S(1)} %get-tuple-element.52.refs_6_.refs_8_.refs_0_, bf16[384,512]{1,0:T(8,128)(2,1)S(1)} %collective-permute-done.13.refs_1_, bf16[384,512]{1,0:T(8,128)(2,1)S(1)} %collective-permute-done.14.refs_2_, ...), custom_call_target="tpu_custom_call" | custom-call | flops 2415919104 | bytes 18087936 | tf_op jit(solution)/shard_map/expert_hidden/pallas_call | solution.py:36
  217.9 3.8 %expert_down.5 = (bf16[384,512]{1,0:T(8,128)(2,1)S(1)}, bf16[384,512]{1,0:T(8,128)(2,1)S(1)}, bf16[384,512]{1,0:T(8,128)(2,1)S(1)}, bf16[384,512]{1,0:T(8,128)(2,1)S(1)}) custom-call(bf16[4,384,768]{2,1,0:T(8,128)(2,1)S(1)} %expert_hidden.7.h_ref, bf16[4,768,2048]{2,1,0:T(8,128)(2,1)} %w_ref.7), custom_call_target="tpu_custom_call" | custom-call | flops 1207959552 | bytes 7077888 | tf_op jit(solution)/shard_map/expert_down/pallas_call | solution.py:221
  225.3 3.8 %expert_down.4 = (bf16[384,512]{1,0:T(8,128)(2,1)S(1)}, bf16[384,512]{1,0:T(8,128)(2,1)S(1)}, bf16[384,512]{1,0:T(8,128)(2,1)S(1)}, bf16[384,512]{1,0:T(8,128)(2,1)S(1)}) custom-call(bf16[4,384,768]{2,1,0:T(8,128)(2,1)S(1)} %expert_hidden.7.h_ref, bf16[4,768,2048]{2,1,0:T(8,128)(2,1)} %w_ref.7), custom_call_target="tpu_custom_call" | custom-call | flops 1207959552 | bytes 7077888 | tf_op jit(solution)/shard_map/expert_down/pallas_call | solution.py:221
  235.1 3.8 %expert_down.7 = (bf16[384,512]{1,0:T(8,128)(2,1)S(1)}, bf16[384,512]{1,0:T(8,128)(2,1)S(1)}, bf16[384,512]{1,0:T(8,128)(2,1)S(1)}, bf16[384,512]{1,0:T(8,128)(2,1)S(1)}) custom-call(bf16[4,384,768]{2,1,0:T(8,128)(2,1)S(1)} %expert_hidden.7.h_ref, bf16[4,768,2048]{2,1,0:T(8,128)(2,1)} %w_ref.7), custom_call_target="tpu_custom_call" | custom-call | flops 1207959552 | bytes 7077888 | tf_op jit(solution)/shard_map/expert_down/pallas_call | solution.py:221
  240.4 3.9 %expert_down.6 = (bf16[384,512]{1,0:T(8,128)(2,1)S(1)}, bf16[384,512]{1,0:T(8,128)(2,1)S(1)}, bf16[384,512]{1,0:T(8,128)(2,1)S(1)}, bf16[384,512]{1,0:T(8,128)(2,1)S(1)}) custom-call(bf16[4,384,768]{2,1,0:T(8,128)(2,1)S(1)} %expert_hidden.7.h_ref, bf16[4,768,2048]{2,1,0:T(8,128)(2,1)} %w_ref.7), custom_call_target="tpu_custom_call" | custom-call | flops 1207959552 | bytes 7077888 | tf_op jit(solution)/shard_map/expert_down/pallas_call | solution.py:221
  244.3 4.2 %mix_rows.7 = bf16[1024,512]{1,0:T(8,128)(2,1)S(1)} custom-call(s32[8]{0:T(128)S(1)} %get-tuple-element.96.order_ref.refs_0_, bf16[1024,1536]{1,0:T(8,128)(2,1)} %get-tuple-element.49.refs_24_.refs_1_, bf16[384,512]{1,0:T(8,128)(2,1)S(1)} %get-tuple-element.79.refs_6_.refs_2_, bf16[384,512]{1,0:T(8,128)(2,1)S(1)} %collective-permute-done.32.refs_3_, ...), custom_call_target="tpu_custom_call" | custom-call | flops 1610612736 | bytes 5767168 | tf_op jit(solution)/shard_map/mix_rows/pallas_call | solution.py:36
  250.7 7.0 %collective-permute-done.31.refs_5_ = bf16[384,512]{1,0:T(8,128)(2,1)S(1)} collective-permute-done((bf16[384,512]{1,0:T(8,128)(2,1)S(1)}, bf16[384,512]{1,0:T(8,128)(2,1)S(1)}, u32[]{:S(2)}, u32[]{:S(2)}) %collective-permute-start.31) | collective-permute-done | bytes 393248 | tf_op jit(solution)/shard_map/ppermute | solution.py:358
  257.7 3.7 %mix_rows.6 = bf16[1024,512]{1,0:T(8,128)(2,1)S(1)} custom-call(s32[8]{0:T(128)S(1)} %get-tuple-element.96.order_ref.refs_0_, bf16[1024,1536]{1,0:T(8,128)(2,1)} %get-tuple-element.49.refs_24_.refs_1_, bf16[384,512]{1,0:T(8,128)(2,1)S(1)} %get-tuple-element.75.refs_2_, bf16[384,512]{1,0:T(8,128)(2,1)S(1)} %collective-permute-done.29.refs_3_, ...), custom_call_target="tpu_custom_call" | custom-call | flops 1610612736 | bytes 5767168 | tf_op jit(solution)/shard_map/mix_rows/pallas_call | solution.py:36
  266.8 8.8 %collective-permute-done.35.refs_3_ = bf16[384,512]{1,0:T(8,128)(2,1)S(1)} collective-permute-done((bf16[384,512]{1,0:T(8,128)(2,1)}, bf16[384,512]{1,0:T(8,128)(2,1)S(1)}, u32[]{:S(2)}, u32[]{:S(2)}) %collective-permute-start.35) | collective-permute-done | bytes 393248 | tf_op jit(solution)/shard_map/ppermute | solution.py:358
  275.7 5.2 %collective-permute-done.37.refs_5_ = bf16[384,512]{1,0:T(8,128)(2,1)S(1)} collective-permute-done((bf16[384,512]{1,0:T(8,128)(2,1)}, bf16[384,512]{1,0:T(8,128)(2,1)S(1)}, u32[]{:S(2)}, u32[]{:S(2)}) %collective-permute-start.37) | collective-permute-done | bytes 393248 | tf_op jit(solution)/shard_map/ppermute | solution.py:358
  292.4 4.2 %collective-permute-done.41 = bf16[128,512]{1,0:T(8,128)(2,1)S(1)} collective-permute-done((bf16[128,512]{1,0:T(8,128)(2,1)S(1)}, bf16[128,512]{1,0:T(8,128)(2,1)S(1)}, u32[]{:S(2)}, u32[]{:S(2)}) %collective-permute-start.41) | collective-permute-done | bytes 131104 | tf_op jit(solution)/shard_map/ppermute | solution.py:366
  296.7 6.2 %collective-permute-start.39 = (bf16[128,512]{1,0:T(8,128)(2,1)S(1)}, bf16[128,512]{1,0:T(8,128)(2,1)S(1)}, u32[]{:S(2)}, u32[]{:S(2)}) collective-permute-start(bf16[128,512]{1,0:T(8,128)(2,1)S(1)} %get-tuple-element.100), channel_id=1, source_target_pairs={{0,2},{1,7},{2,0},{3,5},{4,6},{5,3},{6,4},{7,1},{8,10},{9,15},{10,... | collective-permute-start | bytes 393224 | tf_op jit(solution)/shard_map/ppermute | solution.py:366
  315.0 3.7 %collective-permute-done.48 = bf16[128,512]{1,0:T(8,128)(2,1)S(1)} collective-permute-done((bf16[128,512]{1,0:T(8,128)(2,1)S(1)}, bf16[128,512]{1,0:T(8,128)(2,1)S(1)}, u32[]{:S(2)}, u32[]{:S(2)}) %collective-permute-start.48) | collective-permute-done | bytes 131104 | tf_op jit(solution)/shard_map/ppermute | solution.py:366
  318.7 7.5 %collective-permute-done.47 = bf16[128,512]{1,0:T(8,128)(2,1)S(1)} collective-permute-done((bf16[128,512]{1,0:T(8,128)(2,1)S(1)}, bf16[128,512]{1,0:T(8,128)(2,1)S(1)}, u32[]{:S(2)}, u32[]{:S(2)}) %collective-permute-start.47) | collective-permute-done | bytes 131104 | tf_op jit(solution)/shard_map/ppermute | solution.py:366
  (209 shorter events, 117.2 us)
Async XLA Ops:
  6.5 51.3 %all-gather.6.cloned.1.call-start = ((), (), s32[]{:S(2)}) async-start(), calls=%async_computation.3 | async-start | bytes 2359296 | tf_op jit(solution)/shard_map/all_gather | solution.py:407
  8.3 143.4 %all-gather.4.cloned.1.call-start = ((), (), s32[]{:S(2)}) async-start(), calls=%async_computation.1 | async-start | bytes 3538944 | tf_op jit(solution)/shard_map/all_gather | solution.py:460
  9.8 15.9 %collective-permute-start = (bf16[144,1024]{1,0:T(8,128)(2,1)S(1)}, bf16[144,1024]{1,0:T(8,128)(2,1)S(1)}, u32[]{:S(2)}, u32[]{:S(2)}) collective-permute-start(bf16[144,1024]{1,0:T(8,128)(2,1)S(1)} %fusion.3.refs_3_.refs_12_), channel_id=1, source_target_pairs={{0,2},{1,7},{2,0},{3,5},{4,6},{5,3},{6,4},{7,1},{8,10},{9,15},{10,... | collective-permute-start | bytes 884744 | tf_op jit(solution)/shard_map/ppermute | solution.py:366
  12.9 27.9 %collective-permute-start.1 = (bf16[144,1024]{1,0:T(8,128)(2,1)S(1)}, bf16[144,1024]{1,0:T(8,128)(2,1)S(1)}, u32[]{:S(2)}, u32[]{:S(2)}) collective-permute-start(bf16[144,1024]{1,0:T(8,128)(2,1)S(1)} %fusion.3.refs_3_.refs_12_), channel_id=1, source_target_pairs={{0,4},{1,5},{2,6},{3,7},{4,0},{5,1},{6,2},{7,3},{8,12},{9,13},{10,... | collective-permute-start | bytes 884744 | tf_op jit(solution)/shard_map/ppermute | solution.py:366
  15.5 39.5 %collective-permute-start.2 = (bf16[144,1024]{1,0:T(8,128)(2,1)S(1)}, bf16[144,1024]{1,0:T(8,128)(2,1)S(1)}, u32[]{:S(2)}, u32[]{:S(2)}) collective-permute-start(bf16[144,1024]{1,0:T(8,128)(2,1)S(1)} %fusion.3.refs_3_.refs_12_), channel_id=1, source_target_pairs={{0,6},{1,3},{2,4},{3,1},{4,2},{5,7},{6,0},{7,5},{8,14},{9,11},{10,... | collective-permute-start | bytes 884744 | tf_op jit(solution)/shard_map/ppermute | solution.py:366
  15.5 39.6 %collective-permute-start.3 = (bf16[144,1024]{1,0:T(8,128)(2,1)S(1)}, bf16[144,1024]{1,0:T(8,128)(2,1)S(1)}, u32[]{:S(2)}, u32[]{:S(2)}) collective-permute-start(bf16[144,1024]{1,0:T(8,128)(2,1)S(1)} %fusion.3.refs_3_.refs_12_), channel_id=1, source_target_pairs={{0,1},{1,0},{2,3},{3,2},{4,5},{5,4},{6,7},{7,6},{8,9},{9,8},{10,11... | collective-permute-start | bytes 884744 | tf_op jit(solution)/shard_map/ppermute | solution.py:358
  25.7 29.3 %collective-permute-start.4 = (bf16[144,1024]{1,0:T(8,128)(2,1)S(1)}, bf16[144,1024]{1,0:T(8,128)(2,1)S(1)}, u32[]{:S(2)}, u32[]{:S(2)}) collective-permute-start(bf16[144,1024]{1,0:T(8,128)(2,1)S(1)} %collective-permute-done.refs_4_.refs_13_), channel_id=1, source_target_pairs={{0,1},{1,0},{2,3},{3,2},{4,5},{5,4},{6,7},{7,6},{8,9},{9,8},{10,11... | collective-permute-start | bytes 884744 | tf_op jit(solution)/shard_map/ppermute | solution.py:358
  40.8 15.3 %collective-permute-start.5 = (bf16[144,1024]{1,0:T(8,128)(2,1)S(1)}, bf16[144,1024]{1,0:T(8,128)(2,1)S(1)}, u32[]{:S(2)}, u32[]{:S(2)}) collective-permute-start(bf16[144,1024]{1,0:T(8,128)(2,1)S(1)} %collective-permute-done.1.refs_5_.refs_14_), channel_id=1, source_target_pairs={{0,1},{1,0},{2,3},{3,2},{4,5},{5,4},{6,7},{7,6},{8,9},{9,8},{10,11... | collective-permute-start | bytes 884744 | tf_op jit(solution)/shard_map/ppermute | solution.py:358
  78.9 21.3 %collective-permute-start.10 = (bf16[128,2048]{1,0:T(8,128)(2,1)}, bf16[128,2048]{1,0:T(8,128)(2,1)}, u32[]{:S(2)}, u32[]{:S(2)}) collective-permute-start(bf16[128,2048]{1,0:T(8,128)(2,1)} %convolution_convert_fusion.2.refs_20_), channel_id=1, source_target_pairs={{0,24},{8,16},{16,8},{24,0},{1,25},{9,17},{17,9},{25,1},{2,26},{10... | collective-permute-start | bytes 1572872 | tf_op jit(solution)/shard_map/ppermute | solution.py:358
  82.8 24.3 %collective-permute-start.11 = (bf16[128,2048]{1,0:T(8,128)(2,1)}, bf16[128,2048]{1,0:T(8,128)(2,1)}, u32[]{:S(2)}, u32[]{:S(2)}) collective-permute-start(bf16[128,2048]{1,0:T(8,128)(2,1)} %convolution_convert_fusion.1.refs_21_), channel_id=1, source_target_pairs={{0,16},{8,24},{16,0},{24,8},{1,17},{9,25},{17,1},{25,9},{2,18},{10... | collective-permute-start | bytes 1572872 | tf_op jit(solution)/shard_map/ppermute | solution.py:358
  87.5 19.8 %collective-permute-start.12 = (bf16[128,2048]{1,0:T(8,128)(2,1)}, bf16[128,2048]{1,0:T(8,128)(2,1)}, u32[]{:S(2)}, u32[]{:S(2)}) collective-permute-start(bf16[128,2048]{1,0:T(8,128)(2,1)} %convolution_convert_fusion.refs_22_), channel_id=1, source_target_pairs={{0,8},{8,0},{16,24},{24,16},{1,9},{9,1},{17,25},{25,17},{2,10},{10... | collective-permute-start | bytes 1572872 | tf_op jit(solution)/shard_map/ppermute | solution.py:358
  110.8 215.6 %reduce-scatter.2.cloned.1.call-start = ((), (), s32[]{:S(2)}) async-start(), calls=%async_computation.2 | async-start | bytes 2359296 | tf_op jit(solution)/shard_map/reduce_scatter | solution.py:488
  132.4 27.6 %collective-permute-start.26 = (bf16[384,512]{1,0:T(8,128)(2,1)}, bf16[384,512]{1,0:T(8,128)(2,1)}, u32[]{:S(2)}, u32[]{:S(2)}) collective-permute-start(bf16[384,512]{1,0:T(8,128)(2,1)} %get-tuple-element.66), channel_id=1, source_target_pairs={{0,8},{8,0},{16,24},{24,16},{1,9},{9,1},{17,25},{25,17},{2,10},{10... | collective-permute-start | bytes 1179656 | tf_op jit(solution)/shard_map/ppermute | solution.py:358
  132.4 29.0 %collective-permute-start.27 = (bf16[384,512]{1,0:T(8,128)(2,1)}, bf16[384,512]{1,0:T(8,128)(2,1)}, u32[]{:S(2)}, u32[]{:S(2)}) collective-permute-start(bf16[384,512]{1,0:T(8,128)(2,1)} %get-tuple-element.67), channel_id=1, source_target_pairs={{0,16},{8,24},{16,0},{24,8},{1,17},{9,25},{17,1},{25,9},{2,18},{10... | collective-permute-start | bytes 1179656 | tf_op jit(solution)/shard_map/ppermute | solution.py:358
  133.8 32.0 %collective-permute-start.28 = (bf16[384,512]{1,0:T(8,128)(2,1)}, bf16[384,512]{1,0:T(8,128)(2,1)}, u32[]{:S(2)}, u32[]{:S(2)}) collective-permute-start(bf16[384,512]{1,0:T(8,128)(2,1)} %get-tuple-element.68), channel_id=1, source_target_pairs={{0,24},{8,16},{16,8},{24,0},{1,25},{9,17},{17,9},{25,1},{2,26},{10... | collective-permute-start | bytes 1179656 | tf_op jit(solution)/shard_map/ppermute | solution.py:358
  158.4 20.8 %collective-permute-start.19 = (bf16[384,512]{1,0:T(8,128)(2,1)S(1)}, bf16[384,512]{1,0:T(8,128)(2,1)S(1)}, u32[]{:S(2)}, u32[]{:S(2)}) collective-permute-start(bf16[384,512]{1,0:T(8,128)(2,1)S(1)} %get-tuple-element.61), channel_id=1, source_target_pairs={{0,8},{8,0},{16,24},{24,16},{1,9},{9,1},{17,25},{25,17},{2,10},{10... | collective-permute-start | bytes 1179656 | tf_op jit(solution)/shard_map/ppermute | solution.py:358
  160.0 20.0 %collective-permute-start.20 = (bf16[384,512]{1,0:T(8,128)(2,1)S(1)}, bf16[384,512]{1,0:T(8,128)(2,1)S(1)}, u32[]{:S(2)}, u32[]{:S(2)}) collective-permute-start(bf16[384,512]{1,0:T(8,128)(2,1)S(1)} %get-tuple-element.62), channel_id=1, source_target_pairs={{0,16},{8,24},{16,0},{24,8},{1,17},{9,25},{17,1},{25,9},{2,18},{10... | collective-permute-start | bytes 1179656 | tf_op jit(solution)/shard_map/ppermute | solution.py:358
  161.4 23.2 %collective-permute-start.21 = (bf16[384,512]{1,0:T(8,128)(2,1)S(1)}, bf16[384,512]{1,0:T(8,128)(2,1)S(1)}, u32[]{:S(2)}, u32[]{:S(2)}) collective-permute-start(bf16[384,512]{1,0:T(8,128)(2,1)S(1)} %get-tuple-element.63), channel_id=1, source_target_pairs={{0,24},{8,16},{16,8},{24,0},{1,25},{9,17},{17,9},{25,1},{2,26},{10... | collective-permute-start | bytes 1179656 | tf_op jit(solution)/shard_map/ppermute | solution.py:358
  165.8 31.5 %collective-permute-start.17 = (bf16[384,512]{1,0:T(8,128)(2,1)S(1)}, bf16[384,512]{1,0:T(8,128)(2,1)S(1)}, u32[]{:S(2)}, u32[]{:S(2)}) collective-permute-start(bf16[384,512]{1,0:T(8,128)(2,1)S(1)} %get-tuple-element.58), channel_id=1, source_target_pairs={{0,16},{8,24},{16,0},{24,8},{1,17},{9,25},{17,1},{25,9},{2,18},{10... | collective-permute-start | bytes 1179656 | tf_op jit(solution)/shard_map/ppermute | solution.py:358
  167.9 29.4 %collective-permute-start.18 = (bf16[384,512]{1,0:T(8,128)(2,1)S(1)}, bf16[384,512]{1,0:T(8,128)(2,1)S(1)}, u32[]{:S(2)}, u32[]{:S(2)}) collective-permute-start(bf16[384,512]{1,0:T(8,128)(2,1)S(1)} %get-tuple-element.59), channel_id=1, source_target_pairs={{0,24},{8,16},{16,8},{24,0},{1,25},{9,17},{17,9},{25,1},{2,26},{10... | collective-permute-start | bytes 1179656 | tf_op jit(solution)/shard_map/ppermute | solution.py:358
  179.2 24.3 %collective-permute-start.13 = (bf16[384,512]{1,0:T(8,128)(2,1)}, bf16[384,512]{1,0:T(8,128)(2,1)S(1)}, u32[]{:S(2)}, u32[]{:S(2)}) collective-permute-start(bf16[384,512]{1,0:T(8,128)(2,1)} %get-tuple-element.53), channel_id=1, source_target_pairs={{0,8},{8,0},{16,24},{24,16},{1,9},{9,1},{17,25},{25,17},{2,10},{10... | collective-permute-start | bytes 1179656 | tf_op jit(solution)/shard_map/ppermute | solution.py:358
  180.0 32.8 %collective-permute-start.14 = (bf16[384,512]{1,0:T(8,128)(2,1)}, bf16[384,512]{1,0:T(8,128)(2,1)S(1)}, u32[]{:S(2)}, u32[]{:S(2)}) collective-permute-start(bf16[384,512]{1,0:T(8,128)(2,1)} %get-tuple-element.54), channel_id=1, source_target_pairs={{0,16},{8,24},{16,0},{24,8},{1,17},{9,25},{17,1},{25,9},{2,18},{10... | collective-permute-start | bytes 1179656 | tf_op jit(solution)/shard_map/ppermute | solution.py:358
  184.6 28.3 %collective-permute-start.15 = (bf16[384,512]{1,0:T(8,128)(2,1)}, bf16[384,512]{1,0:T(8,128)(2,1)S(1)}, u32[]{:S(2)}, u32[]{:S(2)}) collective-permute-start(bf16[384,512]{1,0:T(8,128)(2,1)} %get-tuple-element.55), channel_id=1, source_target_pairs={{0,24},{8,16},{16,8},{24,0},{1,25},{9,17},{17,9},{25,1},{2,26},{10... | collective-permute-start | bytes 1179656 | tf_op jit(solution)/shard_map/ppermute | solution.py:358
  222.2 22.1 %collective-permute-start.33 = (bf16[384,512]{1,0:T(8,128)(2,1)S(1)}, bf16[384,512]{1,0:T(8,128)(2,1)S(1)}, u32[]{:S(2)}, u32[]{:S(2)}) collective-permute-start(bf16[384,512]{1,0:T(8,128)(2,1)S(1)} %get-tuple-element.83), channel_id=1, source_target_pairs={{0,16},{8,24},{16,0},{24,8},{1,17},{9,25},{17,1},{25,9},{2,18},{10... | collective-permute-start | bytes 1179656 | tf_op jit(solution)/shard_map/ppermute | solution.py:358
  223.6 20.7 %collective-permute-start.34 = (bf16[384,512]{1,0:T(8,128)(2,1)S(1)}, bf16[384,512]{1,0:T(8,128)(2,1)S(1)}, u32[]{:S(2)}, u32[]{:S(2)}) collective-permute-start(bf16[384,512]{1,0:T(8,128)(2,1)S(1)} %get-tuple-element.84), channel_id=1, source_target_pairs={{0,24},{8,16},{16,8},{24,0},{1,25},{9,17},{17,9},{25,1},{2,26},{10... | collective-permute-start | bytes 1179656 | tf_op jit(solution)/shard_map/ppermute | solution.py:358
  229.0 21.7 %collective-permute-start.29 = (bf16[384,512]{1,0:T(8,128)(2,1)S(1)}, bf16[384,512]{1,0:T(8,128)(2,1)S(1)}, u32[]{:S(2)}, u32[]{:S(2)}) collective-permute-start(bf16[384,512]{1,0:T(8,128)(2,1)S(1)} %get-tuple-element.76), channel_id=1, source_target_pairs={{0,8},{8,0},{16,24},{24,16},{1,9},{9,1},{17,25},{25,17},{2,10},{10... | collective-permute-start | bytes 1179656 | tf_op jit(solution)/shard_map/ppermute | solution.py:358
  229.6 21.2 %collective-permute-start.30 = (bf16[384,512]{1,0:T(8,128)(2,1)S(1)}, bf16[384,512]{1,0:T(8,128)(2,1)S(1)}, u32[]{:S(2)}, u32[]{:S(2)}) collective-permute-start(bf16[384,512]{1,0:T(8,128)(2,1)S(1)} %get-tuple-element.77), channel_id=1, source_target_pairs={{0,16},{8,24},{16,0},{24,8},{1,17},{9,25},{17,1},{25,9},{2,18},{10... | collective-permute-start | bytes 1179656 | tf_op jit(solution)/shard_map/ppermute | solution.py:358
  233.8 23.9 %collective-permute-start.31 = (bf16[384,512]{1,0:T(8,128)(2,1)S(1)}, bf16[384,512]{1,0:T(8,128)(2,1)S(1)}, u32[]{:S(2)}, u32[]{:S(2)}) collective-permute-start(bf16[384,512]{1,0:T(8,128)(2,1)S(1)} %get-tuple-element.78), channel_id=1, source_target_pairs={{0,24},{8,16},{16,8},{24,0},{1,25},{9,17},{17,9},{25,1},{2,26},{10... | collective-permute-start | bytes 1179656 | tf_op jit(solution)/shard_map/ppermute | solution.py:358
  265.5 15.4 %collective-permute-start.37 = (bf16[384,512]{1,0:T(8,128)(2,1)}, bf16[384,512]{1,0:T(8,128)(2,1)S(1)}, u32[]{:S(2)}, u32[]{:S(2)}) collective-permute-start(bf16[384,512]{1,0:T(8,128)(2,1)} %copy-done.22), channel_id=1, source_target_pairs={{0,24},{8,16},{16,8},{24,0},{1,25},{9,17},{17,9},{25,1},{2,26},{10... | collective-permute-start | bytes 1179656 | tf_op jit(solution)/shard_map/ppermute | solution.py:358
  288.4 18.0 %collective-permute-start.42 = (bf16[384,512]{1,0:T(8,128)(2,1)S(1)}, bf16[384,512]{1,0:T(8,128)(2,1)S(1)}, u32[]{:S(2)}, u32[]{:S(2)}) collective-permute-start(bf16[384,512]{1,0:T(8,128)(2,1)S(1)} %copy-done.21), channel_id=1, source_target_pairs={{0,8},{8,0},{16,24},{24,16},{1,9},{9,1},{17,25},{25,17},{2,10},{10... | collective-permute-start | bytes 1179656 | tf_op jit(solution)/shard_map/ppermute | solution.py:358
  289.8 17.0 %collective-permute-start.43 = (bf16[384,512]{1,0:T(8,128)(2,1)S(1)}, bf16[384,512]{1,0:T(8,128)(2,1)S(1)}, u32[]{:S(2)}, u32[]{:S(2)}) collective-permute-start(bf16[384,512]{1,0:T(8,128)(2,1)S(1)} %copy-done.19), channel_id=1, source_target_pairs={{0,16},{8,24},{16,0},{24,8},{1,17},{9,25},{17,1},{25,9},{2,18},{10... | collective-permute-start | bytes 1179656 | tf_op jit(solution)/shard_map/ppermute | solution.py:358
  290.5 16.3 %collective-permute-start.44 = (bf16[384,512]{1,0:T(8,128)(2,1)S(1)}, bf16[384,512]{1,0:T(8,128)(2,1)S(1)}, u32[]{:S(2)}, u32[]{:S(2)}) collective-permute-start(bf16[384,512]{1,0:T(8,128)(2,1)S(1)} %copy-done.17), channel_id=1, source_target_pairs={{0,24},{8,16},{16,8},{24,0},{1,25},{9,17},{17,9},{25,1},{2,26},{10... | collective-permute-start | bytes 1179656 | tf_op jit(solution)/shard_map/ppermute | solution.py:358
  (51 other events, 501.7 us)
Sparse Core Ops, SparseCore 0:
  9.0 48.7 all-gather.5
  110.9 40.7 all-gather.3
  263.3 37.6 reduce-scatter.1

commit v5 on v4

--- a/solution.py
+++ b/solution.py
@@ -271,7 +271,7 @@
             transcendentals=0,
         ),
         name="mix_rows",
-        vmem=48 * 1024 * 1024,
+        vmem=24 * 1024 * 1024,
     )
 
 

time: 336 us -> 335 us (level)
  local copies, waits for them, and re-layouts: 13.4 us -> 18.1 us
    unnamed x68 -> x72, local copies, waits for them, and re-layouts: 11.3 us -> 16 us
  transfers between devices with their start and end apart: 52 -> 52, of which waited for: 29 -> 27; matrix products, arithmetic and copies ran while one was open for 3% -> 3% of each run, Pallas kernels for 21% -> 21%
where the time goes in v5:
time: 335 us; the launch traced here: 334 us
  waiting for transfers between devices  126 us (38%)
  Pallas kernels  88.8 us (27%)
  starting transfers between devices  75.2 us (22%)
  local copies, waits for them, and re-layouts  18.1 us (5%)
  between operations  13.7 us (4%)
  other arithmetic  6.6 us (2%)
  matrix products  5.45 us (2%)
    pallas_call x19, Pallas kernels, call(): pl.pallas_call(run, compiler_params=params, **kwargs)(*operands, *deps)  69.1 us
    ppermute x37, waiting for transfers between devices, exchange(): lax.ppermute(value, axis, [(i, i ^ k) for i in range(lax.axis_size(axis))])  57.3 us
    ppermute x12, waiting for transfers between devices, chip_exchange(): lax.ppermute(value, 'ctx', [(i, i ^ steps[i % 2]) for i in range(count)])  52.4 us
    ppermute x37, starting transfers between devices, exchange(): lax.ppermute(value, axis, [(i, i ^ k) for i in range(lax.axis_size(axis))])  50.9 us
    ppermute x12, starting transfers between devices, chip_exchange(): lax.ppermute(value, 'ctx', [(i, i ^ steps[i % 2]) for i in range(count)])  24.2 us
    unnamed x72, local copies, waits for them, and re-layouts  16 us
    pallas_call x4, Pallas kernels, expert_down(): pl.pallas_call(down_kernel, grid=(local,), in_specs=[pl.BlockSpec((1, row...  15.8 us
    all_gather x1, waiting for transfers between devices, per_device(): rest = lax.all_gather(rest, 'ctx', axis=0, tiled=True)  15.8 us
  transfers between devices with their start and end apart: 52, of which 27 were waited for; matrix products, arithmetic and copies ran while one was open for 3% of the time, Pallas kernels for 21%

profile of v5, /device:TPU:0, one launch (start us, length us, event | category | flops | bytes accessed | tf_op | source)
XLA Modules:
  0.0 334.1 jit_solution(5669472900980446752)
XLA Ops:
  16.0 9.7 %collective-permute-done.refs_4_.refs_13_ = bf16[144,1024]{1,0:T(8,128)(2,1)S(1)} collective-permute-done((bf16[144,1024]{1,0:T(8,128)(2,1)S(1)}, bf16[144,1024]{1,0:T(8,128)(2,1)S(1)}, u32[]{:S(2)}, u32[]{:S(2)}) %collective-permute-start) | collective-permute-done | bytes 294944 | tf_op jit(solution)/shard_map/ppermute | solution.py:366
  25.7 15.1 %collective-permute-done.1.refs_5_.refs_14_ = bf16[144,1024]{1,0:T(8,128)(2,1)S(1)} collective-permute-done((bf16[144,1024]{1,0:T(8,128)(2,1)S(1)}, bf16[144,1024]{1,0:T(8,128)(2,1)S(1)}, u32[]{:S(2)}, u32[]{:S(2)}) %collective-permute-start.1) | collective-permute-done | bytes 294944 | tf_op jit(solution)/shard_map/ppermute | solution.py:366
  40.8 14.1 %collective-permute-start.5 = (bf16[144,1024]{1,0:T(8,128)(2,1)S(1)}, bf16[144,1024]{1,0:T(8,128)(2,1)S(1)}, u32[]{:S(2)}, u32[]{:S(2)}) collective-permute-start(bf16[144,1024]{1,0:T(8,128)(2,1)S(1)} %collective-permute-done.1.refs_5_.refs_14_), channel_id=1, source_target_pairs={{0,1},{1,0},{2,3},{3,2},{4,5},{5,4},{6,7},{7,6},{8,9},{9,8},{10,11... | collective-permute-start | bytes 884744 | tf_op jit(solution)/shard_map/ppermute | solution.py:358
  57.8 5.1 %attention.4 = bf16[128,1024]{1,0:T(8,128)(2,1)S(1)} custom-call(s32[11]{0:T(128)S(1)} %get-tuple-element.107.refs_0_, bf16[128,4096]{1,0:T(8,128)(2,1)} %refs_1_.7, bf16[1024,1024]{1,0:T(8,128)(2,1)} %bitcast.31, bf16[144,1024]{1,0:T(8,128)(2,1)S(1)} %fusion.3.refs_3_.refs_12_, bf16[144,1024]{1,0:T(8,128)(2,1)S(1)} %collective-permute-done.refs_4_.refs_13_, ...), custom_call_target="tpu_custom_call" | custom-call | flops 1073741824 | bytes 1572864 | tf_op jit(solution)/shard_map/attention/pallas_call | solution.py:36
  65.4 5.1 %attention.5 = bf16[128,1024]{1,0:T(8,128)(2,1)S(1)} custom-call(s32[11]{0:T(128)S(1)} %get-tuple-element.106.refs_0_, bf16[128,4096]{1,0:T(8,128)(2,1)} %refs_1_.7, bf16[1024,1024]{1,0:T(8,128)(2,1)} %bitcast.33, bf16[144,1024]{1,0:T(8,128)(2,1)S(1)} %fusion.3.refs_3_.refs_12_, bf16[144,1024]{1,0:T(8,128)(2,1)S(1)} %collective-permute-done.refs_4_.refs_13_, ...), custom_call_target="tpu_custom_call" | custom-call | flops 1073741824 | bytes 1572864 | tf_op jit(solution)/shard_map/attention/pallas_call | solution.py:36
  71.2 5.4 %attention.6 = bf16[128,1024]{1,0:T(8,128)(2,1)S(1)} custom-call(s32[11]{0:T(128)S(1)} %get-tuple-element.105.refs_0_, bf16[128,4096]{1,0:T(8,128)(2,1)} %refs_1_.7, bf16[1024,1024]{1,0:T(8,128)(2,1)} %bitcast.35, bf16[144,1024]{1,0:T(8,128)(2,1)S(1)} %fusion.3.refs_3_.refs_12_, bf16[144,1024]{1,0:T(8,128)(2,1)S(1)} %collective-permute-done.refs_4_.refs_13_, ...), custom_call_target="tpu_custom_call" | custom-call | flops 1073741824 | bytes 1572864 | tf_op jit(solution)/shard_map/attention/pallas_call | solution.py:36
  88.4 3.9 %tables.1 = (bf16[1536,1024]{1,0:T(8,128)(2,1)S(1)}, bf16[1024,1536]{1,0:T(8,128)(2,1)}) custom-call(s32[8]{0:T(128)S(1)} %get-tuple-element.96.order_ref.refs_0_, s32[4,4,1024]{2,1,0:T(4,128)S(1)} %add_select_fusion.place_ref, f32[4,4,1024]{2,1,0:T(4,128)S(1)} %reshape.43.gate_ref), custom_call_target="tpu_custom_call" | custom-call | flops 6291456 | bytes 6291456 | tf_op jit(solution)/shard_map/tables/pallas_call | solution.py:300
  94.0 5.4 %attention.7 = bf16[128,1024]{1,0:T(8,128)(2,1)S(1)} custom-call(s32[11]{0:T(128)S(1)} %add_add_fusion.refs_0_, bf16[128,4096]{1,0:T(8,128)(2,1)} %refs_1_.7, bf16[1024,1024]{1,0:T(8,128)(2,1)} %bitcast.37, bf16[144,1024]{1,0:T(8,128)(2,1)S(1)} %fusion.3.refs_3_.refs_12_, bf16[144,1024]{1,0:T(8,128)(2,1)S(1)} %collective-permute-done.refs_4_.refs_13_, ...), custom_call_target="tpu_custom_call" | custom-call | flops 1073741824 | bytes 1572864 | tf_op jit(solution)/shard_map/attention/pallas_call | solution.py:36
  100.2 6.9 %collective-permute-done.11.refs_4_ = bf16[128,2048]{1,0:T(8,128)(2,1)} collective-permute-done((bf16[128,2048]{1,0:T(8,128)(2,1)}, bf16[128,2048]{1,0:T(8,128)(2,1)}, u32[]{:S(2)}, u32[]{:S(2)}) %collective-permute-start.11) | collective-permute-done | bytes 524320 | tf_op jit(solution)/shard_map/ppermute | solution.py:358
  115.3 5.5 %collective-permute-done.22.refs_3_ = bf16[128,512]{1,0:T(8,128)(2,1)S(1)} collective-permute-done((bf16[128,512]{1,0:T(8,128)(2,1)S(1)}, bf16[128,512]{1,0:T(8,128)(2,1)S(1)}, u32[]{:S(2)}, u32[]{:S(2)}) %collective-permute-start.22) | collective-permute-done | bytes 131104 | tf_op jit(solution)/shard_map/ppermute | solution.py:366
  120.7 3.6 %collective-permute-done.23.refs_4_ = bf16[128,512]{1,0:T(8,128)(2,1)S(1)} collective-permute-done((bf16[128,512]{1,0:T(8,128)(2,1)S(1)}, bf16[128,512]{1,0:T(8,128)(2,1)S(1)}, u32[]{:S(2)}, u32[]{:S(2)}) %collective-permute-start.23) | collective-permute-done | bytes 131104 | tf_op jit(solution)/shard_map/ppermute | solution.py:366
  135.9 15.8 %all-gather.4.cloned.1.call-done.refs_2_ = bf16[1024,1536]{1,0:T(8,128)(2,1)} async-done(((bf16[128,1536]{1,0:T(8,128)(2,1)}), bf16[1024,1536]{1,0:T(8,128)(2,1)}) %all-gather.4.cloned.1.call-update) | async-done | bytes 3145744 | tf_op jit(solution)/shard_map/all_gather | solution.py:460
  161.9 3.8 %pick_rows.4 = (bf16[384,512]{1,0:T(8,128)(2,1)S(1)}, bf16[384,512]{1,0:T(8,128)(2,1)}, bf16[384,512]{1,0:T(8,128)(2,1)}, bf16[384,512]{1,0:T(8,128)(2,1)}) custom-call(s32[8]{0:T(128)S(1)} %get-tuple-element.96.order_ref.refs_0_, bf16[1536,1024]{1,0:T(8,128)(2,1)S(1)} %copy-done.5, bf16[1024,1536]{1,0:T(8,128)(2,1)} %all-gather.4.cloned.1.call-done.refs_2_), custom_call_target="tpu_custom_call" | custom-call | flops 1610612736 | bytes 5767168 | tf_op jit(solution)/shard_map/pick_rows/pallas_call | solution.py:36
  169.5 4.6 %copy-done = bf16[4,2048,768]{2,1,0:T(8,128)(2,1)S(1)} copy-done((bf16[4,2048,768]{2,1,0:T(8,128)(2,1)S(1)}, bf16[4,2048,768]{2,1,0:T(8,128)(2,1)}, u32[]{:S(2)}) %copy-start) | copy-done | bytes 12582936
  174.1 5.0 %expert_hidden.4 = (f32[4,384,768]{2,1,0:T(8,128)S(1)}, f32[4,384,768]{2,1,0:T(8,128)S(1)}) custom-call(bf16[384,512]{1,0:T(8,128)(2,1)S(1)} %copy-done.16, bf16[384,512]{1,0:T(8,128)(2,1)} %collective-permute-done.26.refs_1_, bf16[384,512]{1,0:T(8,128)(2,1)} %collective-permute-done.27.refs_2_, bf16[384,512]{1,0:T(8,128)(2,1)} %collective-permute-done.28.refs_3_, ...), custom_call_target="tpu_custom_call" | custom-call | flops 2415919104 | bytes 18087936 | tf_op jit(solution)/shard_map/expert_hidden/pallas_call | solution.py:36
  181.0 3.6 %collective-permute-done.21.refs_3_ = bf16[384,512]{1,0:T(8,128)(2,1)S(1)} collective-permute-done((bf16[384,512]{1,0:T(8,128)(2,1)S(1)}, bf16[384,512]{1,0:T(8,128)(2,1)S(1)}, u32[]{:S(2)}, u32[]{:S(2)}) %collective-permute-start.21) | collective-permute-done | bytes 393248 | tf_op jit(solution)/shard_map/ppermute | solution.py:358
  185.1 5.3 %expert_hidden.5 = (f32[4,384,768]{2,1,0:T(8,128)S(1)}, f32[4,384,768]{2,1,0:T(8,128)S(1)}) custom-call(bf16[384,512]{1,0:T(8,128)(2,1)S(1)} %get-tuple-element.60.refs_0_, bf16[384,512]{1,0:T(8,128)(2,1)S(1)} %collective-permute-done.19.refs_1_, bf16[384,512]{1,0:T(8,128)(2,1)S(1)} %collective-permute-done.20.refs_2_, ...), custom_call_target="tpu_custom_call" | custom-call | flops 2415919104 | bytes 18087936 | tf_op jit(solution)/shard_map/expert_hidden/pallas_call | solution.py:36
  190.4 6.9 %collective-permute-done.17.refs_2_ = bf16[384,512]{1,0:T(8,128)(2,1)S(1)} collective-permute-done((bf16[384,512]{1,0:T(8,128)(2,1)S(1)}, bf16[384,512]{1,0:T(8,128)(2,1)S(1)}, u32[]{:S(2)}, u32[]{:S(2)}) %collective-permute-start.17) | collective-permute-done | bytes 393248 | tf_op jit(solution)/shard_map/ppermute | solution.py:358
  197.3 6.1 %expert_hidden.6 = (f32[4,384,768]{2,1,0:T(8,128)S(1)}, f32[4,384,768]{2,1,0:T(8,128)S(1)}) custom-call(bf16[384,512]{1,0:T(8,128)(2,1)S(1)} %get-tuple-element.56.refs_0_, bf16[384,512]{1,0:T(8,128)(2,1)S(1)} %copy-done.14, bf16[384,512]{1,0:T(8,128)(2,1)S(1)} %collective-permute-done.17.refs_2_, bf16[384,512]{1,0:T(8,128)(2,1)S(1)} %collective-permute-done.18.refs_3_, ...), custom_call_target="tpu_custom_call" | custom-call | flops 2415919104 | bytes 18087936 | tf_op jit(solution)/shard_map/expert_hidden/pallas_call | solution.py:36
  203.5 9.3 %collective-permute-done.14.refs_2_ = bf16[384,512]{1,0:T(8,128)(2,1)S(1)} collective-permute-done((bf16[384,512]{1,0:T(8,128)(2,1)}, bf16[384,512]{1,0:T(8,128)(2,1)S(1)}, u32[]{:S(2)}, u32[]{:S(2)}) %collective-permute-start.14) | collective-permute-done | bytes 393248 | tf_op jit(solution)/shard_map/ppermute | solution.py:358
  212.9 5.1 %expert_hidden.7.h_ref = bf16[4,384,768]{2,1,0:T(8,128)(2,1)S(1)} custom-call(bf16[384,512]{1,0:T(8,128)(2,1)S(1)} %get-tuple-element.52.refs_6_.refs_8_.refs_0_, bf16[384,512]{1,0:T(8,128)(2,1)S(1)} %collective-permute-done.13.refs_1_, bf16[384,512]{1,0:T(8,128)(2,1)S(1)} %collective-permute-done.14.refs_2_, ...), custom_call_target="tpu_custom_call" | custom-call | flops 2415919104 | bytes 18087936 | tf_op jit(solution)/shard_map/expert_hidden/pallas_call | solution.py:36
  217.9 4.4 %expert_down.5 = (bf16[384,512]{1,0:T(8,128)(2,1)S(1)}, bf16[384,512]{1,0:T(8,128)(2,1)S(1)}, bf16[384,512]{1,0:T(8,128)(2,1)S(1)}, bf16[384,512]{1,0:T(8,128)(2,1)S(1)}) custom-call(bf16[4,384,768]{2,1,0:T(8,128)(2,1)S(1)} %expert_hidden.7.h_ref, bf16[4,768,2048]{2,1,0:T(8,128)(2,1)} %w_ref.7), custom_call_target="tpu_custom_call" | custom-call | flops 1207959552 | bytes 7077888 | tf_op jit(solution)/shard_map/expert_down/pallas_call | solution.py:221
  225.9 3.8 %expert_down.4 = (bf16[384,512]{1,0:T(8,128)(2,1)S(1)}, bf16[384,512]{1,0:T(8,128)(2,1)S(1)}, bf16[384,512]{1,0:T(8,128)(2,1)S(1)}, bf16[384,512]{1,0:T(8,128)(2,1)S(1)}) custom-call(bf16[4,384,768]{2,1,0:T(8,128)(2,1)S(1)} %expert_hidden.7.h_ref, bf16[4,768,2048]{2,1,0:T(8,128)(2,1)} %w_ref.7), custom_call_target="tpu_custom_call" | custom-call | flops 1207959552 | bytes 7077888 | tf_op jit(solution)/shard_map/expert_down/pallas_call | solution.py:221
  235.7 3.8 %expert_down.7 = (bf16[384,512]{1,0:T(8,128)(2,1)S(1)}, bf16[384,512]{1,0:T(8,128)(2,1)S(1)}, bf16[384,512]{1,0:T(8,128)(2,1)S(1)}, bf16[384,512]{1,0:T(8,128)(2,1)S(1)}) custom-call(bf16[4,384,768]{2,1,0:T(8,128)(2,1)S(1)} %expert_hidden.7.h_ref, bf16[4,768,2048]{2,1,0:T(8,128)(2,1)} %w_ref.7), custom_call_target="tpu_custom_call" | custom-call | flops 1207959552 | bytes 7077888 | tf_op jit(solution)/shard_map/expert_down/pallas_call | solution.py:221
  243.4 3.9 %expert_down.6 = (bf16[384,512]{1,0:T(8,128)(2,1)S(1)}, bf16[384,512]{1,0:T(8,128)(2,1)S(1)}, bf16[384,512]{1,0:T(8,128)(2,1)S(1)}, bf16[384,512]{1,0:T(8,128)(2,1)S(1)}) custom-call(bf16[4,384,768]{2,1,0:T(8,128)(2,1)S(1)} %copy-done.3, bf16[4,768,2048]{2,1,0:T(8,128)(2,1)} %w_ref.7), custom_call_target="tpu_custom_call" | custom-call | flops 1207959552 | bytes 7077888 | tf_op jit(solution)/shard_map/expert_down/pallas_call | solution.py:221
  252.0 6.4 %collective-permute-done.31.refs_5_ = bf16[384,512]{1,0:T(8,128)(2,1)S(1)} collective-permute-done((bf16[384,512]{1,0:T(8,128)(2,1)S(1)}, bf16[384,512]{1,0:T(8,128)(2,1)S(1)}, u32[]{:S(2)}, u32[]{:S(2)}) %collective-permute-start.31) | collective-permute-done | bytes 393248 | tf_op jit(solution)/shard_map/ppermute | solution.py:358
  265.9 8.8 %collective-permute-done.35.refs_3_ = bf16[384,512]{1,0:T(8,128)(2,1)S(1)} collective-permute-done((bf16[384,512]{1,0:T(8,128)(2,1)}, bf16[384,512]{1,0:T(8,128)(2,1)S(1)}, u32[]{:S(2)}, u32[]{:S(2)}) %collective-permute-start.35) | collective-permute-done | bytes 393248 | tf_op jit(solution)/shard_map/ppermute | solution.py:358
  274.7 5.4 %collective-permute-done.36.refs_4_ = bf16[384,512]{1,0:T(8,128)(2,1)S(1)} collective-permute-done((bf16[384,512]{1,0:T(8,128)(2,1)}, bf16[384,512]{1,0:T(8,128)(2,1)S(1)}, u32[]{:S(2)}, u32[]{:S(2)}) %collective-permute-start.36) | collective-permute-done | bytes 393248 | tf_op jit(solution)/shard_map/ppermute | solution.py:358
  291.6 4.0 %collective-permute-done.41 = bf16[128,512]{1,0:T(8,128)(2,1)S(1)} collective-permute-done((bf16[128,512]{1,0:T(8,128)(2,1)S(1)}, bf16[128,512]{1,0:T(8,128)(2,1)S(1)}, u32[]{:S(2)}, u32[]{:S(2)}) %collective-permute-start.41) | collective-permute-done | bytes 131104 | tf_op jit(solution)/shard_map/ppermute | solution.py:366
  295.6 6.5 %collective-permute-start.39 = (bf16[128,512]{1,0:T(8,128)(2,1)S(1)}, bf16[128,512]{1,0:T(8,128)(2,1)S(1)}, u32[]{:S(2)}, u32[]{:S(2)}) collective-permute-start(bf16[128,512]{1,0:T(8,128)(2,1)S(1)} %get-tuple-element.100), channel_id=1, source_target_pairs={{0,2},{1,7},{2,0},{3,5},{4,6},{5,3},{6,4},{7,1},{8,10},{9,15},{10,... | collective-permute-start | bytes 393224 | tf_op jit(solution)/shard_map/ppermute | solution.py:366
  314.1 3.7 %collective-permute-done.48 = bf16[128,512]{1,0:T(8,128)(2,1)S(1)} collective-permute-done((bf16[128,512]{1,0:T(8,128)(2,1)S(1)}, bf16[128,512]{1,0:T(8,128)(2,1)S(1)}, u32[]{:S(2)}, u32[]{:S(2)}) %collective-permute-start.48) | collective-permute-done | bytes 131104 | tf_op jit(solution)/shard_map/ppermute | solution.py:366
  317.9 7.5 %collective-permute-done.47 = bf16[128,512]{1,0:T(8,128)(2,1)S(1)} collective-permute-done((bf16[128,512]{1,0:T(8,128)(2,1)S(1)}, bf16[128,512]{1,0:T(8,128)(2,1)S(1)}, u32[]{:S(2)}, u32[]{:S(2)}) %collective-permute-start.47) | collective-permute-done | bytes 131104 | tf_op jit(solution)/shard_map/ppermute | solution.py:366
  (213 shorter events, 117.0 us)
Async XLA Ops:
  6.5 51.3 %all-gather.6.cloned.1.call-start = ((), (), s32[]{:S(2)}) async-start(), calls=%async_computation.3 | async-start | bytes 2359296 | tf_op jit(solution)/shard_map/all_gather | solution.py:407
  8.3 143.3 %all-gather.4.cloned.1.call-start = ((), (), s32[]{:S(2)}) async-start(), calls=%async_computation.1 | async-start | bytes 3538944 | tf_op jit(solution)/shard_map/all_gather | solution.py:460
  9.8 15.9 %collective-permute-start = (bf16[144,1024]{1,0:T(8,128)(2,1)S(1)}, bf16[144,1024]{1,0:T(8,128)(2,1)S(1)}, u32[]{:S(2)}, u32[]{:S(2)}) collective-permute-start(bf16[144,1024]{1,0:T(8,128)(2,1)S(1)} %fusion.3.refs_3_.refs_12_), channel_id=1, source_target_pairs={{0,2},{1,7},{2,0},{3,5},{4,6},{5,3},{6,4},{7,1},{8,10},{9,15},{10,... | collective-permute-start | bytes 884744 | tf_op jit(solution)/shard_map/ppermute | solution.py:366
  12.9 27.9 %collective-permute-start.1 = (bf16[144,1024]{1,0:T(8,128)(2,1)S(1)}, bf16[144,1024]{1,0:T(8,128)(2,1)S(1)}, u32[]{:S(2)}, u32[]{:S(2)}) collective-permute-start(bf16[144,1024]{1,0:T(8,128)(2,1)S(1)} %fusion.3.refs_3_.refs_12_), channel_id=1, source_target_pairs={{0,4},{1,5},{2,6},{3,7},{4,0},{5,1},{6,2},{7,3},{8,12},{9,13},{10,... | collective-permute-start | bytes 884744 | tf_op jit(solution)/shard_map/ppermute | solution.py:366
  15.5 39.5 %collective-permute-start.2 = (bf16[144,1024]{1,0:T(8,128)(2,1)S(1)}, bf16[144,1024]{1,0:T(8,128)(2,1)S(1)}, u32[]{:S(2)}, u32[]{:S(2)}) collective-permute-start(bf16[144,1024]{1,0:T(8,128)(2,1)S(1)} %fusion.3.refs_3_.refs_12_), channel_id=1, source_target_pairs={{0,6},{1,3},{2,4},{3,1},{4,2},{5,7},{6,0},{7,5},{8,14},{9,11},{10,... | collective-permute-start | bytes 884744 | tf_op jit(solution)/shard_map/ppermute | solution.py:366
  15.5 39.6 %collective-permute-start.3 = (bf16[144,1024]{1,0:T(8,128)(2,1)S(1)}, bf16[144,1024]{1,0:T(8,128)(2,1)S(1)}, u32[]{:S(2)}, u32[]{:S(2)}) collective-permute-start(bf16[144,1024]{1,0:T(8,128)(2,1)S(1)} %fusion.3.refs_3_.refs_12_), channel_id=1, source_target_pairs={{0,1},{1,0},{2,3},{3,2},{4,5},{5,4},{6,7},{7,6},{8,9},{9,8},{10,11... | collective-permute-start | bytes 884744 | tf_op jit(solution)/shard_map/ppermute | solution.py:358
  25.7 29.3 %collective-permute-start.4 = (bf16[144,1024]{1,0:T(8,128)(2,1)S(1)}, bf16[144,1024]{1,0:T(8,128)(2,1)S(1)}, u32[]{:S(2)}, u32[]{:S(2)}) collective-permute-start(bf16[144,1024]{1,0:T(8,128)(2,1)S(1)} %collective-permute-done.refs_4_.refs_13_), channel_id=1, source_target_pairs={{0,1},{1,0},{2,3},{3,2},{4,5},{5,4},{6,7},{7,6},{8,9},{9,8},{10,11... | collective-permute-start | bytes 884744 | tf_op jit(solution)/shard_map/ppermute | solution.py:358
  78.9 21.3 %collective-permute-start.10 = (bf16[128,2048]{1,0:T(8,128)(2,1)}, bf16[128,2048]{1,0:T(8,128)(2,1)}, u32[]{:S(2)}, u32[]{:S(2)}) collective-permute-start(bf16[128,2048]{1,0:T(8,128)(2,1)} %convolution_convert_fusion.2.refs_20_), channel_id=1, source_target_pairs={{0,24},{8,16},{16,8},{24,0},{1,25},{9,17},{17,9},{25,1},{2,26},{10... | collective-permute-start | bytes 1572872 | tf_op jit(solution)/shard_map/ppermute | solution.py:358
  82.8 24.3 %collective-permute-start.11 = (bf16[128,2048]{1,0:T(8,128)(2,1)}, bf16[128,2048]{1,0:T(8,128)(2,1)}, u32[]{:S(2)}, u32[]{:S(2)}) collective-permute-start(bf16[128,2048]{1,0:T(8,128)(2,1)} %convolution_convert_fusion.1.refs_21_), channel_id=1, source_target_pairs={{0,16},{8,24},{16,0},{24,8},{1,17},{9,25},{17,1},{25,9},{2,18},{10... | collective-permute-start | bytes 1572872 | tf_op jit(solution)/shard_map/ppermute | solution.py:358
  87.5 19.7 %collective-permute-start.12 = (bf16[128,2048]{1,0:T(8,128)(2,1)}, bf16[128,2048]{1,0:T(8,128)(2,1)}, u32[]{:S(2)}, u32[]{:S(2)}) collective-permute-start(bf16[128,2048]{1,0:T(8,128)(2,1)} %convolution_convert_fusion.refs_22_), channel_id=1, source_target_pairs={{0,8},{8,0},{16,24},{24,16},{1,9},{9,1},{17,25},{25,17},{2,10},{10... | collective-permute-start | bytes 1572872 | tf_op jit(solution)/shard_map/ppermute | solution.py:358
  110.8 214.8 %reduce-scatter.2.cloned.1.call-start = ((), (), s32[]{:S(2)}) async-start(), calls=%async_computation.2 | async-start | bytes 2359296 | tf_op jit(solution)/shard_map/reduce_scatter | solution.py:488
  132.4 27.6 %collective-permute-start.26 = (bf16[384,512]{1,0:T(8,128)(2,1)}, bf16[384,512]{1,0:T(8,128)(2,1)}, u32[]{:S(2)}, u32[]{:S(2)}) collective-permute-start(bf16[384,512]{1,0:T(8,128)(2,1)} %get-tuple-element.66), channel_id=1, source_target_pairs={{0,8},{8,0},{16,24},{24,16},{1,9},{9,1},{17,25},{25,17},{2,10},{10... | collective-permute-start | bytes 1179656 | tf_op jit(solution)/shard_map/ppermute | solution.py:358
  132.4 29.0 %collective-permute-start.27 = (bf16[384,512]{1,0:T(8,128)(2,1)}, bf16[384,512]{1,0:T(8,128)(2,1)}, u32[]{:S(2)}, u32[]{:S(2)}) collective-permute-start(bf16[384,512]{1,0:T(8,128)(2,1)} %get-tuple-element.67), channel_id=1, source_target_pairs={{0,16},{8,24},{16,0},{24,8},{1,17},{9,25},{17,1},{25,9},{2,18},{10... | collective-permute-start | bytes 1179656 | tf_op jit(solution)/shard_map/ppermute | solution.py:358
  133.8 31.9 %collective-permute-start.28 = (bf16[384,512]{1,0:T(8,128)(2,1)}, bf16[384,512]{1,0:T(8,128)(2,1)}, u32[]{:S(2)}, u32[]{:S(2)}) collective-permute-start(bf16[384,512]{1,0:T(8,128)(2,1)} %get-tuple-element.68), channel_id=1, source_target_pairs={{0,24},{8,16},{16,8},{24,0},{1,25},{9,17},{17,9},{25,1},{2,26},{10... | collective-permute-start | bytes 1179656 | tf_op jit(solution)/shard_map/ppermute | solution.py:358
  158.4 20.8 %collective-permute-start.19 = (bf16[384,512]{1,0:T(8,128)(2,1)S(1)}, bf16[384,512]{1,0:T(8,128)(2,1)S(1)}, u32[]{:S(2)}, u32[]{:S(2)}) collective-permute-start(bf16[384,512]{1,0:T(8,128)(2,1)S(1)} %get-tuple-element.61), channel_id=1, source_target_pairs={{0,8},{8,0},{16,24},{24,16},{1,9},{9,1},{17,25},{25,17},{2,10},{10... | collective-permute-start | bytes 1179656 | tf_op jit(solution)/shard_map/ppermute | solution.py:358
  160.0 20.0 %collective-permute-start.20 = (bf16[384,512]{1,0:T(8,128)(2,1)S(1)}, bf16[384,512]{1,0:T(8,128)(2,1)S(1)}, u32[]{:S(2)}, u32[]{:S(2)}) collective-permute-start(bf16[384,512]{1,0:T(8,128)(2,1)S(1)} %get-tuple-element.62), channel_id=1, source_target_pairs={{0,16},{8,24},{16,0},{24,8},{1,17},{9,25},{17,1},{25,9},{2,18},{10... | collective-permute-start | bytes 1179656 | tf_op jit(solution)/shard_map/ppermute | solution.py:358
  161.4 23.2 %collective-permute-start.21 = (bf16[384,512]{1,0:T(8,128)(2,1)S(1)}, bf16[384,512]{1,0:T(8,128)(2,1)S(1)}, u32[]{:S(2)}, u32[]{:S(2)}) collective-permute-start(bf16[384,512]{1,0:T(8,128)(2,1)S(1)} %get-tuple-element.63), channel_id=1, source_target_pairs={{0,24},{8,16},{16,8},{24,0},{1,25},{9,17},{17,9},{25,1},{2,26},{10... | collective-permute-start | bytes 1179656 | tf_op jit(solution)/shard_map/ppermute | solution.py:358
  165.7 31.6 %collective-permute-start.17 = (bf16[384,512]{1,0:T(8,128)(2,1)S(1)}, bf16[384,512]{1,0:T(8,128)(2,1)S(1)}, u32[]{:S(2)}, u32[]{:S(2)}) collective-permute-start(bf16[384,512]{1,0:T(8,128)(2,1)S(1)} %get-tuple-element.58), channel_id=1, source_target_pairs={{0,16},{8,24},{16,0},{24,8},{1,17},{9,25},{17,1},{25,9},{2,18},{10... | collective-permute-start | bytes 1179656 | tf_op jit(solution)/shard_map/ppermute | solution.py:358
  167.8 29.5 %collective-permute-start.18 = (bf16[384,512]{1,0:T(8,128)(2,1)S(1)}, bf16[384,512]{1,0:T(8,128)(2,1)S(1)}, u32[]{:S(2)}, u32[]{:S(2)}) collective-permute-start(bf16[384,512]{1,0:T(8,128)(2,1)S(1)} %get-tuple-element.59), channel_id=1, source_target_pairs={{0,24},{8,16},{16,8},{24,0},{1,25},{9,17},{17,9},{25,1},{2,26},{10... | collective-permute-start | bytes 1179656 | tf_op jit(solution)/shard_map/ppermute | solution.py:358
  179.1 24.4 %collective-permute-start.13 = (bf16[384,512]{1,0:T(8,128)(2,1)}, bf16[384,512]{1,0:T(8,128)(2,1)S(1)}, u32[]{:S(2)}, u32[]{:S(2)}) collective-permute-start(bf16[384,512]{1,0:T(8,128)(2,1)} %get-tuple-element.53), channel_id=1, source_target_pairs={{0,8},{8,0},{16,24},{24,16},{1,9},{9,1},{17,25},{25,17},{2,10},{10... | collective-permute-start | bytes 1179656 | tf_op jit(solution)/shard_map/ppermute | solution.py:358
  180.0 32.8 %collective-permute-start.14 = (bf16[384,512]{1,0:T(8,128)(2,1)}, bf16[384,512]{1,0:T(8,128)(2,1)S(1)}, u32[]{:S(2)}, u32[]{:S(2)}) collective-permute-start(bf16[384,512]{1,0:T(8,128)(2,1)} %get-tuple-element.54), channel_id=1, source_target_pairs={{0,16},{8,24},{16,0},{24,8},{1,17},{9,25},{17,1},{25,9},{2,18},{10... | collective-permute-start | bytes 1179656 | tf_op jit(solution)/shard_map/ppermute | solution.py:358
  184.6 28.3 %collective-permute-start.15 = (bf16[384,512]{1,0:T(8,128)(2,1)}, bf16[384,512]{1,0:T(8,128)(2,1)S(1)}, u32[]{:S(2)}, u32[]{:S(2)}) collective-permute-start(bf16[384,512]{1,0:T(8,128)(2,1)} %get-tuple-element.55), channel_id=1, source_target_pairs={{0,24},{8,16},{16,8},{24,0},{1,25},{9,17},{17,9},{25,1},{2,26},{10... | collective-permute-start | bytes 1179656 | tf_op jit(solution)/shard_map/ppermute | solution.py:358
  222.9 26.8 %collective-permute-start.33 = (bf16[384,512]{1,0:T(8,128)(2,1)S(1)}, bf16[384,512]{1,0:T(8,128)(2,1)S(1)}, u32[]{:S(2)}, u32[]{:S(2)}) collective-permute-start(bf16[384,512]{1,0:T(8,128)(2,1)S(1)} %get-tuple-element.83), channel_id=1, source_target_pairs={{0,16},{8,24},{16,0},{24,8},{1,17},{9,25},{17,1},{25,9},{2,18},{10... | collective-permute-start | bytes 1179656 | tf_op jit(solution)/shard_map/ppermute | solution.py:358
  224.2 25.4 %collective-permute-start.34 = (bf16[384,512]{1,0:T(8,128)(2,1)S(1)}, bf16[384,512]{1,0:T(8,128)(2,1)S(1)}, u32[]{:S(2)}, u32[]{:S(2)}) collective-permute-start(bf16[384,512]{1,0:T(8,128)(2,1)S(1)} %get-tuple-element.84), channel_id=1, source_target_pairs={{0,24},{8,16},{16,8},{24,0},{1,25},{9,17},{17,9},{25,1},{2,26},{10... | collective-permute-start | bytes 1179656 | tf_op jit(solution)/shard_map/ppermute | solution.py:358
  229.7 22.3 %collective-permute-start.29 = (bf16[384,512]{1,0:T(8,128)(2,1)S(1)}, bf16[384,512]{1,0:T(8,128)(2,1)S(1)}, u32[]{:S(2)}, u32[]{:S(2)}) collective-permute-start(bf16[384,512]{1,0:T(8,128)(2,1)S(1)} %get-tuple-element.76), channel_id=1, source_target_pairs={{0,8},{8,0},{16,24},{24,16},{1,9},{9,1},{17,25},{25,17},{2,10},{10... | collective-permute-start | bytes 1179656 | tf_op jit(solution)/shard_map/ppermute | solution.py:358
  230.2 21.8 %collective-permute-start.30 = (bf16[384,512]{1,0:T(8,128)(2,1)S(1)}, bf16[384,512]{1,0:T(8,128)(2,1)S(1)}, u32[]{:S(2)}, u32[]{:S(2)}) collective-permute-start(bf16[384,512]{1,0:T(8,128)(2,1)S(1)} %get-tuple-element.77), channel_id=1, source_target_pairs={{0,16},{8,24},{16,0},{24,8},{1,17},{9,25},{17,1},{25,9},{2,18},{10... | collective-permute-start | bytes 1179656 | tf_op jit(solution)/shard_map/ppermute | solution.py:358
  234.5 23.9 %collective-permute-start.31 = (bf16[384,512]{1,0:T(8,128)(2,1)S(1)}, bf16[384,512]{1,0:T(8,128)(2,1)S(1)}, u32[]{:S(2)}, u32[]{:S(2)}) collective-permute-start(bf16[384,512]{1,0:T(8,128)(2,1)S(1)} %get-tuple-element.78), channel_id=1, source_target_pairs={{0,24},{8,16},{16,8},{24,0},{1,25},{9,17},{17,9},{25,1},{2,26},{10... | collective-permute-start | bytes 1179656 | tf_op jit(solution)/shard_map/ppermute | solution.py:358
  263.3 16.8 %collective-permute-start.36 = (bf16[384,512]{1,0:T(8,128)(2,1)}, bf16[384,512]{1,0:T(8,128)(2,1)S(1)}, u32[]{:S(2)}, u32[]{:S(2)}) collective-permute-start(bf16[384,512]{1,0:T(8,128)(2,1)} %copy-done.25), channel_id=1, source_target_pairs={{0,16},{8,24},{16,0},{24,8},{1,17},{9,25},{17,1},{25,9},{2,18},{10... | collective-permute-start | bytes 1179656 | tf_op jit(solution)/shard_map/ppermute | solution.py:358
  264.7 15.4 %collective-permute-start.37 = (bf16[384,512]{1,0:T(8,128)(2,1)}, bf16[384,512]{1,0:T(8,128)(2,1)S(1)}, u32[]{:S(2)}, u32[]{:S(2)}) collective-permute-start(bf16[384,512]{1,0:T(8,128)(2,1)} %copy-done.24), channel_id=1, source_target_pairs={{0,24},{8,16},{16,8},{24,0},{1,25},{9,17},{17,9},{25,1},{2,26},{10... | collective-permute-start | bytes 1179656 | tf_op jit(solution)/shard_map/ppermute | solution.py:358
  287.5 18.0 %collective-permute-start.42 = (bf16[384,512]{1,0:T(8,128)(2,1)S(1)}, bf16[384,512]{1,0:T(8,128)(2,1)S(1)}, u32[]{:S(2)}, u32[]{:S(2)}) collective-permute-start(bf16[384,512]{1,0:T(8,128)(2,1)S(1)} %copy-done.23), channel_id=1, source_target_pairs={{0,8},{8,0},{16,24},{24,16},{1,9},{9,1},{17,25},{25,17},{2,10},{10... | collective-permute-start | bytes 1179656 | tf_op jit(solution)/shard_map/ppermute | solution.py:358
  288.9 17.0 %collective-permute-start.43 = (bf16[384,512]{1,0:T(8,128)(2,1)S(1)}, bf16[384,512]{1,0:T(8,128)(2,1)S(1)}, u32[]{:S(2)}, u32[]{:S(2)}) collective-permute-start(bf16[384,512]{1,0:T(8,128)(2,1)S(1)} %copy-done.21), channel_id=1, source_target_pairs={{0,16},{8,24},{16,0},{24,8},{1,17},{9,25},{17,1},{25,9},{2,18},{10... | collective-permute-start | bytes 1179656 | tf_op jit(solution)/shard_map/ppermute | solution.py:358
  289.6 16.3 %collective-permute-start.44 = (bf16[384,512]{1,0:T(8,128)(2,1)S(1)}, bf16[384,512]{1,0:T(8,128)(2,1)S(1)}, u32[]{:S(2)}, u32[]{:S(2)}) collective-permute-start(bf16[384,512]{1,0:T(8,128)(2,1)S(1)} %copy-done.19), channel_id=1, source_target_pairs={{0,24},{8,16},{16,8},{24,0},{1,25},{9,17},{17,9},{25,1},{2,26},{10... | collective-permute-start | bytes 1179656 | tf_op jit(solution)/shard_map/ppermute | solution.py:358
  (53 other events, 453.0 us)
Sparse Core Ops, SparseCore 0:
  9.0 48.7 all-gather.5
  110.9 40.7 all-gather.3
  262.5 37.8 reduce-scatter.1
